TPU v7x, 32 devices: a whole 2x2x4 slice. The times are simulated.
32 devices in a mesh: ctx: 16 (over z, x, core), head: 2 (over y).
Axes of the slice: x: 2, y: 2, z: 4, core: 2. Of those that a mesh axis runs over, the one named last changes fastest.
Arguments:
- queries: bfloat16 [4096, 4096], P('ctx', 'head')
- keys: bfloat16 [4096, 256], P('ctx', 'head')
- values: bfloat16 [4096, 256], P('ctx', 'head'), may hold values from -6 to 6
- comp_keys: bfloat16 [64, 256], P('ctx', 'head')
- comp_values: bfloat16 [64, 256], P('ctx', 'head'), may hold values from -6 to 6
- selected: int32 [64, 15], replicated, may hold values from -1 to 59, as said below
- inputs: bfloat16 [4096, 2560], P('ctx'), may hold values from -6 to 6
- w_gate: bfloat16 [2560, 64], P(None, 'head'), may hold values from -0.125 to 0.125
- d_out: bfloat16 [4096, 4096], P('ctx', 'head'), may hold values from -6 to 6
Outputs:
- d_queries: bfloat16 [4096, 4096], P('ctx', 'head')
- d_keys: bfloat16 [4096, 256], P('ctx', 'head')
- d_values: bfloat16 [4096, 256], P('ctx', 'head')
- d_comp_keys: bfloat16 [64, 256], P('ctx', 'head')
- d_comp_values: bfloat16 [64, 256], P('ctx', 'head')
- d_inputs: bfloat16 [4096, 2560], P('ctx', 'head')
Inputs may be any that keep to these rules, and one draw needn't show every extreme that they name: `selected`: block c lies on index c // 4 of ctx. Let H = 16 // 2. Entry j of row b names a block on the index that lies r places before the index holding block b, where r = 1 + j * max(H - 1, 0) // 14 for even b and r = H + 1 + j * max(H - 2, 0) // 14 for odd b; the entry is -1 where that index would be below 0 or where r equals that of entry j - 1 of the same row. Over the 4 rows of one index of ctx, each index that is named is named exactly 2 times.
All inputs are finite; a program needn't handle non-finite values.
Results may differ from a plain program's by a relative error of at most 0.019.
Values may be sent and summed in bfloat16 or wider, within the bound.
No kernel may reach another device: no remote copies, remote signals or barrier semaphores. Data moves between devices by JAX's collectives and lax.ppermute only.
A program may use at most 128 MiB of HBM per device.

v0:
```python
import jax
import jax.numpy as jnp
from jax import lax
from jax.sharding import PartitionSpec as P

BLK = 64
PICKS = 15


def attend(query_blk, key_set, value_set, visible, dout_blk, gate_blk):
    scale = key_set.shape[1] ** (-0.5)
    scores = (
        jnp.einsum("thd,kd->thk", query_blk, key_set, preferred_element_type=jnp.float32) * scale
    )
    scores = jnp.where(visible[:, None, :], scores, -jnp.inf)
    top = jnp.max(scores, axis=-1, keepdims=True)
    expo = jnp.exp(scores - top)
    probs = (expo / jnp.sum(expo, axis=-1, keepdims=True)).astype(jnp.bfloat16)
    out = jnp.einsum("thk,kd->thd", probs, value_set, preferred_element_type=jnp.float32)
    d_gate = jnp.sum(dout_blk.astype(jnp.float32) * out, axis=-1)
    d_branch = (gate_blk[:, :, None] * dout_blk.astype(jnp.float32)).astype(jnp.bfloat16)
    d_prob = jnp.einsum("thd,kd->thk", d_branch, value_set, preferred_element_type=jnp.float32)
    delta = jnp.sum(probs.astype(jnp.float32) * d_prob, axis=-1, keepdims=True)
    d_score = (probs.astype(jnp.float32) * (d_prob - delta) * scale).astype(jnp.bfloat16)
    d_query = jnp.einsum("thk,kd->thd", d_score, key_set, preferred_element_type=jnp.float32)
    d_key = jnp.einsum("thk,thd->kd", d_score, query_blk, preferred_element_type=jnp.float32)
    d_value = jnp.einsum("thk,thd->kd", probs, d_branch, preferred_element_type=jnp.float32)
    return (d_query, d_key, d_value, d_gate)


def body(queries, keys, values, comp_keys, comp_values, selected, inputs, w_gate, d_out):
    tokens_here = queries.shape[0]
    head_size = keys.shape[1]
    heads = queries.shape[1] // head_size
    blocks_here = tokens_here // BLK
    capacity = blocks_here // 2
    ranks = lax.axis_size("ctx")
    rank_here = lax.axis_index("ctx")
    all_blocks = blocks_here * ranks
    entries = blocks_here * PICKS
    gate = jax.nn.sigmoid(jnp.dot(inputs, w_gate, preferred_element_type=jnp.float32))
    all_ck, all_cv = (
        lax.all_gather(comp_keys, "ctx", axis=0, tiled=True),
        lax.all_gather(comp_values, "ctx", axis=0, tiled=True),
    )
    my_rows = lax.dynamic_slice_in_dim(selected, rank_here * blocks_here, blocks_here, 0).reshape(
        entries
    )
    valid = my_rows >= 0
    valid_rows = valid.reshape(blocks_here, PICKS)
    key_blocks = keys.reshape(blocks_here, BLK, head_size)
    value_blocks = values.reshape(blocks_here, BLK, head_size)
    owner = jnp.where(valid, my_rows // blocks_here, -1)
    order_ids = jnp.arange(entries, dtype=jnp.int32)
    earlier = (
        (owner[:, None] == owner[None, :])
        & (order_ids[None, :] < order_ids[:, None])
        & valid[None, :]
    )
    rank_mine = jnp.sum(earlier.astype(jnp.int32), axis=1)
    slot = jnp.where(valid, owner * capacity + rank_mine, ranks * capacity)
    table = selected.reshape(ranks, entries)
    asked = (table >= 0) & (table // blocks_here == rank_here)
    asked_rank = jnp.cumsum(asked.astype(jnp.int32), axis=1) - 1
    local_block = table % blocks_here
    hit = asked[:, :, None] & (
        asked_rank[:, :, None] == jnp.arange(capacity, dtype=jnp.int32)[None, None, :]
    )
    present = jnp.any(hit, axis=1)
    local_index = jnp.sum(jnp.where(hit, local_block[:, :, None], 0), axis=1)
    send_k = jnp.where(
        present[:, :, None, None], key_blocks[local_index], jnp.zeros((), jnp.bfloat16)
    )
    send_v = jnp.where(
        present[:, :, None, None], value_blocks[local_index], jnp.zeros((), jnp.bfloat16)
    )
    recv_k, recv_v = (
        lax.all_to_all(send_k, "ctx", split_axis=0, concat_axis=0, tiled=True),
        lax.all_to_all(send_v, "ctx", split_axis=0, concat_axis=0, tiled=True),
    )
    fetch_index = jnp.where(valid, slot, 0)
    fetch_k = recv_k.reshape(ranks * capacity, BLK, head_size)[fetch_index].reshape(
        blocks_here, PICKS, BLK, head_size
    )
    fetch_v = recv_v.reshape(ranks * capacity, BLK, head_size)[fetch_index].reshape(
        blocks_here, PICKS, BLK, head_size
    )
    lower = jnp.arange(BLK)[:, None] >= jnp.arange(BLK)[None, :]

    def step(carry, block):
        dck_acc, dcv_acc = carry
        query_blk = lax.dynamic_slice_in_dim(queries, block * BLK, BLK, 0).reshape(
            BLK, heads, head_size
        )
        dout_blk = lax.dynamic_slice_in_dim(d_out, block * BLK, BLK, 0).reshape(
            BLK, heads, head_size
        )
        gate_blk = lax.dynamic_slice_in_dim(gate, block * BLK, BLK, 0)
        pos = rank_here * tokens_here + block * BLK + jnp.arange(BLK, dtype=jnp.int32)
        vis_c = jnp.arange(all_blocks, dtype=jnp.int32)[None, :] * BLK <= pos[:, None]
        dqc, dckb, dcvb, dgc = attend(
            query_blk, all_ck, all_cv, vis_c, dout_blk, gate_blk[:, :heads]
        )
        own_k = lax.dynamic_slice_in_dim(keys, block * BLK, BLK, 0)
        own_v = lax.dynamic_slice_in_dim(values, block * BLK, BLK, 0)
        key_set = jnp.concatenate([own_k, fetch_k[block].reshape(PICKS * BLK, head_size)], axis=0)
        value_set = jnp.concatenate([own_v, fetch_v[block].reshape(PICKS * BLK, head_size)], axis=0)
        vis_p = jnp.broadcast_to(jnp.repeat(valid_rows[block], BLK)[None, :], (BLK, PICKS * BLK))
        vis_s = jnp.concatenate([lower, vis_p], axis=1)
        dqs, dks, dvs, dgs = attend(
            query_blk, key_set, value_set, vis_s, dout_blk, gate_blk[:, heads:]
        )
        d_query = (dqc + dqs).reshape(BLK, heads * head_size).astype(jnp.bfloat16)
        d_gate = jnp.concatenate([dgc, dgs], axis=-1)
        picks_k = dks[BLK:].reshape(PICKS, BLK, head_size)
        picks_v = dvs[BLK:].reshape(PICKS, BLK, head_size)
        return (
            (dck_acc + dckb, dcv_acc + dcvb),
            (d_query, d_gate, dks[:BLK], dvs[:BLK], picks_k, picks_v),
        )

    start = (
        jnp.zeros((all_blocks, head_size), jnp.float32),
        jnp.zeros((all_blocks, head_size), jnp.float32),
    )
    carry, outs = lax.scan(step, start, jnp.arange(blocks_here, dtype=jnp.int32))
    d_queries = outs[0].reshape(tokens_here, heads * head_size)
    d_gate = outs[1].reshape(tokens_here, 2 * heads)
    empty = jnp.zeros((ranks * capacity, BLK, head_size), jnp.float32)
    back_k = empty.at[slot].set(outs[4].reshape(entries, BLK, head_size), mode="drop")
    back_v = empty.at[slot].set(outs[5].reshape(entries, BLK, head_size), mode="drop")
    back_k = back_k.reshape(ranks, capacity, BLK, head_size)
    back_v = back_v.reshape(ranks, capacity, BLK, head_size)
    home_k, home_v = (
        lax.all_to_all(
            back_k.astype(jnp.bfloat16), "ctx", split_axis=0, concat_axis=0, tiled=True
        ).astype(back_k.dtype),
        lax.all_to_all(
            back_v.astype(jnp.bfloat16), "ctx", split_axis=0, concat_axis=0, tiled=True
        ).astype(back_v.dtype),
    )
    onehot = present[:, :, None] & (
        local_index[:, :, None] == jnp.arange(blocks_here, dtype=jnp.int32)[None, None, :]
    )
    onehot = onehot.astype(jnp.float32).reshape(ranks * capacity, blocks_here)
    sum_k = jnp.einsum(
        "nj,nx->jx",
        onehot,
        home_k.reshape(ranks * capacity, BLK * head_size),
        precision=lax.Precision.HIGHEST,
    )
    sum_v = jnp.einsum(
        "nj,nx->jx",
        onehot,
        home_v.reshape(ranks * capacity, BLK * head_size),
        precision=lax.Precision.HIGHEST,
    )
    d_keys = (
        outs[2].reshape(tokens_here, head_size) + sum_k.reshape(tokens_here, head_size)
    ).astype(jnp.bfloat16)
    d_values = (
        outs[3].reshape(tokens_here, head_size) + sum_v.reshape(tokens_here, head_size)
    ).astype(jnp.bfloat16)
    dck_sum, dcv_sum = (
        lax.psum_scatter(carry[0], "ctx", scatter_dimension=0, tiled=True),
        lax.psum_scatter(carry[1], "ctx", scatter_dimension=0, tiled=True),
    )
    d_z = (d_gate * gate * (1.0 - gate)).astype(jnp.bfloat16)
    partial_terms = lax.dot_general(
        d_z, w_gate, (((1,), (1,)), ((), ())), preferred_element_type=jnp.float32
    )
    d_inputs = lax.psum_scatter(
        partial_terms.astype(jnp.bfloat16), "head", scatter_dimension=1, tiled=True
    )
    return (
        d_queries,
        d_keys,
        d_values,
        dck_sum.astype(jnp.bfloat16),
        dcv_sum.astype(jnp.bfloat16),
        d_inputs,
    )


def solution(mesh):
    in_specs = (
        P("ctx", "head"),
        P("ctx", "head"),
        P("ctx", "head"),
        P("ctx", "head"),
        P("ctx", "head"),
        P(),
        P("ctx", None),
        P(None, "head"),
        P("ctx", "head"),
    )
    out_specs = (
        P("ctx", "head"),
        P("ctx", "head"),
        P("ctx", "head"),
        P("ctx", "head"),
        P("ctx", "head"),
        P("ctx", "head"),
    )
    return jax.shard_map(body, mesh=mesh, in_specs=in_specs, out_specs=out_specs, check_vma=False)
```

profile of v0, /device:TPU:0, one launch (start us, length us, event | category | flops | bytes accessed | tf_op | source)
XLA Modules:
  0.0 372.9 jit_solution(1682258410007690342)
XLA Ops:
  13.1 7.4 %all-to-all-start = ((bf16[16,2,64,128]{3,2,1,0:T(8,128)(2,1)}), bf16[16,2,64,128]{3,2,1,0:T(8,128)(2,1)S(1)}, u32[]{:S(2)}, u32[]{:S(2)}) async-start(bf16[16,2,64,128]{3,2,1,0:T(8,128)(2,1)} %get-tuple-element.486), calls=%async_computation | async-start | bytes 1048576 | tf_op jit(solution)/shard_map/all_to_all | solution.py:78
  20.5 14.3 %all-to-all-done = bf16[16,2,64,128]{3,2,1,0:T(8,128)(2,1)S(1)} async-done(((bf16[16,2,64,128]{3,2,1,0:T(8,128)(2,1)}), bf16[16,2,64,128]{3,2,1,0:T(8,128)(2,1)S(1)}, u32[]{:S(2)}, u32[]{:S(2)}) %all-to-all-start) | async-done | bytes 524320 | tf_op jit(solution)/shard_map/all_to_all | solution.py:78
  34.9 4.1 %all-to-all-start.1 = ((bf16[16,2,64,128]{3,2,1,0:T(8,128)(2,1)}), bf16[16,2,64,128]{3,2,1,0:T(8,128)(2,1)S(1)}, u32[]{:S(2)}, u32[]{:S(2)}) async-start(bf16[16,2,64,128]{3,2,1,0:T(8,128)(2,1)} %get-tuple-element.485), calls=%async_computation.1 | async-start | bytes 1048576 | tf_op jit(solution)/shard_map/all_to_all | solution.py:79
  39.2 24.8 %all-gather = bf16[16,4,128]{2,1,0:T(4,128)(2,1)S(1)} all-gather(bf16[1,4,128]{2,1,0:T(4,128)(2,1)S(1)} %bitcast.228), channel_id=1, replica_groups=mesh['ctx'=16,'head'=2] {'ctx'}, dimensions={0}, use_global_device_ids=true | all-gather | bytes 17408 | tf_op jit(solution)/shard_map/all_gather | solution.py:43
  64.0 18.9 %all-gather.1 = bf16[16,4,128]{2,1,0:T(4,128)(2,1)S(1)} all-gather(bf16[1,4,128]{2,1,0:T(4,128)(2,1)S(1)} %bitcast.229), channel_id=1, replica_groups=mesh['ctx'=16,'head'=2] {'ctx'}, dimensions={0}, use_global_device_ids=true | all-gather | bytes 17408 | tf_op jit(solution)/shard_map/all_gather | solution.py:44
  84.1 1.6 gather_fusion.1
  85.8 1.6 gather_fusion.3
  87.4 180.4 %while.27 = (s32[]{:T(128)}, f32[64,128]{1,0:T(8,128)}, f32[64,128]{1,0:T(8,128)}, bf16[4,64,2048]{2,1,0:T(8,128)(2,1)}, f32[4,64,32]{2,1,0:T(8,128)}, /*index=5...) while((s32[]{:T(128)}, f32[64,128]{1,0:T(8,128)}, ...), condition=%wide.region_13.14_spmd.clone, body=%wide.region_4.13_spmd.clone.sunk | while | flops 1737735424 | bytes 50798564 | solution.py:126
  97.3 3.4 fusion.175
  100.7 4.1 %divide_convert_fusion.5 = bf16[64,16,1024]{2,1,0:T(8,128)(2,1)} fusion(f32[64,16,1024]{2,1,0:T(8,128)} %get-tuple-element.639, f32[64,16]{1,0:T(8,128)S(1)} %get-tuple-element.640), kind=kLoop, calls=%fused_computation.15.clone.1 | loop fusion | flops 2097152 | bytes 6295552 | tf_op jit(solution)/shard_map/while/body/eval_jaxpr/convert_element_type | solution.py:18
  104.9 2.7 fusion.176
  107.5 6.6 %fusion.177 = f32[64,16,128]{2,1,0:T(8,128)} fusion(bf16[64,16,1024]{2,1,0:T(8,128)(2,1)} %divide_convert_fusion.5, f32[64,16,1024]{2,1,0:T(8,128)} %fusion.176, bf16[960,128]{1,0:T(8,128)(2,1)S(1)} %bitcast.212, bf16[64,128]{1,0:T(8,128)(2,1)S(1)} %get-tuple-element.638), kind=kOutput, calls=%fused_computation.24.clone.1 | convolution fusion | flops 276301824 | bytes 7077888 | tf_op jit(solution)/shard_map/while/body/eval_jaxpr/thk,kd->thd/dot_general | solution.py:25
  116.3 2.4 fusion.179
  119.7 6.0 %fusion.182 = f32[1024,128]{1,0:T(8,128)S(1)} fusion(bf16[64,16,128]{2,1,0:T(8,128)(2,1)S(1)} %bitcast.210, bf16[64,16,1024]{2,1,0:T(8,128)(2,1)} %divide_convert_fusion.5, f32[64,16,1024]{2,1,0:T(8,128)} %fusion.176), kind=kOutput, calls=%fused_computation.36.clone.1 | convolution fusion | flops 275777536 | bytes 7077888 | tf_op jit(solution)/shard_map/while/body/eval_jaxpr/thk,thd->kd/dot_general | solution.py:26
  126.4 2.6 convolution_bitcast_fusion.4
  135.2 1.8 fusion.172
  137.0 1.8 fusion.173
  142.8 3.4 fusion.175
  146.2 4.1 %divide_convert_fusion.5 = bf16[64,16,1024]{2,1,0:T(8,128)(2,1)} fusion(f32[64,16,1024]{2,1,0:T(8,128)} %get-tuple-element.639, f32[64,16]{1,0:T(8,128)S(1)} %get-tuple-element.640), kind=kLoop, calls=%fused_computation.15.clone.1 | loop fusion | flops 2097152 | bytes 6295552 | tf_op jit(solution)/shard_map/while/body/eval_jaxpr/convert_element_type | solution.py:18
  150.4 2.7 fusion.176
  153.0 6.6 %fusion.177 = f32[64,16,128]{2,1,0:T(8,128)} fusion(bf16[64,16,1024]{2,1,0:T(8,128)(2,1)} %divide_convert_fusion.5, f32[64,16,1024]{2,1,0:T(8,128)} %fusion.176, bf16[960,128]{1,0:T(8,128)(2,1)S(1)} %bitcast.212, bf16[64,128]{1,0:T(8,128)(2,1)S(1)} %get-tuple-element.638), kind=kOutput, calls=%fused_computation.24.clone.1 | convolution fusion | flops 276301824 | bytes 7077888 | tf_op jit(solution)/shard_map/while/body/eval_jaxpr/thk,kd->thd/dot_general | solution.py:25
  161.8 2.4 fusion.179
  165.3 6.0 %fusion.182 = f32[1024,128]{1,0:T(8,128)S(1)} fusion(bf16[64,16,128]{2,1,0:T(8,128)(2,1)S(1)} %bitcast.210, bf16[64,16,1024]{2,1,0:T(8,128)(2,1)} %divide_convert_fusion.5, f32[64,16,1024]{2,1,0:T(8,128)} %fusion.176), kind=kOutput, calls=%fused_computation.36.clone.1 | convolution fusion | flops 275777536 | bytes 7077888 | tf_op jit(solution)/shard_map/while/body/eval_jaxpr/thk,thd->kd/dot_general | solution.py:26
  171.9 2.6 convolution_bitcast_fusion.4
  180.7 1.8 fusion.172
  182.5 1.8 fusion.173
  188.4 3.4 fusion.175
  191.7 4.1 %divide_convert_fusion.5 = bf16[64,16,1024]{2,1,0:T(8,128)(2,1)} fusion(f32[64,16,1024]{2,1,0:T(8,128)} %get-tuple-element.639, f32[64,16]{1,0:T(8,128)S(1)} %get-tuple-element.640), kind=kLoop, calls=%fused_computation.15.clone.1 | loop fusion | flops 2097152 | bytes 6295552 | tf_op jit(solution)/shard_map/while/body/eval_jaxpr/convert_element_type | solution.py:18
  195.9 2.7 fusion.176
  198.6 6.6 %fusion.177 = f32[64,16,128]{2,1,0:T(8,128)} fusion(bf16[64,16,1024]{2,1,0:T(8,128)(2,1)} %divide_convert_fusion.5, f32[64,16,1024]{2,1,0:T(8,128)} %fusion.176, bf16[960,128]{1,0:T(8,128)(2,1)S(1)} %bitcast.212, bf16[64,128]{1,0:T(8,128)(2,1)S(1)} %get-tuple-element.638), kind=kOutput, calls=%fused_computation.24.clone.1 | convolution fusion | flops 276301824 | bytes 7077888 | tf_op jit(solution)/shard_map/while/body/eval_jaxpr/thk,kd->thd/dot_general | solution.py:25
  207.4 2.4 fusion.179
  210.8 6.0 %fusion.182 = f32[1024,128]{1,0:T(8,128)S(1)} fusion(bf16[64,16,128]{2,1,0:T(8,128)(2,1)S(1)} %bitcast.210, bf16[64,16,1024]{2,1,0:T(8,128)(2,1)} %divide_convert_fusion.5, f32[64,16,1024]{2,1,0:T(8,128)} %fusion.176), kind=kOutput, calls=%fused_computation.36.clone.1 | convolution fusion | flops 275777536 | bytes 7077888 | tf_op jit(solution)/shard_map/while/body/eval_jaxpr/thk,thd->kd/dot_general | solution.py:26
  217.4 2.6 convolution_bitcast_fusion.4
  226.2 1.8 fusion.172
  228.0 1.8 fusion.173
  233.9 3.4 fusion.175
  237.2 4.1 %divide_convert_fusion.5 = bf16[64,16,1024]{2,1,0:T(8,128)(2,1)} fusion(f32[64,16,1024]{2,1,0:T(8,128)} %get-tuple-element.639, f32[64,16]{1,0:T(8,128)S(1)} %get-tuple-element.640), kind=kLoop, calls=%fused_computation.15.clone.1 | loop fusion | flops 2097152 | bytes 6295552 | tf_op jit(solution)/shard_map/while/body/eval_jaxpr/convert_element_type | solution.py:18
  241.4 2.7 fusion.176
  244.1 6.6 %fusion.177 = f32[64,16,128]{2,1,0:T(8,128)} fusion(bf16[64,16,1024]{2,1,0:T(8,128)(2,1)} %divide_convert_fusion.5, f32[64,16,1024]{2,1,0:T(8,128)} %fusion.176, bf16[960,128]{1,0:T(8,128)(2,1)S(1)} %bitcast.212, bf16[64,128]{1,0:T(8,128)(2,1)S(1)} %get-tuple-element.638), kind=kOutput, calls=%fused_computation.24.clone.1 | convolution fusion | flops 276301824 | bytes 7077888 | tf_op jit(solution)/shard_map/while/body/eval_jaxpr/thk,kd->thd/dot_general | solution.py:25
  252.9 2.4 fusion.179
  256.3 6.0 %fusion.182 = f32[1024,128]{1,0:T(8,128)S(1)} fusion(bf16[64,16,128]{2,1,0:T(8,128)(2,1)S(1)} %bitcast.210, bf16[64,16,1024]{2,1,0:T(8,128)(2,1)} %divide_convert_fusion.5, f32[64,16,1024]{2,1,0:T(8,128)} %fusion.176), kind=kOutput, calls=%fused_computation.36.clone.1 | convolution fusion | flops 275777536 | bytes 7077888 | tf_op jit(solution)/shard_map/while/body/eval_jaxpr/thk,thd->kd/dot_general | solution.py:26
  262.9 2.6 convolution_bitcast_fusion.4
  267.9 6.8 %scatter_fusion = f32[32,64,128]{2,1,0:T(8,128)S(1)} fusion(f32[32,64,128]{2,1,0:T(8,128)S(1)} %broadcast_in_dim.163.clone, s32[60]{0:T(128)} %get-tuple-element.465, f32[60,64,128]{2,1,0:T(8,128)} %bitcast.224), kind=kCustom, calls=%fused_computation.4 | custom fusion | bytes 5898480 | tf_op jit(solution)/shard_map/scatter | solution.py:130
  275.7 3.6 all-to-all-start.2
  281.3 6.6 %scatter_fusion.1 = f32[32,64,128]{2,1,0:T(8,128)S(1)} fusion(f32[32,64,128]{2,1,0:T(8,128)S(1)} %broadcast_in_dim.163.clone.1, s32[60]{0:T(128)S(1)} %copy-done.10, f32[60,64,128]{2,1,0:T(8,128)} %bitcast.225), kind=kCustom, calls=%fused_computation.5 | custom fusion | bytes 5898480 | tf_op jit(solution)/shard_map/scatter | solution.py:131
  288.9 4.8 %all-to-all-done.2 = bf16[16,2,64,128]{3,2,1,0:T(8,128)(2,1)S(1)} async-done(((bf16[16,2,64,128]{3,2,1,0:T(8,128)(2,1)}), bf16[16,2,64,128]{3,2,1,0:T(8,128)(2,1)S(1)}, u32[]{:S(2)}, u32[]{:S(2)}) %all-to-all-start.2) | async-done | bytes 524320 | tf_op jit(solution)/shard_map/all_to_all | solution.py:135
  293.7 4.0 %all-to-all-start.3 = ((bf16[16,2,64,128]{3,2,1,0:T(8,128)(2,1)}), bf16[16,2,64,128]{3,2,1,0:T(8,128)(2,1)S(1)}, u32[]{:S(2)}, u32[]{:S(2)}) async-start(bf16[16,2,64,128]{3,2,1,0:T(8,128)(2,1)} %bitcast.22), calls=%async_computation.3 | async-start | bytes 1048576 | tf_op jit(solution)/shard_map/all_to_all | solution.py:138
  299.2 63.3 %all-reduce.2 = (bf16[64,128]{1,0:T(8,128)(2,1)S(1)}, bf16[64,128]{1,0:T(8,128)(2,1)S(1)}) all-reduce(f32[64,128]{1,0:T(8,128)S(1)} %copy-done.8, f32[64,128]{1,0:T(8,128)S(1)} %copy-done.9), channel_id=2, replica_groups=mesh['ctx'=16,'head'=2] {'ctx'}, use_global_device_ids=true, to_apply=%region_16.17.clone | all-reduce | flops 16384 | bytes 98304
  (255 shorter events, 63.9 us)
Async XLA Ops:
  7.2 76.4 %copy-start = (bf16[256,2560]{1,0:T(8,128)(2,1)S(1)}, bf16[256,2560]{1,0:T(8,128)(2,1)}, u32[]{:S(2)}) copy-start(bf16[256,2560]{1,0:T(8,128)(2,1)} %param.17) | copy-start | bytes 3932164
  11.9 27.3 %copy-start.11 = (bf16[4,128]{1,0:T(4,128)(2,1)S(1)}, bf16[4,128]{1,0:T(4,128)(2,1)}, u32[]{:S(2)}) copy-start(bf16[4,128]{1,0:T(4,128)(2,1)} %param.14) | copy-start | bytes 3076
  11.9 52.0 %copy-start.12 = (bf16[4,128]{1,0:T(4,128)(2,1)S(1)}, bf16[4,128]{1,0:T(4,128)(2,1)}, u32[]{:S(2)}) copy-start(bf16[4,128]{1,0:T(4,128)(2,1)} %param.15) | copy-start | bytes 3076
  11.9 71.7 %copy-start.3 = (bf16[2560,32]{0,1:T(8,128)(2,1)S(1)}, bf16[2560,32]{0,1:T(8,128)(2,1)}, u32[]{:S(2)}) copy-start(bf16[2560,32]{0,1:T(8,128)(2,1)} %param.18) | copy-start | bytes 491524
  13.1 21.8 %all-to-all-start = ((bf16[16,2,64,128]{3,2,1,0:T(8,128)(2,1)}), bf16[16,2,64,128]{3,2,1,0:T(8,128)(2,1)S(1)}, u32[]{:S(2)}, u32[]{:S(2)}) async-start(bf16[16,2,64,128]{3,2,1,0:T(8,128)(2,1)} %get-tuple-element.486), calls=%async_computation | async-start | bytes 1048576 | tf_op jit(solution)/shard_map/all_to_all | solution.py:78
  34.9 50.9 %all-to-all-start.1 = ((bf16[16,2,64,128]{3,2,1,0:T(8,128)(2,1)}), bf16[16,2,64,128]{3,2,1,0:T(8,128)(2,1)S(1)}, u32[]{:S(2)}, u32[]{:S(2)}) async-start(bf16[16,2,64,128]{3,2,1,0:T(8,128)(2,1)} %get-tuple-element.485), calls=%async_computation.1 | async-start | bytes 1048576 | tf_op jit(solution)/shard_map/all_to_all | solution.py:79
  87.4 2.6 copy-start.1
  87.4 3.6 copy-start.16
  87.4 7.8 %copy-start.13 = (pred[4,15]{1,0:T(4,128)(4,1)}, pred[4,15]{1,0:T(4,128)(4,1)S(1)}, u32[]{:S(2)}) copy-start(pred[4,15]{1,0:T(4,128)(4,1)S(1)} %get-tuple-element.716) | copy-start | bytes 184 | tf_op jit(solution)/shard_map/while
  128.9 2.4 copy-start.2
  129.0 2.4 copy-start.14
  129.0 2.4 copy-start.17
  131.4 2.6 copy-start.1
  131.4 3.6 copy-start.16
  131.4 9.3 %copy-start.13 = (pred[4,15]{1,0:T(4,128)(4,1)}, pred[4,15]{1,0:T(4,128)(4,1)S(1)}, u32[]{:S(2)}) copy-start(pred[4,15]{1,0:T(4,128)(4,1)S(1)} %get-tuple-element.716) | copy-start | bytes 184 | tf_op jit(solution)/shard_map/while
  174.5 2.4 copy-start.2
  174.5 2.4 copy-start.14
  174.5 2.4 copy-start.17
  176.9 2.6 copy-start.1
  176.9 3.6 copy-start.16
  176.9 9.3 %copy-start.13 = (pred[4,15]{1,0:T(4,128)(4,1)}, pred[4,15]{1,0:T(4,128)(4,1)S(1)}, u32[]{:S(2)}) copy-start(pred[4,15]{1,0:T(4,128)(4,1)S(1)} %get-tuple-element.716) | copy-start | bytes 184 | tf_op jit(solution)/shard_map/while
  220.0 2.4 copy-start.2
  220.0 2.4 copy-start.14
  220.0 2.4 copy-start.17
  222.4 2.6 copy-start.1
  222.4 3.6 copy-start.16
  222.4 9.3 %copy-start.13 = (pred[4,15]{1,0:T(4,128)(4,1)}, pred[4,15]{1,0:T(4,128)(4,1)S(1)}, u32[]{:S(2)}) copy-start(pred[4,15]{1,0:T(4,128)(4,1)S(1)} %get-tuple-element.716) | copy-start | bytes 184 | tf_op jit(solution)/shard_map/while
  265.5 2.4 copy-start.2
  265.5 2.4 copy-start.14
  265.5 2.3 copy-start.17
  274.7 4.8 %copy-start.5 = (f32[4,64,32]{2,1,0:T(8,128)S(1)}, f32[4,64,32]{2,1,0:T(8,128)}, u32[]{:S(2)}) copy-start(f32[4,64,32]{2,1,0:T(8,128)} %get-tuple-element.268) | copy-start | bytes 98308
  274.7 4.8 %copy-start.4 = (bf16[2560,32]{0,1:T(8,128)(2,1)S(1)}, bf16[2560,32]{0,1:T(8,128)(2,1)}, u32[]{:S(2)}) copy-start(bf16[2560,32]{0,1:T(8,128)(2,1)} %param.18) | copy-start | bytes 491524
  275.7 18.0 %all-to-all-start.2 = ((bf16[16,2,64,128]{3,2,1,0:T(8,128)(2,1)}), bf16[16,2,64,128]{3,2,1,0:T(8,128)(2,1)S(1)}, u32[]{:S(2)}, u32[]{:S(2)}) async-start(bf16[16,2,64,128]{3,2,1,0:T(8,128)(2,1)} %bitcast.19), calls=%async_computation.2 | async-start | bytes 1048576 | tf_op jit(solution)/shard_map/all_to_all | solution.py:135
  279.2 2.1 copy-start.10
  279.2 86.8 %reduce-scatter.2.cloned.1.call-start = ((), (), s32[]{:S(2)}) async-start(), calls=%async_computation.5 | async-start | bytes 1966080 | tf_op jit(solution)/shard_map/reduce_scatter | solution.py:172
  287.9 10.0 %copy-start.15 = (u32[32]{0:T(128)S(1)}, u32[32]{0:T(128)}, u32[]{:S(2)}) copy-start(u32[32]{0:T(128)} %constant.128) | copy-start | bytes 388
  288.0 11.3 %copy-start.8 = (f32[64,128]{1,0:T(8,128)S(1)}, f32[64,128]{1,0:T(8,128)}, u32[]{:S(2)}) copy-start(f32[64,128]{1,0:T(8,128)} %get-tuple-element.266) | copy-start | bytes 98308
  288.0 11.3 %copy-start.9 = (f32[64,128]{1,0:T(8,128)S(1)}, f32[64,128]{1,0:T(8,128)}, u32[]{:S(2)}) copy-start(f32[64,128]{1,0:T(8,128)} %get-tuple-element.267) | copy-start | bytes 98308
  288.0 76.8 %copy-start.6 = (f32[4,64,128]{2,1,0:T(8,128)S(1)}, f32[4,64,128]{2,1,0:T(8,128)}, u32[]{:S(2)}) copy-start(f32[4,64,128]{2,1,0:T(8,128)} %get-tuple-element.262) | copy-start | bytes 393220
  288.0 77.4 %copy-start.7 = (f32[4,64,128]{2,1,0:T(8,128)S(1)}, f32[4,64,128]{2,1,0:T(8,128)}, u32[]{:S(2)}) copy-start(f32[4,64,128]{2,1,0:T(8,128)} %get-tuple-element.264) | copy-start | bytes 393220
  293.7 70.6 %all-to-all-start.3 = ((bf16[16,2,64,128]{3,2,1,0:T(8,128)(2,1)}), bf16[16,2,64,128]{3,2,1,0:T(8,128)(2,1)S(1)}, u32[]{:S(2)}, u32[]{:S(2)}) async-start(bf16[16,2,64,128]{3,2,1,0:T(8,128)(2,1)} %bitcast.22), calls=%async_computation.3 | async-start | bytes 1048576 | tf_op jit(solution)/shard_map/all_to_all | solution.py:138
Sparse Core Ops, SparseCore 0:
  282.9 24.4 reduce-scatter.1
where the time goes:
time: 376 us; the launch traced here: 373 us
  matrix products  120 us (32%)
  blocking collectives  107 us (28%)
  local copies, waits for them, and re-layouts  51.1 us (14%)
  other arithmetic  30.1 us (8%)
  starting transfers between devices  19.3 us (5%)
  waiting for transfers between devices  19.1 us (5%)
  between operations  15.1 us (4%)
  loops' own time  11.1 us (3%)
    unnamed x1, blocking collectives  63.3 us
    dot_general x8, matrix products, attend(): jnp.einsum('thk,kd->thd', d_score, key_set, preferred_element_type=jnp.fl...  31.8 us
    dot_general x8, matrix products, attend(): jnp.einsum('thk,thd->kd', d_score, query_blk, preferred_element_type=jnp....  30.4 us
    all_gather x1, blocking collectives, body(): lax.all_gather(comp_keys, 'ctx', axis=0, tiled=True)  24.8 us
    all_gather x1, blocking collectives, body(): lax.all_gather(comp_values, 'ctx', axis=0, tiled=True)  18.9 us
    convert_element_type x8, other arithmetic, attend(): probs = (expo / jnp.sum(expo, axis=-1, keepdims=True)).astype(jnp.bfloat16)  17 us
    dot_general x8, matrix products, attend(): jnp.einsum('thk,thd->kd', probs, d_branch, preferred_element_type=jnp.flo...  16.6 us
    sub x8, matrix products, attend(): expo = jnp.exp(scores - top)  15.5 us
  transfers between devices with their start and end apart: 5, of which 2 were waited for; matrix products, arithmetic and copies ran while one was open for 5% of the time, Pallas kernels for 0%

commit v1 on v0

v1 whole, which is shorter than its diff:
```python
import functools

import jax
import jax.numpy as jnp
from jax import lax
from jax.experimental import pallas as pl
from jax.experimental.pallas import tpu as pltpu
from jax.sharding import PartitionSpec as P

BLK = 64
PICKS = 15
LOG2E = 1.4426950408889634
LANES = 256
NEG = -1e30
F32, BF16 = jnp.float32, jnp.bfloat16


def reach_lists(ranks):
    half = ranks // 2
    even, odd = [], []
    for j in range(PICKS):
        near = 1 + j * max(half - 1, 0) // 14
        far = half + 1 + j * max(half - 2, 0) // 14
        if j == 0 or near != 1 + (j - 1) * max(half - 1, 0) // 14:
            even.append((j, near))
        if j == 0 or far != half + 1 + (j - 1) * max(half - 2, 0) // 14:
            odd.append((j, far))
    return even, odd


def in_vmem():
    return pl.BlockSpec(memory_space=pltpu.VMEM)


def in_smem():
    return pl.BlockSpec(memory_space=pltpu.SMEM)


def params():
    return pltpu.CompilerParams(vmem_limit_bytes=60 * 1024 * 1024)


def fill_picks(ranks, qb, lists, p, me, sel_ref, k_ref, v_ref, out_ref):
    for parity, reach in enumerate(lists):
        for j, r in reach:
            dest = jnp.where(me + r < ranks, me + r, me)
            named = sel_ref[j, dest * qb + 2 * p + parity]
            local = jnp.clip(named - me * qb, 0, qb - 1)
            rows = pl.ds(pl.multiple_of(local * BLK, BLK), BLK)
            out_ref[dest, :BLK, :] = k_ref[rows, :]
            out_ref[dest, BLK : 2 * BLK, :] = v_ref[rows, :]


def pack_kernel(ranks, qb, lists, rank_ref, sel_ref, k_ref, v_ref, ck_ref, cv_ref, out_ref):
    hd = k_ref.shape[1]
    me = rank_ref[0]
    comp = jnp.concatenate([ck_ref[...].astype(F32), cv_ref[...].astype(F32)], axis=0).astype(BF16)

    def every(n, carry):
        out_ref[n, 2 * BLK :, :] = comp
        return carry

    lax.fori_loop(0, ranks, every, 0)
    out_ref[me, : 2 * BLK, :] = jnp.zeros((2 * BLK, hd), BF16)
    fill_picks(ranks, qb, lists, 0, me, sel_ref, k_ref, v_ref, out_ref)


def restack(heads, q_ref, do_ref, out_ref):
    hd = out_ref.shape[2] // 4
    per = LANES // BLK
    for i in range(2):
        for c in range(heads // per):
            for n, src in enumerate((q_ref, do_ref)):
                piece = jnp.concatenate(
                    [
                        src[i * BLK : (i + 1) * BLK, h * hd : (h + 1) * hd]
                        for h in range(c * per, (c + 1) * per)
                    ],
                    axis=0,
                )
                out_ref[i, c, n * hd : (n + 1) * hd, :] = turned(piece)
                out_ref[i, c, 2 * hd :, n * hd : (n + 1) * hd] = piece


def parts_of(ref, i, c):
    hd = ref.shape[2] // 4
    return (
        ref[i, c, :hd, :],
        ref[i, c, hd : 2 * hd, :],
        ref[i, c, 2 * hd :, :hd],
        ref[i, c, 2 * hd :, hd:],
    )


def prep_kernel(qb, heads, x_ref, w_ref, q_ref, do_ref, gate_ref, stack_ref):
    nt = (((1,), (1,)), ((), ()))
    z = lax.dot_general(w_ref[...], x_ref[...], nt, preferred_element_type=F32)
    zt = jax.nn.sigmoid(z)
    for i in range(qb):
        for branch in range(2):
            for h in range(heads):
                row = branch * heads + h
                gate_ref[i, branch : branch + 1, h * BLK : (h + 1) * BLK] = zt[
                    row : row + 1, i * BLK : (i + 1) * BLK
                ]
    restack(heads, q_ref, do_ref, stack_ref)


def fold(x, op):
    return op(x.reshape(x.shape[0] // 8, 8, x.shape[1]), axis=0)


def branch_grad(parts, gate, s_scr, u_scr, w_scr, d_scr):
    c2 = 128 ** -0.5 * LOG2E
    top = jnp.full((8, LANES), NEG, F32)
    for at, live, mask in parts:
        s = s_scr[at, :]
        if mask is not None:
            s = jnp.where(mask, s, NEG)
            s_scr[at, :] = s
        part = fold(s, jnp.max)
        top = jnp.maximum(top, part if live is None else jnp.where(live, part, NEG))
    top = jnp.max(top, axis=0, keepdims=True) * c2
    total = jnp.zeros((8, LANES), F32)
    mixed = jnp.zeros((8, LANES), F32)
    for at, live, mask in parts:
        e = jnp.exp2(s_scr[at, :] * c2 - (top if live is None else jnp.where(live, top, -NEG)))
        total = total + fold(e, jnp.sum)
        mixed = mixed + fold(e * u_scr[at, :], jnp.sum)
        s_scr[at, :] = e
    inv = 1.0 / jnp.sum(total, axis=0, keepdims=True)
    d_gate = jnp.sum(mixed, axis=0, keepdims=True) * inv
    weight = gate * inv
    for at, live, mask in parts:
        pw = s_scr[at, :] * weight
        w_scr[at, :] = pw.astype(BF16)
        d_scr[at, :] = (pw * (u_scr[at, :] - d_gate)).astype(BF16)
    return d_gate


def lanes_of(c):
    return slice(c * LANES, (c + 1) * LANES)


def gather(me, row, reach, own_ref, picks_ref, offset, out):
    out[:BLK, :] = own_ref[row * BLK : (row + 1) * BLK, :]
    for n, (_, r) in enumerate(reach):
        src = jnp.where(me >= r, me - r, me)
        out[(n + 1) * BLK : (n + 2) * BLK, :] = picks_ref[src, offset : offset + BLK, :]


def spread(row_vectors, columns, out_ref, heads, first_row):
    for h in range(heads):
        out_ref[first_row + h : first_row + h + 1, columns] = row_vectors[:, h * BLK : (h + 1) * BLK]


def attend_kernel(ranks, qb, heads, lists, p, *refs):
    rank_ref, sel_ref, stack_hbm, k_ref, v_ref, gate_ref, picks_hbm = refs[:7]
    if p == 0:
        refs = refs[7:]
    else:
        dc_ref, *refs = refs[7:]
    own_hbm, dg_ref, dsel_hbm, send_hbm, kcat, vcat, s_scr, u_scr, w_scr, dv_acc, dk_acc = refs[:11]
    own_ref, dsel_ref, send_ref, stack, picks_ref, sems = refs[11:]
    hd = k_ref.shape[1]
    scale = hd ** -0.5
    me = rank_ref[0]
    chunks = heads * BLK // LANES
    copies = []

    def put(src, dst):
        copy = pltpu.make_async_copy(src, dst, sems.at[len(copies)])
        copy.start()
        copies.append(copy)

    put(picks_hbm.at[:, : 2 * BLK, :], picks_ref)
    for g in range(2 * chunks):
        put(stack_hbm.at[g // chunks, g % chunks], stack.at[g // chunks, g % chunks])

    send_ref[me] = jnp.zeros(send_ref.shape[1:], BF16)
    for parity, reach in enumerate(lists):
        if (1 + len(reach)) * BLK < dsel_ref.shape[2]:
            dsel_ref[parity, :, (1 + len(reach)) * BLK :, :] = jnp.zeros(
                (dsel_ref.shape[1], dsel_ref.shape[2] - (1 + len(reach)) * BLK, LANES), BF16
            )
    if p == 0:
        fill_picks(ranks, qb, lists, 1, me, sel_ref, k_ref, v_ref, send_ref)
    else:
        for r in range(1, ranks):
            dest = jnp.where(me >= r, me - r, me)
            at = slice(r * qb, (r + 1) * qb)
            piece = jnp.concatenate([dc_ref[at, :hd], dc_ref[at, hd:]], axis=0)
            send_ref[dest, 2 * BLK :, :] = piece.astype(BF16)

    key_pos = lax.broadcasted_iota(jnp.int32, (BLK, LANES), 0)
    tok_pos = lax.rem(lax.broadcasted_iota(jnp.int32, (BLK, LANES), 1), BLK)
    causal = key_pos <= tok_pos
    parts, sizes = [], []
    for parity, reach in enumerate(lists):
        parts.append([(slice(0, BLK), None, causal)])
        for n, (_, r) in enumerate(reach):
            parts[-1].append((slice((n + 1) * BLK, (n + 2) * BLK), me >= r, None))
        sizes.append((1 + len(reach)) * BLK)

    def fetch(parity):
        row = 2 * p + parity
        gather(me, row, lists[parity], k_ref, picks_ref, 0, kcat.at[parity])
        gather(me, row, lists[parity], v_ref, picks_ref, BLK, vcat.at[parity])

    def scores(g):
        parity, c = g // chunks, g % chunks
        nk = sizes[parity]
        copies[1 + g].wait()
        qt, dt, _, _ = parts_of(stack, parity, c)
        s_scr[g % 2, :nk, :] = jnp.dot(kcat[parity, :nk, :], qt, preferred_element_type=F32)
        u_scr[g % 2, :nk, :] = jnp.dot(vcat[parity, :nk, :], dt, preferred_element_type=F32)

    def soften(g):
        parity, lanes = g // chunks, lanes_of(g % chunks)
        gate = gate_ref[2 * p + parity, 1:2, lanes]
        dg = branch_grad(
            parts[parity], gate, s_scr.at[g % 2], u_scr.at[g % 2], w_scr.at[g % 2],
            dsel_ref.at[parity, g % chunks],
        )
        put(dsel_ref.at[parity, g % chunks], dsel_hbm.at[parity, g % chunks])
        dg_ref[parity : parity + 1, lanes] = dg * gate * (1.0 - gate)

    def gradients(g):
        parity, c = g // chunks, g % chunks
        nk = sizes[parity]
        _, _, qs, ds = parts_of(stack, parity, c)
        dv = jnp.dot(w_scr[g % 2, :nk, :], ds, preferred_element_type=F32)
        dk = jnp.dot(dsel_ref[parity, c, :nk, :], qs, preferred_element_type=F32)
        if c == 0:
            dv_acc[parity, :nk, :] = dv
            dk_acc[parity, :nk, :] = dk
        else:
            dv_acc[parity, :nk, :] += dv
            dk_acc[parity, :nk, :] += dk

    def deliver(parity):
        rows = slice(parity * BLK, (parity + 1) * BLK)
        own_ref[rows, :hd] = dk_acc[parity, :BLK, :] * scale
        own_ref[rows, hd:] = dv_acc[parity, :BLK, :]
        put(own_ref.at[rows], own_hbm.at[rows])
        for n, (_, r) in enumerate(lists[parity]):
            at = slice((n + 1) * BLK, (n + 2) * BLK)
            dest = jnp.where(me >= r, me - r, me)
            send_ref[dest, :BLK, :] = (dk_acc[parity, at, :] * scale).astype(BF16)
            send_ref[dest, BLK : 2 * BLK, :] = dv_acc[parity, at, :].astype(BF16)

    copies[0].wait()
    fetch(0)
    scores(0)
    fetch(1)
    for g in range(2 * chunks):
        if g + 1 < 2 * chunks:
            scores(g + 1)
        if g > 0:
            gradients(g - 1)
        if g == chunks:
            deliver(0)
        soften(g)
    gradients(2 * chunks - 1)
    deliver(1)
    put(send_ref, send_hbm)
    for copy in copies[1 + 2 * chunks :]:
        copy.wait()


def write_dq(row, heads, hd, pairs, dq_ref):
    per = LANES // BLK
    rows = slice(row * BLK, (row + 1) * BLK)
    for c in range(heads // per):
        total = None
        for kt, d_of in pairs:
            part = jnp.dot(kt, d_of(c), preferred_element_type=F32)
            total = part if total is None else total + part
        dq = (total.T * hd ** -0.5).astype(BF16)
        for h in range(per):
            head = c * per + h
            dq_ref[rows, head * hd : (head + 1) * hd] = dq[h * BLK : (h + 1) * BLK, :]


def turned(x):
    return x.astype(F32).T.astype(BF16)


def middle_kernel(ranks, qb, heads, lists, rank_ref, stack0, q_ref, do_ref, k_ref, gate_ref,
                  fetched_ref, dsel_ref, dg_ref, dq_ref, dz_ref, dc_ref, dcomp_ref, kct_ref,
                  stack1, kcat, ckey, cval, s_scr, u_scr, w_scr, d_scr):
    hd = k_ref.shape[1]
    me = rank_ref[0]
    nblocks = ranks * qb
    chunks = heads * BLK // LANES
    span = min(nblocks, BLK)
    pieces = []
    for r in range(ranks):
        pieces.append(fetched_ref[jnp.maximum(me - r, 0), 2 * BLK :, :].astype(F32))
    ckey[...] = jnp.concatenate([x[:qb] for x in pieces], axis=0).astype(BF16)
    cval[...] = jnp.concatenate([x[qb:] for x in pieces], axis=0).astype(BF16)
    kct_ref[...] = turned(ckey[...])
    dz_ref[...] = jnp.zeros_like(dz_ref)
    restack(heads, q_ref, do_ref, stack1)

    for row in range(qb):
        stack = stack0 if row < 2 else stack1
        parts = []
        for n in range(nblocks // span):
            place = lax.broadcasted_iota(jnp.int32, (span, LANES), 0) + n * span
            away, within = place // qb, lax.rem(place, qb)
            seen = (away <= me) & ((away > 0) | (within <= row))
            parts.append((slice(n * span, (n + 1) * span), None, seen))
        dgs, dvs, dks = [], [], []
        for c in range(chunks):
            lanes = lanes_of(c)
            qt, dt, qs, ds = parts_of(stack, row % 2, c)
            s_scr[c % 2] = jnp.dot(ckey[...], qt, preferred_element_type=F32)
            u_scr[c % 2] = jnp.dot(cval[...], dt, preferred_element_type=F32)
            gate = gate_ref[row, 0:1, lanes]
            dg = branch_grad(parts, gate, s_scr.at[c % 2], u_scr.at[c % 2], w_scr.at[:, lanes], d_scr.at[row, :, lanes])
            dgs.append(dg * gate * (1.0 - gate))
            dvs.append(jnp.dot(w_scr[:, lanes], ds, preferred_element_type=F32))
            dks.append(jnp.dot(d_scr[row, :, lanes], qs, preferred_element_type=F32))
        dv = sum(dvs[1:], dvs[0])
        dk = sum(dks[1:], dks[0]) * hd ** -0.5
        if row == 0:
            dc_ref[:, :hd] = dk
            dc_ref[:, hd:] = dv
        else:
            dc_ref[:, :hd] += dk
            dc_ref[:, hd:] += dv
        columns = slice(row * BLK, (row + 1) * BLK)
        spread(jnp.concatenate(dgs, axis=1), columns, dz_ref, heads, 0)

    for parity, reach in enumerate(lists):
        nk = (1 + len(reach)) * BLK
        gather(me, parity, reach, k_ref, fetched_ref, 0, kcat)
        write_dq(
            parity, heads, hd,
            [
                (turned(kcat[:nk, :]), lambda c, nk=nk, parity=parity: dsel_ref[parity, c, :nk, :]),
                (kct_ref[...], lambda c, parity=parity: d_scr[parity, :, lanes_of(c)]),
            ],
            dq_ref,
        )
        spread(dg_ref[parity : parity + 1, :], slice(parity * BLK, (parity + 1) * BLK), dz_ref, heads, heads)
    for i in range(2):
        dcomp_ref[i] = d_scr[2 + i]


def tail_kernel(ranks, qb, heads, lists, rank_ref, k_ref, picks_ref, dsel_ref, dcomp_ref, kct_ref, _, dq_ref, kcat):
    hd = k_ref.shape[1]
    me = rank_ref[0]
    for parity, reach in enumerate(lists):
        nk = (1 + len(reach)) * BLK
        gather(me, 2 + parity, reach, k_ref, picks_ref, 0, kcat)
        write_dq(
            parity, heads, hd,
            [
                (turned(kcat[:nk, :]), lambda c, nk=nk, parity=parity: dsel_ref[parity, c, :nk, :]),
                (kct_ref[...], lambda c, parity=parity: dcomp_ref[parity, :, lanes_of(c)]),
            ],
            dq_ref,
        )


def dz_kernel(heads, dz_in, dg_ref, dz_ref):
    dz = dz_in[...]
    dz_ref[...] = dz
    for i in range(2):
        spread(dg_ref[i : i + 1, :], slice((2 + i) * BLK, (3 + i) * BLK), dz_ref, heads, heads)


def add_homes(ranks, qb, lists, p, me, sel_ref, home_ref, acc):
    hd = home_ref.shape[2]
    for parity, reach in enumerate(lists):
        for j, r in reach:
            src = jnp.minimum(me + r, ranks - 1)
            named = sel_ref[j, src * qb + 2 * p + parity]
            local = jnp.clip(named - me * qb, 0, qb - 1)
            rows = pl.ds(pl.multiple_of(local * BLK, BLK), BLK)
            live = me + r < ranks
            acc[rows, :hd] += jnp.where(live, home_ref[src, :BLK, :].astype(F32), 0.0)
            acc[rows, hd:] += jnp.where(live, home_ref[src, BLK : 2 * BLK, :].astype(F32), 0.0)


def collect_kernel(ranks, qb, lists, rank_ref, sel_ref, own0_ref, own1_ref, home_ref, acc_ref):
    acc_ref[: 2 * BLK, :] = own0_ref[...]
    acc_ref[2 * BLK :, :] = own1_ref[...]
    add_homes(ranks, qb, lists, 0, rank_ref[0], sel_ref, home_ref, acc_ref)


def finish_kernel(ranks, qb, lists, rank_ref, sel_ref, part_ref, dc_ref, home_ref,
                  dk_ref, dv_ref, dck_ref, dcv_ref, acc):
    hd = dk_ref.shape[1]
    me = rank_ref[0]
    acc[...] = part_ref[...]
    add_homes(ranks, qb, lists, 1, me, sel_ref, home_ref, acc)
    dk_ref[...] = acc[:, :hd].astype(BF16)
    dv_ref[...] = acc[:, hd:].astype(BF16)

    def add(n, total):
        return total + home_ref[n, 2 * BLK :, :].astype(F32)

    total = lax.fori_loop(me + 1, ranks, add, jnp.zeros((2 * qb, hd), F32))
    dck_ref[...] = (total[:qb] + dc_ref[:qb, :hd]).astype(BF16)
    dcv_ref[...] = (total[qb:] + dc_ref[:qb, hd:]).astype(BF16)


def body(queries, keys, values, comp_keys, comp_values, selected, inputs, w_gate, d_out):
    tokens, width = queries.shape
    hd = keys.shape[1]
    heads = width // hd
    qb = tokens // BLK
    pair = qb // 2
    ranks = lax.axis_size("ctx")
    rank = lax.axis_index("ctx").astype(jnp.int32)
    me = rank.reshape(1)
    head = lax.axis_index("head")
    nblocks = ranks * qb
    lists = reach_lists(ranks)
    table = selected.T

    slot = 2 * BLK + 2 * qb

    def exchange(x):
        return lax.all_to_all(x, "ctx", split_axis=0, concat_axis=0, tiled=True)

    send = pl.pallas_call(
        functools.partial(pack_kernel, ranks, qb, lists),
        out_shape=jax.ShapeDtypeStruct((ranks, slot, hd), BF16),
        in_specs=[in_smem(), in_smem()] + [in_vmem()] * 4,
        out_specs=in_vmem(),
        compiler_params=params(),
        name="pack",
    )(me, table, keys, values, comp_keys, comp_values)
    fetched = exchange(send)

    def call(kernel, outs, args, name, scratch=(), specs=None, out_specs=None, aliases=None, cost=0, grid=(), sems=0):
        return pl.pallas_call(
            kernel,
            grid=grid,
            out_shape=[jax.ShapeDtypeStruct(shape, dtype) for shape, dtype in outs],
            in_specs=specs or [in_vmem()] * len(args),
            out_specs=out_specs or [in_vmem()] * len(outs),
            scratch_shapes=[pltpu.VMEM(shape, dtype) for shape, dtype in scratch]
            + [pltpu.SemaphoreType.DMA((sems,))] * (sems > 0),
            input_output_aliases=aliases or {},
            compiler_params=params(),
            cost_estimate=pl.CostEstimate(flops=cost, bytes_accessed=4 << 20, transcendentals=0),
            name=name,
        )(*args)

    wide = heads * BLK
    chunks = wide // LANES
    stack_shape = (2, chunks, 4 * hd, LANES)

    def rows_of(p):
        return pl.BlockSpec((2 * BLK, width), lambda i: (p, 0))

    gate, stack0 = call(
        functools.partial(prep_kernel, qb, heads),
        [((qb, 2, wide), F32), (stack_shape, BF16)],
        [inputs, w_gate.T, queries, d_out],
        "prep",
        specs=[in_vmem()] * 2 + [rows_of(0)] * 2,
        grid=(1,),
        cost=2 * inputs.size * w_gate.shape[1],
    )
    half = w_gate.shape[0] // 2
    swap = [(0, 1), (1, 0)]
    w_send = lax.dynamic_slice_in_dim(w_gate, (1 - head) * half, half, 0)
    w_mine = lax.dynamic_slice_in_dim(w_gate, head * half, half, 0)
    w_other = lax.ppermute(w_send, "head", swap)

    nsel = (1 + max(len(x) for x in lists)) * BLK
    smem2 = [in_smem(), in_smem()]

    in_any = pl.BlockSpec(memory_space=pl.ANY)

    def attend(p, picks, stack, previous):
        args = [me, table, stack, keys, values, gate, picks] + previous
        own, dsel, send = (2 * BLK, 2 * hd), (2, chunks, nsel, LANES), (ranks, slot if p else 2 * BLK, hd)
        return call(
            functools.partial(attend_kernel, ranks, qb, heads, lists, p),
            [(own, F32), ((2, wide), F32), (dsel, BF16), (send, BF16)],
            args,
            f"attend{p}",
            specs=smem2 + [in_any] + [in_vmem()] * 3 + [in_any] + [in_vmem()] * len(previous),
            out_specs=[in_any, in_vmem(), in_any, in_any],
            scratch=[
                ((2, nsel, hd), BF16),
                ((2, nsel, hd), BF16),
                ((2, nsel, LANES), F32),
                ((2, nsel, LANES), F32),
                ((2, nsel, LANES), BF16),
                ((2, nsel, hd), F32),
                ((2, nsel, hd), F32),
                (own, F32),
                (dsel, BF16),
                (send, BF16),
                (stack_shape, BF16),
                ((ranks, 2 * BLK, hd), BF16),
            ],
            sems=4 * chunks + 4,
            cost=8 * nsel * wide * 2 * hd,
        )

    own0, dg0, dsel0, send = attend(0, fetched, stack0, [])
    mixed = exchange(send)
    dq, dz, dc, dcomp, kct, stack1 = call(
        functools.partial(middle_kernel, ranks, qb, heads, lists),
        [
            (queries.shape, BF16),
            ((2 * heads, tokens), F32),
            ((nblocks, 2 * hd), F32),
            ((2, nblocks, wide), BF16),
            ((hd, nblocks), BF16),
            (stack_shape, BF16),
        ],
        [me, stack0, queries, d_out, keys, gate, fetched, dsel0, dg0],
        "middle",
        specs=[in_smem(), in_vmem()] + [rows_of(1)] * 2 + [in_vmem()] * 5,
        out_specs=[rows_of(0)] + [in_vmem()] * 5,
        grid=(1,),
        scratch=[
            ((nsel, hd), BF16),
            ((nblocks, hd), BF16),
            ((nblocks, hd), BF16),
            ((2, nblocks, LANES), F32),
            ((2, nblocks, LANES), F32),
            ((nblocks, wide), BF16),
            ((qb, nblocks, wide), BF16),
        ],
        cost=10 * nblocks * wide * qb * hd,
    )
    own1, dg1, dsel1, send = attend(1, mixed, stack1, [dc])
    home = exchange(send)
    (dz,) = call(functools.partial(dz_kernel, heads), [((2 * heads, tokens), F32)], [dz, dg1], "dz")
    (d_queries,) = call(
        functools.partial(tail_kernel, ranks, qb, heads, lists),
        [(queries.shape, BF16)],
        [me, keys, mixed, dsel1, dcomp, kct, dq],
        "tail",
        specs=[in_smem()] + [in_vmem()] * 5 + [pl.BlockSpec(memory_space=pl.ANY)],
        out_specs=[rows_of(1)],
        grid=(1,),
        scratch=[((nsel, hd), BF16)],
        aliases={6: 0},
        cost=2 * nsel * wide * 2 * hd,
    )

    part = pl.pallas_call(
        functools.partial(collect_kernel, ranks, qb, lists),
        out_shape=jax.ShapeDtypeStruct((tokens, 2 * hd), F32),
        in_specs=[in_smem(), in_smem()] + [in_vmem()] * 3,
        out_specs=in_vmem(),
        compiler_params=params(),
        name="collect",
    )(me, table, own0, own1, mixed)
    d_keys, d_values, d_ck, d_cv = pl.pallas_call(
        functools.partial(finish_kernel, ranks, qb, lists),
        out_shape=[
            jax.ShapeDtypeStruct(x.shape, BF16) for x in (keys, values, comp_keys, comp_values)
        ],
        in_specs=[in_smem(), in_smem()] + [in_vmem()] * 3,
        out_specs=[in_vmem()] * 4,
        scratch_shapes=[pltpu.VMEM((tokens, 2 * hd), F32)],
        compiler_params=params(),
        name="finish",
    )(me, table, part, dc, home)

    dz = dz.astype(BF16)
    dz_other = lax.ppermute(dz, "head", swap)
    tn = (((0,), (1,)), ((), ()))
    d_inputs = (
        lax.dot_general(dz, w_mine, tn, preferred_element_type=F32)
        + lax.dot_general(dz_other, w_other, tn, preferred_element_type=F32)
    ).astype(BF16)

    return d_queries, d_keys, d_values, d_ck, d_cv, d_inputs


def solution(mesh):
    split = P("ctx", "head")
    in_specs = (split,) * 5 + (P(), P("ctx", None), P(None, "head"), split)
    return jax.shard_map(
        body, mesh=mesh, in_specs=in_specs, out_specs=(split,) * 6, check_vma=False
    )
```

time: 376 us -> 84.1 us (0.22)
  matrix products: 120 us -> 1.55 us
  blocking collectives: 107 us -> 0 us
  local copies, waits for them, and re-layouts: 51.1 us -> 2.43 us
  Pallas kernels: 0 us -> 37.9 us
  other arithmetic: 30.1 us -> 0.76 us
  between operations: 15.1 us -> 0.71 us
  loops' own time: 11.1 us -> 0 us
    dot_general x44 -> x2, matrix products: 105 us -> 1.55 us  [the longest x1 1.2 us: body(): lax.dot_general(dz_other, w_other, tn, preferred_element_type=F32)]
    unnamed x1 -> x0, blocking collectives: 63.3 us -> none
    all_gather x2 -> x0, blocking collectives: 43.6 us -> none  [the longest x1 24.8 us: body(): lax.all_gather(comp_keys, 'ctx', axis=0, tiled=True)]
    pallas_call x0 -> x9, Pallas kernels: none -> 37.9 us  [the longest x6 31.9 us: call(): pl.pallas_call(kernel, grid=grid, out_shape=[jax.ShapeDtypeStruct(shape,...]
    convert_element_type x13 -> x1, other arithmetic: 20.2 us -> 0.76 us  [body(): dz = dz.astype(BF16)]
    sub x8 -> x0, matrix products: 15.5 us -> none  [attend(): expo = jnp.exp(scores - top)]
    dynamic_update_slice x20 -> x0, local copies, waits for them, and re-layouts: 14.5 us -> none  [body(): lax.scan(step, start, jnp.arange(blocks_here, dtype=jnp.int32))]
    scatter x2 -> x0, local copies, waits for them, and re-layouts: 13.4 us -> none  [the longest x1 6.76 us: body(): empty.at[slot].set(outs[4].reshape(entries, BLK, head_size), mode='drop')]
  transfers between devices with their start and end apart: 5 -> 5, of which waited for: 2 -> 3; matrix products, arithmetic and copies ran while one was open for 5% -> 3% of each run, Pallas kernels for 0% -> 22%
where the time goes in v1:
time: 84.1 us; the launch traced here: 83.3 us
  Pallas kernels  37.9 us (45%)
  waiting for transfers between devices  22.1 us (26%)
  starting transfers between devices  17.8 us (21%)
  local copies, waits for them, and re-layouts  2.43 us (3%)
  matrix products  1.55 us (2%)
    pallas_call x6, Pallas kernels, call(): pl.pallas_call(kernel, grid=grid, out_shape=[jax.ShapeDtypeStruct(shape,...  31.9 us
    all_to_all x3, waiting for transfers between devices, exchange(): return lax.all_to_all(x, 'ctx', split_axis=0, concat_axis=0, tiled=True)  22.1 us
    all_to_all x3, starting transfers between devices, exchange(): return lax.all_to_all(x, 'ctx', split_axis=0, concat_axis=0, tiled=True)  15.7 us
    unnamed x8, local copies, waits for them, and re-layouts  2.41 us
    pallas_call x1, Pallas kernels, body(): pl.pallas_call(functools.partial(finish_kernel, ranks, qb, lists), out_sh...  2.08 us
    pallas_call x1, Pallas kernels, body(): pl.pallas_call(functools.partial(collect_kernel, ranks, qb, lists), out_s...  2.04 us
    pallas_call x1, Pallas kernels, body(): pl.pallas_call(functools.partial(pack_kernel, ranks, qb, lists), out_shap...  1.93 us
  transfers between devices with their start and end apart: 5, of which 3 were waited for; matrix products, arithmetic and copies ran while one was open for 3% of the time, Pallas kernels for 22%

profile of v1, /device:TPU:0, one launch (start us, length us, event | category | flops | bytes accessed | tf_op | source)
XLA Modules:
  0.0 83.3 jit_solution(13090007964709384880)
XLA Ops:
  0.6 1.9 %pack.1 = bf16[16,136,128]{2,1,0:T(8,128)(2,1)} custom-call(s32[1]{0:T(128)} %bitcast.rank_ref.refs_0_, s32[15,64]{1,0:T(8,128)} %bitcast.7, bf16[256,128]{1,0:T(8,128)(2,1)} %k_ref.5, bf16[256,128]{1,0:T(8,128)(2,1)} %refs_4_.3, bf16[4,128]{1,0:T(4,128)(2,1)} %ck_ref.1, bf16[4,128]{1,0:T(4,128)(2,1)} %cv_ref.1), custom_call_target="tpu_custom_call" | custom-call | tf_op jit(solution)/shard_map/pack/pallas_call | solution.py:430
  2.6 7.4 %all-to-all-start = ((bf16[16,136,128]{2,1,0:T(8,128)(2,1)}), bf16[16,136,128]{2,1,0:T(8,128)(2,1)S(1)}, u32[]{:S(2)}, u32[]{:S(2)}) async-start(bf16[16,136,128]{2,1,0:T(8,128)(2,1)} %pack.1), calls=%async_computation | async-start | bytes 1114112 | tf_op jit(solution)/shard_map/all_to_all | solution.py:428
  9.9 3.8 %prep.1 = (f32[4,2,1024]{2,1,0:T(2,128)}, bf16[2,4,512,256]{3,2,1,0:T(8,128)(2,1)}) custom-call(bf16[256,2560]{1,0:T(8,128)(2,1)} %x_ref.1, bf16[32,2560]{1,0:T(8,128)(2,1)} %bitcast.6, bf16[256,2048]{1,0:T(8,128)(2,1)} %q_ref.3, bf16[256,2048]{1,0:T(8,128)(2,1)} %do_ref.3), custom_call_target="tpu_custom_call" | custom-call | flops 41943040 | bytes 4194304 | tf_op jit(solution)/shard_map/prep/pallas_call | solution.py:441
  13.7 11.2 %all-to-all-done.refs_6_.fetched_ref = bf16[16,136,128]{2,1,0:T(8,128)(2,1)S(1)} async-done(((bf16[16,136,128]{2,1,0:T(8,128)(2,1)}), bf16[16,136,128]{2,1,0:T(8,128)(2,1)S(1)}, u32[]{:S(2)}, u32[]{:S(2)}) %all-to-all-start) | async-done | bytes 557088 | tf_op jit(solution)/shard_map/all_to_all | solution.py:428
  25.0 0.0 copy-start.1
  25.0 0.8 copy-done.1
  25.8 8.0 %attend0.1 = (f32[128,256]{1,0:T(8,128)}, f32[2,1024]{1,0:T(2,128)}, bf16[2,4,576,256]{3,2,1,0:T(8,128)(2,1)}, bf16[16,128,128]{2,1,0:T(8,128)(2,1)}) custom-call(s32[1]{0:T(128)} %bitcast.rank_ref.refs_0_, s32[15,64]{1,0:T(8,128)} %bitcast.8, bf16[2,4,512,256]{3,2,1,0:T(8,128)(2,1)} %get-tuple-element.26.refs_2_.stack0, bf16[256,128]{1,0:T(8,128)(2,1)} %k_ref.5, ...), custom_call_target="tpu_custom_call" | custom-call | flops 1207959552 | bytes 4194304 | tf_op jit(solution)/shard_map/attend0/pallas_call | solution.py:441
  33.7 4.3 %all-to-all-start.1 = ((bf16[16,128,128]{2,1,0:T(8,128)(2,1)}), bf16[16,128,128]{2,1,0:T(8,128)(2,1)S(1)}, u32[]{:S(2)}, u32[]{:S(2)}) async-start(bf16[16,128,128]{2,1,0:T(8,128)(2,1)} %get-tuple-element.28), calls=%async_computation.1 | async-start | bytes 1048576 | tf_op jit(solution)/shard_map/all_to_all | solution.py:428
  38.0 7.2 %middle.1 = (bf16[256,2048]{1,0:T(8,128)(2,1)}, f32[32,256]{1,0:T(8,128)}, f32[64,256]{1,0:T(8,128)}, bf16[2,64,1024]{2,1,0:T(8,128)(2,1)}, bf16[128,64]{1,0:T(8,128)(2,1)}, /*index=5*/bf16[2,4,512,256]{3,2,1,0:T(8,128)(2,1)}) custom-call(s32[1]{0:T(128)} %bitcast.rank_ref.refs_0_, bf16[2,4,512,256]{3,2,1,0:T(8,128)(2,1)} %get-tuple-element.26.refs_2_.stack0, ...), custom_call_target="tpu_custom_call" | custom-call | flops 335544320 | bytes 4194304 | tf_op jit(solution)/shard_map/middle/pallas_call | solution.py:441
  45.2 7.3 %all-to-all-done.1.refs_6_.picks_ref.home_ref = bf16[16,128,128]{2,1,0:T(8,128)(2,1)S(1)} async-done(((bf16[16,128,128]{2,1,0:T(8,128)(2,1)}), bf16[16,128,128]{2,1,0:T(8,128)(2,1)S(1)}, u32[]{:S(2)}, u32[]{:S(2)}) %all-to-all-start.1) | async-done | bytes 524320 | tf_op jit(solution)/shard_map/all_to_all | solution.py:428
  52.5 0.0 copy-start
  52.5 0.8 copy-done
  53.3 0.0 copy-start.3
  53.3 7.9 %attend1.1 = (f32[128,256]{1,0:T(8,128)}, f32[2,1024]{1,0:T(2,128)}, bf16[2,4,576,256]{3,2,1,0:T(8,128)(2,1)}, bf16[16,136,128]{2,1,0:T(8,128)(2,1)}) custom-call(s32[1]{0:T(128)} %bitcast.rank_ref.refs_0_, s32[15,64]{1,0:T(8,128)} %bitcast.9, bf16[2,4,512,256]{3,2,1,0:T(8,128)(2,1)} %get-tuple-element.31.refs_2_, bf16[256,128]{1,0:T(8,128)(2,1)} %k_ref.5, ...), custom_call_target="tpu_custom_call" | custom-call | flops 1207959552 | bytes 4194304 | tf_op jit(solution)/shard_map/attend1/pallas_call | solution.py:441
  61.2 4.1 %all-to-all-start.2 = ((bf16[16,136,128]{2,1,0:T(8,128)(2,1)}), bf16[16,136,128]{2,1,0:T(8,128)(2,1)S(1)}, u32[]{:S(2)}, u32[]{:S(2)}) async-start(bf16[16,136,128]{2,1,0:T(8,128)(2,1)} %get-tuple-element.39), calls=%async_computation.2 | async-start | bytes 1114112 | tf_op jit(solution)/shard_map/all_to_all | solution.py:428
  65.3 0.0 copy-done.3
  65.4 1.6 %collective-permute-start.1 = (bf16[1280,32]{0,1:T(8,128)(2,1)S(1)}, bf16[1280,32]{0,1:T(8,128)(2,1)S(1)}, u32[]{:S(2)}, u32[]{:S(2)}) collective-permute-start(bf16[1280,32]{0,1:T(8,128)(2,1)S(1)} %constant_dynamic-slice_fusion), channel_id=1, source_target_pairs={{0,1},{1,0},{2,3},{3,2},{4,5},{5,4},{6,7},{7,6},{8,9},{9,8},{10,11... | collective-permute-start | bytes 245768 | tf_op jit(solution)/shard_map/ppermute | solution.py:475
  67.0 1.5 %dz.1 = f32[32,256]{1,0:T(8,128)} custom-call(f32[32,256]{1,0:T(8,128)} %get-tuple-element.44.dz_in, f32[2,1024]{1,0:T(2,128)} %get-tuple-element.45.dg_ref), custom_call_target="tpu_custom_call" | custom-call | bytes 4194304 | tf_op jit(solution)/shard_map/dz/pallas_call | solution.py:441
  68.4 0.8 convert_element_type.6
  69.2 0.5 collective-permute-start
  69.7 0.3 fusion.1
  70.0 2.0 %collect.1.part_ref = f32[256,256]{1,0:T(8,128)} custom-call(s32[1]{0:T(128)} %bitcast.rank_ref.refs_0_, s32[15,64]{1,0:T(8,128)} %bitcast.10, f32[128,256]{1,0:T(8,128)} %get-tuple-element.37.own0_ref, f32[128,256]{1,0:T(8,128)} %get-tuple-element.38.own1_ref, bf16[16,128,128]{2,1,0:T(8,128)(2,1)} %copy-done), custom_call_target="tpu_custom_call" | custom-call | tf_op jit(solution)/shard_map/collect/pallas_call | solution.py:554
  72.1 3.5 %tail.1 = bf16[256,2048]{1,0:T(8,128)(2,1)} custom-call(s32[1]{0:T(128)} %bitcast.rank_ref.refs_0_, bf16[256,128]{1,0:T(8,128)(2,1)} %k_ref.5, bf16[16,128,128]{2,1,0:T(8,128)(2,1)} %copy-done, bf16[2,4,576,256]{3,2,1,0:T(8,128)(2,1)} %get-tuple-element.33.dsel_ref, ...), custom_call_target="tpu_custom_call", output_to_operand_aliasing={{}: (6, {})} | custom-call | flops 301989888 | bytes 4194304 | tf_op jit(solution)/shard_map/tail/pallas_call | solution.py:441
  75.6 0.0 collective-permute-done.1
  75.6 0.0 collective-permute-done
  75.6 1.2 %fusion = bf16[256,1280]{1,0:T(8,128)(2,1)} fusion(f32[256,1280]{1,0:T(8,128)S(1)} %fusion.1, bf16[32,256]{1,0:T(8,128)(2,1)S(1)} %collective-permute-done, bf16[1280,32]{0,1:T(8,128)(2,1)S(1)} %collective-permute-done.1), kind=kOutput, calls=%fused_computation.1 | convolution fusion | flops 21626880 | bytes 2064384 | tf_op jit(solution)/shard_map/dot_general | solution.py:579
  76.8 3.6 %all-to-all-done.2.home_ref = bf16[16,136,128]{2,1,0:T(8,128)(2,1)S(1)} async-done(((bf16[16,136,128]{2,1,0:T(8,128)(2,1)}), bf16[16,136,128]{2,1,0:T(8,128)(2,1)S(1)}, u32[]{:S(2)}, u32[]{:S(2)}) %all-to-all-start.2) | async-done | bytes 557088 | tf_op jit(solution)/shard_map/all_to_all | solution.py:428
  80.4 0.0 copy-start.2
  80.4 0.8 copy-done.2
  81.2 2.1 %finish.1 = (bf16[256,128]{1,0:T(8,128)(2,1)}, bf16[256,128]{1,0:T(8,128)(2,1)}, bf16[4,128]{1,0:T(4,128)(2,1)}, bf16[4,128]{1,0:T(4,128)(2,1)}) custom-call(s32[1]{0:T(128)} %bitcast.rank_ref.refs_0_, s32[15,64]{1,0:T(8,128)} %bitcast.11, f32[256,256]{1,0:T(8,128)} %collect.1.part_ref, f32[64,256]{1,0:T(8,128)} %get-tuple-element.32.refs_7_.dc_ref, ...), custom_call_target="tpu_custom_call" | custom-call | tf_op jit(solution)/shard_map/finish/pallas_call | solution.py:562
  (1 shorter events, 0.0 us)
Async XLA Ops:
  2.6 22.4 %all-to-all-start = ((bf16[16,136,128]{2,1,0:T(8,128)(2,1)}), bf16[16,136,128]{2,1,0:T(8,128)(2,1)S(1)}, u32[]{:S(2)}, u32[]{:S(2)}) async-start(bf16[16,136,128]{2,1,0:T(8,128)(2,1)} %pack.1), calls=%async_computation | async-start | bytes 1114112 | tf_op jit(solution)/shard_map/all_to_all | solution.py:428
  25.0 0.8 copy-start.1
  33.7 18.7 %all-to-all-start.1 = ((bf16[16,128,128]{2,1,0:T(8,128)(2,1)}), bf16[16,128,128]{2,1,0:T(8,128)(2,1)S(1)}, u32[]{:S(2)}, u32[]{:S(2)}) async-start(bf16[16,128,128]{2,1,0:T(8,128)(2,1)} %get-tuple-element.28), calls=%async_computation.1 | async-start | bytes 1048576 | tf_op jit(solution)/shard_map/all_to_all | solution.py:428
  52.5 0.8 copy-start
  53.3 12.1 %copy-start.3 = (bf16[2560,32]{0,1:T(8,128)(2,1)S(1)}, bf16[2560,32]{0,1:T(8,128)(2,1)}, u32[]{:S(2)}) copy-start(bf16[2560,32]{0,1:T(8,128)(2,1)} %param.16) | copy-start | bytes 491524
  61.2 19.1 %all-to-all-start.2 = ((bf16[16,136,128]{2,1,0:T(8,128)(2,1)}), bf16[16,136,128]{2,1,0:T(8,128)(2,1)S(1)}, u32[]{:S(2)}, u32[]{:S(2)}) async-start(bf16[16,136,128]{2,1,0:T(8,128)(2,1)} %get-tuple-element.39), calls=%async_computation.2 | async-start | bytes 1114112 | tf_op jit(solution)/shard_map/all_to_all | solution.py:428
  65.4 10.2 %collective-permute-start.1 = (bf16[1280,32]{0,1:T(8,128)(2,1)S(1)}, bf16[1280,32]{0,1:T(8,128)(2,1)S(1)}, u32[]{:S(2)}, u32[]{:S(2)}) collective-permute-start(bf16[1280,32]{0,1:T(8,128)(2,1)S(1)} %constant_dynamic-slice_fusion), channel_id=1, source_target_pairs={{0,1},{1,0},{2,3},{3,2},{4,5},{5,4},{6,7},{7,6},{8,9},{9,8},{10,11... | collective-permute-start | bytes 245768 | tf_op jit(solution)/shard_map/ppermute | solution.py:475
  69.2 6.4 %collective-permute-start = (bf16[32,256]{1,0:T(8,128)(2,1)S(1)}, bf16[32,256]{1,0:T(8,128)(2,1)S(1)}, u32[]{:S(2)}, u32[]{:S(2)}) collective-permute-start(bf16[32,256]{1,0:T(8,128)(2,1)S(1)} %convert_element_type.6), channel_id=1, source_target_pairs={{0,1},{1,0},{2,3},{3,2},{4,5},{5,4},{6,7},{7,6},{8,9},{9,8},{10,11... | collective-permute-start | bytes 49160 | tf_op jit(solution)/shard_map/ppermute | solution.py:575
  80.4 0.8 copy-start.2

commit v2 on v1

--- a/solution.py
+++ b/solution.py
@@ -36,8 +36,8 @@
     return pl.BlockSpec(memory_space=pltpu.SMEM)
 
 
-def params():
-    return pltpu.CompilerParams(vmem_limit_bytes=60 * 1024 * 1024)
+def params(ranks, limit=16):
+    return pltpu.CompilerParams(vmem_limit_bytes=(limit if ranks <= 16 else 60) * 1024 * 1024)
 
 
 def fill_picks(ranks, qb, lists, p, me, sel_ref, k_ref, v_ref, out_ref):
@@ -155,13 +155,13 @@
 
 
 def attend_kernel(ranks, qb, heads, lists, p, *refs):
-    rank_ref, sel_ref, stack_hbm, k_ref, v_ref, gate_ref, picks_hbm = refs[:7]
+    rank_ref, sel_ref, stack, k_ref, v_ref, gate_ref, picks_ref = refs[:7]
     if p == 0:
         refs = refs[7:]
     else:
         dc_ref, *refs = refs[7:]
-    own_hbm, dg_ref, dsel_hbm, send_hbm, kcat, vcat, s_scr, u_scr, w_scr, dv_acc, dk_acc = refs[:11]
-    own_ref, dsel_ref, send_ref, stack, picks_ref, sems = refs[11:]
+    own_hbm, dg_ref, dsel_hbm, send_ref, kcat, vcat, s_scr, u_scr, w_scr, dv_acc, dk_acc = refs[:11]
+    own_ref, dsel_ref, sems = refs[11:]
     hd = k_ref.shape[1]
     scale = hd ** -0.5
     me = rank_ref[0]
@@ -172,10 +172,6 @@
         copy = pltpu.make_async_copy(src, dst, sems.at[len(copies)])
         copy.start()
         copies.append(copy)
-
-    put(picks_hbm.at[:, : 2 * BLK, :], picks_ref)
-    for g in range(2 * chunks):
-        put(stack_hbm.at[g // chunks, g % chunks], stack.at[g // chunks, g % chunks])
 
     send_ref[me] = jnp.zeros(send_ref.shape[1:], BF16)
     for parity, reach in enumerate(lists):
@@ -210,7 +206,6 @@
     def scores(g):
         parity, c = g // chunks, g % chunks
         nk = sizes[parity]
-        copies[1 + g].wait()
         qt, dt, _, _ = parts_of(stack, parity, c)
         s_scr[g % 2, :nk, :] = jnp.dot(kcat[parity, :nk, :], qt, preferred_element_type=F32)
         u_scr[g % 2, :nk, :] = jnp.dot(vcat[parity, :nk, :], dt, preferred_element_type=F32)
@@ -249,7 +244,6 @@
             send_ref[dest, :BLK, :] = (dk_acc[parity, at, :] * scale).astype(BF16)
             send_ref[dest, BLK : 2 * BLK, :] = dv_acc[parity, at, :].astype(BF16)
 
-    copies[0].wait()
     fetch(0)
     scores(0)
     fetch(1)
@@ -263,8 +257,7 @@
         soften(g)
     gradients(2 * chunks - 1)
     deliver(1)
-    put(send_ref, send_hbm)
-    for copy in copies[1 + 2 * chunks :]:
+    for copy in copies:
         copy.wait()
 
 
@@ -432,12 +425,12 @@
         out_shape=jax.ShapeDtypeStruct((ranks, slot, hd), BF16),
         in_specs=[in_smem(), in_smem()] + [in_vmem()] * 4,
         out_specs=in_vmem(),
-        compiler_params=params(),
+        compiler_params=params(ranks, 60),
         name="pack",
     )(me, table, keys, values, comp_keys, comp_values)
     fetched = exchange(send)
 
-    def call(kernel, outs, args, name, scratch=(), specs=None, out_specs=None, aliases=None, cost=0, grid=(), sems=0):
+    def call(kernel, outs, args, name, scratch=(), specs=None, out_specs=None, aliases=None, cost=0, grid=(), sems=0, limit=16):
         return pl.pallas_call(
             kernel,
             grid=grid,
@@ -447,7 +440,7 @@
             scratch_shapes=[pltpu.VMEM(shape, dtype) for shape, dtype in scratch]
             + [pltpu.SemaphoreType.DMA((sems,))] * (sems > 0),
             input_output_aliases=aliases or {},
-            compiler_params=params(),
+            compiler_params=params(ranks, limit),
             cost_estimate=pl.CostEstimate(flops=cost, bytes_accessed=4 << 20, transcendentals=0),
             name=name,
         )(*args)
@@ -487,8 +480,8 @@
             [(own, F32), ((2, wide), F32), (dsel, BF16), (send, BF16)],
             args,
             f"attend{p}",
-            specs=smem2 + [in_any] + [in_vmem()] * 3 + [in_any] + [in_vmem()] * len(previous),
-            out_specs=[in_any, in_vmem(), in_any, in_any],
+            specs=smem2 + [in_vmem()] * (len(args) - 2),
+            out_specs=[in_any, in_vmem(), in_any, in_vmem()],
             scratch=[
                 ((2, nsel, hd), BF16),
                 ((2, nsel, hd), BF16),
@@ -499,11 +492,9 @@
                 ((2, nsel, hd), F32),
                 (own, F32),
                 (dsel, BF16),
-                (send, BF16),
-                (stack_shape, BF16),
-                ((ranks, 2 * BLK, hd), BF16),
             ],
-            sems=4 * chunks + 4,
+            sems=2 * chunks + 2,
+            limit=60,
             cost=8 * nsel * wide * 2 * hd,
         )
 
@@ -548,6 +539,7 @@
         grid=(1,),
         scratch=[((nsel, hd), BF16)],
         aliases={6: 0},
+        limit=60,
         cost=2 * nsel * wide * 2 * hd,
     )
 
@@ -556,7 +548,7 @@
         out_shape=jax.ShapeDtypeStruct((tokens, 2 * hd), F32),
         in_specs=[in_smem(), in_smem()] + [in_vmem()] * 3,
         out_specs=in_vmem(),
-        compiler_params=params(),
+        compiler_params=params(ranks),
         name="collect",
     )(me, table, own0, own1, mixed)
     d_keys, d_values, d_ck, d_cv = pl.pallas_call(
@@ -567,7 +559,7 @@
         in_specs=[in_smem(), in_smem()] + [in_vmem()] * 3,
         out_specs=[in_vmem()] * 4,
         scratch_shapes=[pltpu.VMEM((tokens, 2 * hd), F32)],
-        compiler_params=params(),
+        compiler_params=params(ranks),
         name="finish",
     )(me, table, part, dc, home)
 

time: 84.1 us -> 81.3 us (0.967)
  local copies, waits for them, and re-layouts: 2.43 us -> 14.4 us
  Pallas kernels: 37.9 us -> 27 us
  waiting for transfers between devices: 22.1 us -> 18.4 us
    unnamed x8 -> x50, local copies, waits for them, and re-layouts: 2.41 us -> 14.4 us
    pallas_call x6, Pallas kernels: 31.9 us -> 22.7 us  [call(): pl.pallas_call(kernel, grid=grid, out_shape=[jax.ShapeDtypeStruct(shape,...]
    all_to_all x3, waiting for transfers between devices: 22.1 us -> 18.4 us  [exchange(): return lax.all_to_all(x, 'ctx', split_axis=0, concat_axis=0, tiled=True)]
    pallas_call x1, Pallas kernels: 2.04 us -> 0.82 us  [body(): pl.pallas_call(functools.partial(collect_kernel, ranks, qb, lists), out_s...]
  transfers between devices with their start and end apart: 5 -> 5, of which waited for: 3 -> 3; matrix products, arithmetic and copies ran while one was open for 3% -> 2% of each run, Pallas kernels for 22% -> 12%
where the time goes in v2:
time: 81.3 us; the launch traced here: 80.6 us
  Pallas kernels  27 us (33%)
  waiting for transfers between devices  18.4 us (23%)
  starting transfers between devices  18.3 us (23%)
  local copies, waits for them, and re-layouts  14.4 us (18%)
  matrix products  1.54 us (2%)
  between operations  0.9 us (1%)
    pallas_call x6, Pallas kernels, call(): pl.pallas_call(kernel, grid=grid, out_shape=[jax.ShapeDtypeStruct(shape,...  22.7 us
    all_to_all x3, waiting for transfers between devices, exchange(): return lax.all_to_all(x, 'ctx', split_axis=0, concat_axis=0, tiled=True)  18.4 us
    all_to_all x3, starting transfers between devices, exchange(): return lax.all_to_all(x, 'ctx', split_axis=0, concat_axis=0, tiled=True)  16.1 us
    unnamed x50, local copies, waits for them, and re-layouts  14.4 us
    pallas_call x1, Pallas kernels, body(): pl.pallas_call(functools.partial(pack_kernel, ranks, qb, lists), out_shap...  1.98 us
  transfers between devices with their start and end apart: 5, of which 3 were waited for; matrix products, arithmetic and copies ran while one was open for 2% of the time, Pallas kernels for 12%

profile of v2, /device:TPU:0, one launch (start us, length us, event | category | flops | bytes accessed | tf_op | source)
XLA Modules:
  0.0 80.6 jit_solution(8234973488571775488)
XLA Ops:
  0.6 0.0 copy-start.11
  0.6 0.0 copy-start.2
  0.7 2.0 %pack.1 = bf16[16,136,128]{2,1,0:T(8,128)(2,1)} custom-call(s32[1]{0:T(128)} %bitcast.rank_ref.refs_0_, s32[15,64]{1,0:T(8,128)} %bitcast.7, bf16[256,128]{1,0:T(8,128)(2,1)} %k_ref.5, bf16[256,128]{1,0:T(8,128)(2,1)} %refs_4_.3, bf16[4,128]{1,0:T(4,128)(2,1)} %ck_ref.1, bf16[4,128]{1,0:T(4,128)(2,1)} %cv_ref.1), custom_call_target="tpu_custom_call" | custom-call | tf_op jit(solution)/shard_map/pack/pallas_call | solution.py:423
  2.6 7.4 %all-to-all-start = ((bf16[16,136,128]{2,1,0:T(8,128)(2,1)}), bf16[16,136,128]{2,1,0:T(8,128)(2,1)S(1)}, u32[]{:S(2)}, u32[]{:S(2)}) async-start(bf16[16,136,128]{2,1,0:T(8,128)(2,1)} %pack.1), calls=%async_computation | async-start | bytes 1114112 | tf_op jit(solution)/shard_map/all_to_all | solution.py:421
  10.0 0.0 copy-done.11
  10.0 0.0 copy-done.2
  10.0 0.0 copy-start.3
  10.0 1.2 %copy-done.3 = bf16[256,2048]{1,0:T(8,128)(2,1)S(1)} copy-done((bf16[256,2048]{1,0:T(8,128)(2,1)S(1)}, bf16[256,2048]{1,0:T(8,128)(2,1)}, u32[]{:S(2)}) %copy-start.3) | copy-done | bytes 1048600
  11.3 1.3 %copy-done.10 = bf16[256,2560]{1,0:T(8,128)(2,1)S(1)} copy-done((bf16[256,2560]{1,0:T(8,128)(2,1)S(1)}, bf16[256,2560]{1,0:T(8,128)(2,1)}, u32[]{:S(2)}) %copy-start.10) | copy-done | bytes 1310744
  12.6 0.7 prep.1
  13.3 0.0 copy-start.8
  13.3 1.3 %copy-done.8 = bf16[2,4,512,256]{3,2,1,0:T(8,128)(2,1)} copy-done((bf16[2,4,512,256]{3,2,1,0:T(8,128)(2,1)}, bf16[2,4,512,256]{3,2,1,0:T(8,128)(2,1)S(1)}, u32[]{:S(2)}) %copy-start.8) | copy-done | bytes 2097176
  14.6 0.6 copy-done.20
  15.2 9.8 %all-to-all-done.refs_6_.fetched_ref = bf16[16,136,128]{2,1,0:T(8,128)(2,1)S(1)} async-done(((bf16[16,136,128]{2,1,0:T(8,128)(2,1)}), bf16[16,136,128]{2,1,0:T(8,128)(2,1)S(1)}, u32[]{:S(2)}, u32[]{:S(2)}) %all-to-all-start) | async-done | bytes 557088 | tf_op jit(solution)/shard_map/all_to_all | solution.py:421
  25.0 0.8 copy-done.6
  25.8 7.0 %attend0.1 = (f32[128,256]{1,0:T(8,128)}, f32[2,1024]{1,0:T(2,128)}, bf16[2,4,576,256]{3,2,1,0:T(8,128)(2,1)}, bf16[16,128,128]{2,1,0:T(8,128)(2,1)}) custom-call(s32[1]{0:T(128)} %bitcast.rank_ref.refs_0_, s32[15,64]{1,0:T(8,128)} %bitcast.8, bf16[2,4,512,256]{3,2,1,0:T(8,128)(2,1)} %copy-done.8, bf16[256,128]{1,0:T(8,128)(2,1)} %k_ref.5, ...), custom_call_target="tpu_custom_call" | custom-call | flops 1207959552 | bytes 4194304 | tf_op jit(solution)/shard_map/attend0/pallas_call | solution.py:434
  32.9 0.0 copy-start.4
  32.9 4.4 %all-to-all-start.1 = ((bf16[16,128,128]{2,1,0:T(8,128)(2,1)}), bf16[16,128,128]{2,1,0:T(8,128)(2,1)S(1)}, u32[]{:S(2)}, u32[]{:S(2)}) async-start(bf16[16,128,128]{2,1,0:T(8,128)(2,1)} %get-tuple-element.28), calls=%async_computation.1 | async-start | bytes 1048576 | tf_op jit(solution)/shard_map/all_to_all | solution.py:421
  37.3 0.0 copy-done.12
  37.3 0.0 copy-done.21
  37.3 0.0 copy-done.4
  37.3 0.0 copy-start.5
  37.3 1.7 %copy-done.5 = bf16[2,4,576,256]{3,2,1,0:T(8,128)(2,1)S(1)} copy-done((bf16[2,4,576,256]{3,2,1,0:T(8,128)(2,1)S(1)}, bf16[2,4,576,256]{3,2,1,0:T(8,128)(2,1)}, u32[]{:S(2)}) %copy-start.5) | copy-done | bytes 2359320
  39.0 1.1 %copy-done.7 = bf16[16,136,128]{2,1,0:T(8,128)(2,1)S(1)} copy-done((bf16[16,136,128]{2,1,0:T(8,128)(2,1)S(1)}, bf16[16,136,128]{2,1,0:T(8,128)(2,1)}, u32[]{:S(2)}) %copy-start.7) | copy-done | bytes 557080
  40.1 1.6 %copy-done.9 = bf16[2,4,512,256]{3,2,1,0:T(8,128)(2,1)S(1)} copy-done((bf16[2,4,512,256]{3,2,1,0:T(8,128)(2,1)S(1)}, bf16[2,4,512,256]{3,2,1,0:T(8,128)(2,1)}, u32[]{:S(2)}) %copy-start.9) | copy-done | bytes 2097176
  41.6 0.7 copy-done.23
  42.3 4.3 %middle.1 = (bf16[256,2048]{1,0:T(8,128)(2,1)}, f32[32,256]{1,0:T(8,128)S(1)}, f32[64,256]{1,0:T(8,128)S(1)}, bf16[2,64,1024]{2,1,0:T(8,128)(2,1)S(1)}, bf16[128...) custom-call(s32[1]{0:T(128)} %bitcast.rank_ref.refs_0_, bf16[2,4,512,256]{3,2,1,0:T(8,128)(2,1)S(1)} %copy-done.9, ...), custom_call_target="tpu_custom_call" | custom-call | flops 335544320 | bytes 4194304 | tf_op jit(solution)/shard_map/middle/pallas_call | solution.py:434
  46.7 0.7 copy-done.13
  47.4 0.6 copy-done.17
  48.0 0.6 copy-done.19
  48.6 1.3 %copy-done.24 = bf16[2,4,512,256]{3,2,1,0:T(8,128)(2,1)} copy-done((bf16[2,4,512,256]{3,2,1,0:T(8,128)(2,1)}, bf16[2,4,512,256]{3,2,1,0:T(8,128)(2,1)S(1)}, u32[]{:S(2)}) %copy-start.24) | copy-done | bytes 2097176
  49.9 1.8 %all-to-all-done.1.refs_6_.picks_ref.home_ref = bf16[16,128,128]{2,1,0:T(8,128)(2,1)S(1)} async-done(((bf16[16,128,128]{2,1,0:T(8,128)(2,1)}), bf16[16,128,128]{2,1,0:T(8,128)(2,1)S(1)}, u32[]{:S(2)}, u32[]{:S(2)}) %all-to-all-start.1) | async-done | bytes 524320 | tf_op jit(solution)/shard_map/all_to_all | solution.py:421
  51.8 0.8 copy-done
  52.6 7.0 %attend1.1 = (f32[128,256]{1,0:T(8,128)}, f32[2,1024]{1,0:T(2,128)}, bf16[2,4,576,256]{3,2,1,0:T(8,128)(2,1)}, bf16[16,136,128]{2,1,0:T(8,128)(2,1)}) custom-call(s32[1]{0:T(128)} %bitcast.rank_ref.refs_0_, s32[15,64]{1,0:T(8,128)} %bitcast.9, bf16[2,4,512,256]{3,2,1,0:T(8,128)(2,1)} %copy-done.24, bf16[256,128]{1,0:T(8,128)(2,1)} %k_ref.5, ...), custom_call_target="tpu_custom_call" | custom-call | flops 1207959552 | bytes 4194304 | tf_op jit(solution)/shard_map/attend1/pallas_call | solution.py:434
  59.6 0.0 copy-start.1
  59.6 0.0 copy-start.16
  59.6 4.3 %all-to-all-start.2 = ((bf16[16,136,128]{2,1,0:T(8,128)(2,1)}), bf16[16,136,128]{2,1,0:T(8,128)(2,1)S(1)}, u32[]{:S(2)}, u32[]{:S(2)}) async-start(bf16[16,136,128]{2,1,0:T(8,128)(2,1)} %get-tuple-element.39), calls=%async_computation.2 | async-start | bytes 1114112 | tf_op jit(solution)/shard_map/all_to_all | solution.py:421
  64.0 1.6 %collective-permute-start.1 = (bf16[1280,32]{0,1:T(8,128)(2,1)S(1)}, bf16[1280,32]{0,1:T(8,128)(2,1)S(1)}, u32[]{:S(2)}, u32[]{:S(2)}) collective-permute-start(bf16[1280,32]{0,1:T(8,128)(2,1)S(1)} %constant_dynamic-slice_fusion), channel_id=1, source_target_pairs={{0,1},{1,0},{2,3},{3,2},{4,5},{5,4},{6,7},{7,6},{8,9},{9,8},{10,11... | collective-permute-start | bytes 245768 | tf_op jit(solution)/shard_map/ppermute | solution.py:468
  65.6 0.1 dz.1
  65.7 0.6 collective-permute-start
  66.3 0.3 fusion.1
  66.7 0.8 %collect.1.part_ref = f32[256,256]{1,0:T(8,128)S(1)} custom-call(s32[1]{0:T(128)} %bitcast.rank_ref.refs_0_, s32[15,64]{1,0:T(8,128)S(1)} %bitcast.10, f32[128,256]{1,0:T(8,128)S(1)} %copy-done.14, f32[128,256]{1,0:T(8,128)S(1)} %copy-done.15, bf16[16,128,128]{2,1,0:T(8,128)(2,1)S(1)} %copy-done.1), custom_call_target="tpu_custom_call" | custom-call | tf_op jit(solution)/shard_map/collect/pallas_call | solution.py:546
  67.5 3.5 %tail.1 = bf16[256,2048]{1,0:T(8,128)(2,1)} custom-call(s32[1]{0:T(128)} %bitcast.rank_ref.refs_0_, bf16[256,128]{1,0:T(8,128)(2,1)} %k_ref.5, bf16[16,128,128]{2,1,0:T(8,128)(2,1)} %copy-done, bf16[2,4,576,256]{3,2,1,0:T(8,128)(2,1)} %get-tuple-element.33.dsel_ref, bf16[2,64,1024]{2,1,0:T(8,128)(2,1)} %copy-done.13, ...), custom_call_target="tpu_custom_call", output_to_operand_aliasing={{}: (6, {})} | custom-call | flops 301989888 | bytes 4194304 | tf_op jit(solution)/shard_map/tail/pallas_call | solution.py:434
  71.0 0.0 collective-permute-done.1
  71.0 0.0 collective-permute-done
  71.0 1.2 %fusion = bf16[256,1280]{1,0:T(8,128)(2,1)} fusion(f32[256,1280]{1,0:T(8,128)S(1)} %fusion.1, bf16[32,256]{1,0:T(8,128)(2,1)S(1)} %collective-permute-done, bf16[1280,32]{0,1:T(8,128)(2,1)S(1)} %collective-permute-done.1), kind=kOutput, calls=%fused_computation.1 | convolution fusion | flops 21626880 | bytes 2064384 | tf_op jit(solution)/shard_map/dot_general | solution.py:571
  72.2 6.8 %all-to-all-done.2.home_ref = bf16[16,136,128]{2,1,0:T(8,128)(2,1)S(1)} async-done(((bf16[16,136,128]{2,1,0:T(8,128)(2,1)}), bf16[16,136,128]{2,1,0:T(8,128)(2,1)S(1)}, u32[]{:S(2)}, u32[]{:S(2)}) %all-to-all-start.2) | async-done | bytes 557088 | tf_op jit(solution)/shard_map/all_to_all | solution.py:421
  79.0 1.6 %finish.1 = (bf16[256,128]{1,0:T(8,128)(2,1)}, bf16[256,128]{1,0:T(8,128)(2,1)}, bf16[4,128]{1,0:T(4,128)(2,1)}, bf16[4,128]{1,0:T(4,128)(2,1)}) custom-call(s32[1]{0:T(128)} %bitcast.rank_ref.refs_0_, s32[15,64]{1,0:T(8,128)S(1)} %bitcast.11, f32[256,256]{1,0:T(8,128)S(1)} %collect.1.part_ref, f32[64,256]{1,0:T(8,128)S(1)} %copy-done.18, ...), custom_call_target="tpu_custom_call" | custom-call | tf_op jit(solution)/shard_map/finish/pallas_call | solution.py:554
  (25 shorter events, 0.1 us)
Async XLA Ops:
  0.6 9.4 %copy-start.11 = (bf16[2560,32]{0,1:T(8,128)(2,1)S(1)}, bf16[2560,32]{0,1:T(8,128)(2,1)}, u32[]{:S(2)}) copy-start(bf16[2560,32]{0,1:T(8,128)(2,1)} %param.16) | copy-start | bytes 491524
  0.6 9.4 %copy-start.2 = (bf16[256,2048]{1,0:T(8,128)(2,1)S(1)}, bf16[256,2048]{1,0:T(8,128)(2,1)}, u32[]{:S(2)}) copy-start(bf16[256,2048]{1,0:T(8,128)(2,1)} %q_ref.3) | copy-start | bytes 3145732
  2.6 22.4 %all-to-all-start = ((bf16[16,136,128]{2,1,0:T(8,128)(2,1)}), bf16[16,136,128]{2,1,0:T(8,128)(2,1)S(1)}, u32[]{:S(2)}, u32[]{:S(2)}) async-start(bf16[16,136,128]{2,1,0:T(8,128)(2,1)} %pack.1), calls=%async_computation | async-start | bytes 1114112 | tf_op jit(solution)/shard_map/all_to_all | solution.py:421
  10.0 1.2 %copy-start.3 = (bf16[256,2048]{1,0:T(8,128)(2,1)S(1)}, bf16[256,2048]{1,0:T(8,128)(2,1)}, u32[]{:S(2)}) copy-start(bf16[256,2048]{1,0:T(8,128)(2,1)} %do_ref.3) | copy-start | bytes 3145732
  11.3 1.3 %copy-start.10 = (bf16[256,2560]{1,0:T(8,128)(2,1)S(1)}, bf16[256,2560]{1,0:T(8,128)(2,1)}, u32[]{:S(2)}) copy-start(bf16[256,2560]{1,0:T(8,128)(2,1)} %x_ref.1) | copy-start | bytes 3932164
  13.3 1.4 %copy-start.8 = (bf16[2,4,512,256]{3,2,1,0:T(8,128)(2,1)}, bf16[2,4,512,256]{3,2,1,0:T(8,128)(2,1)S(1)}, u32[]{:S(2)}) copy-start(bf16[2,4,512,256]{3,2,1,0:T(8,128)(2,1)S(1)} %get-tuple-element.26.refs_2_.stack0) | copy-start | bytes 6291460
  14.6 0.6 copy-start.20
  25.0 0.8 copy-start.6
  25.8 11.5 %copy-start.12 = (bf16[256,128]{1,0:T(8,128)(2,1)S(1)}, bf16[256,128]{1,0:T(8,128)(2,1)}, u32[]{:S(2)}) copy-start(bf16[256,128]{1,0:T(8,128)(2,1)} %k_ref.5) | copy-start | bytes 196612
  25.8 11.5 %copy-start.21 = (f32[4,2,1024]{2,1,0:T(2,128)S(1)}, f32[4,2,1024]{2,1,0:T(2,128)}, u32[]{:S(2)}) copy-start(f32[4,2,1024]{2,1,0:T(2,128)} %copy-done.20) | copy-start | bytes 98308
  32.9 4.4 %copy-start.4 = (bf16[256,2048]{1,0:T(8,128)(2,1)S(1)}, bf16[256,2048]{1,0:T(8,128)(2,1)}, u32[]{:S(2)}) copy-start(bf16[256,2048]{1,0:T(8,128)(2,1)} %do_ref.3) | copy-start | bytes 3145732
  32.9 18.9 %all-to-all-start.1 = ((bf16[16,128,128]{2,1,0:T(8,128)(2,1)}), bf16[16,128,128]{2,1,0:T(8,128)(2,1)S(1)}, u32[]{:S(2)}, u32[]{:S(2)}) async-start(bf16[16,128,128]{2,1,0:T(8,128)(2,1)} %get-tuple-element.28), calls=%async_computation.1 | async-start | bytes 1048576 | tf_op jit(solution)/shard_map/all_to_all | solution.py:421
  37.3 1.7 %copy-start.5 = (bf16[2,4,576,256]{3,2,1,0:T(8,128)(2,1)S(1)}, bf16[2,4,576,256]{3,2,1,0:T(8,128)(2,1)}, u32[]{:S(2)}) copy-start(bf16[2,4,576,256]{3,2,1,0:T(8,128)(2,1)} %get-tuple-element.29.dsel_ref) | copy-start | bytes 7077892
  39.0 1.1 %copy-start.7 = (bf16[16,136,128]{2,1,0:T(8,128)(2,1)S(1)}, bf16[16,136,128]{2,1,0:T(8,128)(2,1)}, u32[]{:S(2)}) copy-start(bf16[16,136,128]{2,1,0:T(8,128)(2,1)} %copy-done.6) | copy-start | bytes 1671172
  40.1 1.6 %copy-start.9 = (bf16[2,4,512,256]{3,2,1,0:T(8,128)(2,1)S(1)}, bf16[2,4,512,256]{3,2,1,0:T(8,128)(2,1)}, u32[]{:S(2)}) copy-start(bf16[2,4,512,256]{3,2,1,0:T(8,128)(2,1)} %copy-done.8) | copy-start | bytes 6291460
  41.6 0.7 copy-start.23
  46.7 0.7 copy-start.13
  47.4 0.6 copy-start.17
  48.0 0.6 copy-start.19
  48.6 1.3 %copy-start.24 = (bf16[2,4,512,256]{3,2,1,0:T(8,128)(2,1)}, bf16[2,4,512,256]{3,2,1,0:T(8,128)(2,1)S(1)}, u32[]{:S(2)}) copy-start(bf16[2,4,512,256]{3,2,1,0:T(8,128)(2,1)S(1)} %get-tuple-element.31.refs_2_) | copy-start | bytes 6291460
  51.8 0.8 copy-start
  59.6 6.0 %copy-start.22 = (f32[2,1024]{1,0:T(2,128)S(1)}, f32[2,1024]{1,0:T(2,128)}, u32[]{:S(2)}) copy-start(f32[2,1024]{1,0:T(2,128)} %get-tuple-element.45.dg_ref) | copy-start | bytes 24580
  59.6 7.0 %copy-start.1 = (bf16[16,128,128]{2,1,0:T(8,128)(2,1)S(1)}, bf16[16,128,128]{2,1,0:T(8,128)(2,1)}, u32[]{:S(2)}) copy-start(bf16[16,128,128]{2,1,0:T(8,128)(2,1)} %copy-done) | copy-start | bytes 1572868
  59.6 7.0 %copy-start.14 = (f32[128,256]{1,0:T(8,128)S(1)}, f32[128,256]{1,0:T(8,128)}, u32[]{:S(2)}) copy-start(f32[128,256]{1,0:T(8,128)} %get-tuple-element.37.own0_ref) | copy-start | bytes 393220
  59.6 7.0 %copy-start.15 = (f32[128,256]{1,0:T(8,128)S(1)}, f32[128,256]{1,0:T(8,128)}, u32[]{:S(2)}) copy-start(f32[128,256]{1,0:T(8,128)} %get-tuple-element.38.own1_ref) | copy-start | bytes 393220
  59.6 7.0 %copy-start.16 = (s32[64,15]{0,1:T(8,128)S(1)}, s32[64,15]{0,1:T(8,128)}, u32[]{:S(2)}) copy-start(s32[64,15]{0,1:T(8,128)} %param.14) | copy-start | bytes 11524
  59.6 19.4 %all-to-all-start.2 = ((bf16[16,136,128]{2,1,0:T(8,128)(2,1)}), bf16[16,136,128]{2,1,0:T(8,128)(2,1)S(1)}, u32[]{:S(2)}, u32[]{:S(2)}) async-start(bf16[16,136,128]{2,1,0:T(8,128)(2,1)} %get-tuple-element.39), calls=%async_computation.2 | async-start | bytes 1114112 | tf_op jit(solution)/shard_map/all_to_all | solution.py:421
  64.0 7.0 %collective-permute-start.1 = (bf16[1280,32]{0,1:T(8,128)(2,1)S(1)}, bf16[1280,32]{0,1:T(8,128)(2,1)S(1)}, u32[]{:S(2)}, u32[]{:S(2)}) collective-permute-start(bf16[1280,32]{0,1:T(8,128)(2,1)S(1)} %constant_dynamic-slice_fusion), channel_id=1, source_target_pairs={{0,1},{1,0},{2,3},{3,2},{4,5},{5,4},{6,7},{7,6},{8,9},{9,8},{10,11... | collective-permute-start | bytes 245768 | tf_op jit(solution)/shard_map/ppermute | solution.py:468
  65.7 5.3 %collective-permute-start = (bf16[32,256]{1,0:T(8,128)(2,1)S(1)}, bf16[32,256]{1,0:T(8,128)(2,1)S(1)}, u32[]{:S(2)}, u32[]{:S(2)}) collective-permute-start(bf16[32,256]{1,0:T(8,128)(2,1)S(1)} %convert_element_type.6), channel_id=1, source_target_pairs={{0,1},{1,0},{2,3},{3,2},{4,5},{5,4},{6,7},{7,6},{8,9},{9,8},{10,11... | collective-permute-start | bytes 49160 | tf_op jit(solution)/shard_map/ppermute | solution.py:567
  71.0 8.0 %copy-start.18 = (f32[64,256]{1,0:T(8,128)S(1)}, f32[64,256]{1,0:T(8,128)}, u32[]{:S(2)}) copy-start(f32[64,256]{1,0:T(8,128)} %copy-done.17) | copy-start | bytes 196612

commit v3 on v2

v3 whole, which is shorter than its diff:
```python
import functools

import jax
import jax.numpy as jnp
from jax import lax
from jax.experimental import pallas as pl
from jax.experimental.pallas import tpu as pltpu
from jax.sharding import PartitionSpec as P

BLK = 64
PICKS = 15
LOG2E = 1.4426950408889634
LANES = 256
NEG = -1e30
F32, BF16 = jnp.float32, jnp.bfloat16


def reach_lists(ranks):
    half = ranks // 2
    even, odd = [], []
    for j in range(PICKS):
        near = 1 + j * max(half - 1, 0) // 14
        far = half + 1 + j * max(half - 2, 0) // 14
        if j == 0 or near != 1 + (j - 1) * max(half - 1, 0) // 14:
            even.append((j, near))
        if j == 0 or far != half + 1 + (j - 1) * max(half - 2, 0) // 14:
            odd.append((j, far))
    return even, odd


def in_vmem():
    return pl.BlockSpec(memory_space=pltpu.VMEM)


def in_smem():
    return pl.BlockSpec(memory_space=pltpu.SMEM)


def params(ranks, limit=16):
    return pltpu.CompilerParams(vmem_limit_bytes=(limit if ranks <= 16 else 48) * 1024 * 1024)


def fill_picks(ranks, qb, lists, p, me, sel_ref, k_ref, v_ref, out_ref):
    for parity, reach in enumerate(lists):
        for j, r in reach:
            dest = jnp.where(me + r < ranks, me + r, me)
            named = sel_ref[j, dest * qb + 2 * p + parity]
            local = jnp.clip(named - me * qb, 0, qb - 1)
            rows = pl.ds(pl.multiple_of(local * BLK, BLK), BLK)
            out_ref[dest, :BLK, :] = k_ref[rows, :]
            out_ref[dest, BLK : 2 * BLK, :] = v_ref[rows, :]


def pack_kernel(ranks, qb, lists, rank_ref, sel_ref, k_ref, v_ref, ck_ref, cv_ref, out_ref):
    hd = k_ref.shape[1]
    me = rank_ref[0]
    comp = jnp.concatenate([ck_ref[...].astype(F32), cv_ref[...].astype(F32)], axis=0).astype(BF16)

    def every(n, carry):
        out_ref[n, 2 * BLK :, :] = comp
        return carry

    lax.fori_loop(0, ranks, every, 0)
    out_ref[me, : 2 * BLK, :] = jnp.zeros((2 * BLK, hd), BF16)
    fill_picks(ranks, qb, lists, 0, me, sel_ref, k_ref, v_ref, out_ref)


def gate_kernel(qb, heads, x_ref, w_ref, q_ref, do_ref, out_ref):
    del q_ref, do_ref
    nt = (((1,), (1,)), ((), ()))
    z = lax.dot_general(w_ref[...], x_ref[...], nt, preferred_element_type=F32)
    zt = jax.nn.sigmoid(z)
    for i in range(qb):
        for branch in range(2):
            for h in range(heads):
                row = branch * heads + h
                out_ref[i, branch : branch + 1, h * BLK : (h + 1) * BLK] = zt[
                    row : row + 1, i * BLK : (i + 1) * BLK
                ]


def fold(x, op):
    return op(x.reshape(x.shape[0] // 8, 8, x.shape[1]), axis=0)


def branch_grad(parts, lanes, gate, s_scr, u_scr, w_scr, d_scr):
    c2 = 128 ** -0.5 * LOG2E
    top = jnp.full((8, LANES), NEG, F32)
    for at, live, mask in parts:
        s = s_scr[at, :]
        if mask is not None:
            s = jnp.where(mask, s, NEG)
            s_scr[at, :] = s
        part = fold(s, jnp.max)
        top = jnp.maximum(top, part if live is None else jnp.where(live, part, NEG))
    top = jnp.max(top, axis=0, keepdims=True) * c2
    total = jnp.zeros((8, LANES), F32)
    mixed = jnp.zeros((8, LANES), F32)
    for at, live, mask in parts:
        e = jnp.exp2(s_scr[at, :] * c2 - (top if live is None else jnp.where(live, top, -NEG)))
        total = total + fold(e, jnp.sum)
        mixed = mixed + fold(e * u_scr[at, :], jnp.sum)
        s_scr[at, :] = e
    inv = 1.0 / jnp.sum(total, axis=0, keepdims=True)
    d_gate = jnp.sum(mixed, axis=0, keepdims=True) * inv
    weight = gate * inv
    for at, live, mask in parts:
        pw = s_scr[at, :] * weight
        w_scr[at, lanes] = pw.astype(BF16)
        d_scr[at, lanes] = (pw * (u_scr[at, :] - d_gate)).astype(BF16)
    return d_gate


def attend_kernel(ranks, qb, heads, lists, p, *refs):
    (rank_ref, sel_ref, q_ref, do_ref, k_ref, v_ref, gate_ref, comp_ref, picks_ref) = refs[:9]
    if p == 0:
        dq_ref, own_ref, dz_ref, dc_ref, send_ref, *scratch = refs[9:]
    else:
        _, dz_in, dc_in, dq_ref, own_ref, dz_ref, dc_ref, send_ref, *scratch = refs[9:]
    hd = k_ref.shape[1]
    me = rank_ref[0]
    step = pl.program_id(0)
    dg_scr, dc_scr = scratch[-2:]

    @pl.when(step == 0)
    def _():
        if p == 0:
            dc_scr[...] = jnp.zeros_like(dc_scr)
            dz_ref[...] = jnp.zeros_like(dz_ref)
            send_ref[me] = jnp.zeros(send_ref.shape[1:], BF16)
            fill_picks(ranks, qb, lists, 1, me, sel_ref, k_ref, v_ref, send_ref)
        else:
            dc_scr[...] = dc_in[...]
            dz_ref[...] = dz_in[...]

    for parity in range(2):

        @pl.when(step == parity)
        def _(parity=parity):
            attend_row(ranks, qb, heads, lists[parity], me, 2 * p + parity, parity, q_ref, do_ref, k_ref, v_ref,
                       gate_ref, comp_ref, picks_ref, dq_ref, own_ref, send_ref, *scratch)

    @pl.when(step == 1)
    def _():
        dc_ref[...] = dc_scr[...]
        if p == 1:
            for r in range(1, ranks):

                @pl.when(me >= r)
                def _(r=r):
                    at = slice(r * qb, (r + 1) * qb)
                    piece = jnp.concatenate([dc_scr[at, :hd], dc_scr[at, hd:]], axis=0)
                    send_ref[me - r, 2 * BLK :, :] = piece.astype(BF16)

        for i in range(2):
            for branch in range(2):
                for h in range(heads):
                    row = branch * heads + h
                    lane = (2 * p + i) * BLK
                    dz_ref[row : row + 1, lane : lane + BLK] = dg_scr[
                        i, branch : branch + 1, h * BLK : (h + 1) * BLK
                    ]


def attend_row(ranks, qb, heads, reach, me, row, parity, q_ref, do_ref, k_ref, v_ref, gate_ref,
               comp_ref, picks_ref, dq_ref, own_ref, send_ref, kcat, vcat, kt, qs, ds,
               s_scr, u_scr, w_scr, d_scr, dv_acc, dk_acc, dg_scr, dc_scr):
    npick = len(reach)
    hd = k_ref.shape[1]
    nblocks = ranks * qb
    nsel = (1 + npick) * BLK
    nk = nsel + nblocks
    per = LANES // BLK
    scale = hd ** -0.5

    pieces = []
    for r in range(ranks):
        pieces.append(comp_ref[jnp.maximum(me - r, 0)].astype(F32))
    kcat[nsel:nk, :] = jnp.concatenate([x[:qb] for x in pieces], axis=0).astype(BF16)
    vcat[nsel:nk, :] = jnp.concatenate([x[qb:] for x in pieces], axis=0).astype(BF16)
    kcat[:BLK, :] = k_ref[row * BLK : (row + 1) * BLK, :]
    vcat[:BLK, :] = v_ref[row * BLK : (row + 1) * BLK, :]
    for n, (_, r) in enumerate(reach):
        src = jnp.where(me >= r, me - r, me)
        kcat[(n + 1) * BLK : (n + 2) * BLK, :] = picks_ref[src, :BLK, :]
        vcat[(n + 1) * BLK : (n + 2) * BLK, :] = picks_ref[src, BLK : 2 * BLK, :]
    kt[:, :nk] = kcat[:nk, :].astype(F32).T.astype(BF16)
    for h in range(heads):
        qs[h * BLK : (h + 1) * BLK, :] = q_ref[:, h * hd : (h + 1) * hd]
        ds[h * BLK : (h + 1) * BLK, :] = do_ref[:, h * hd : (h + 1) * hd]

    key_pos = lax.broadcasted_iota(jnp.int32, (BLK, LANES), 0)
    tok_pos = lax.rem(lax.broadcasted_iota(jnp.int32, (BLK, LANES), 1), BLK)
    sel_parts = [(slice(0, BLK), None, key_pos <= tok_pos)]
    for n, (_, r) in enumerate(reach):
        sel_parts.append((slice((n + 1) * BLK, (n + 2) * BLK), me >= r, None))
    comp_parts = []
    span = min(nblocks, BLK)
    for n in range(nblocks // span):
        place = lax.broadcasted_iota(jnp.int32, (span, LANES), 0) + n * span
        away, within = place // qb, lax.rem(place, qb)
        seen = (away <= me) & ((away > 0) | (within <= row))
        comp_parts.append((slice(nsel + n * span, nsel + (n + 1) * span), None, seen))

    nt = (((1,), (1,)), ((), ()))
    chunks = heads // per

    def lanes_of(c):
        return slice(c * LANES, (c + 1) * LANES)

    def scores(c):
        lanes = lanes_of(c)
        s_scr[c % 2, :nk, :] = lax.dot_general(kcat[:nk, :], qs[lanes, :], nt, preferred_element_type=F32)
        u_scr[c % 2, :nk, :] = lax.dot_general(vcat[:nk, :], ds[lanes, :], nt, preferred_element_type=F32)

    def soften(c):
        lanes = lanes_of(c)
        work = (s_scr.at[c % 2], u_scr.at[c % 2], w_scr, d_scr)
        for branch, parts in ((1, sel_parts), (0, comp_parts)):
            gate = gate_ref[0, branch : branch + 1, lanes]
            dg = branch_grad(parts, lanes, gate, *work)
            dg_scr[parity, branch : branch + 1, lanes] = dg * gate * (1.0 - gate)

    def gradients(c):
        lanes = lanes_of(c)
        dv = jnp.dot(w_scr[:nk, lanes], ds[lanes, :], preferred_element_type=F32)
        dk = jnp.dot(d_scr[:nk, lanes], qs[lanes, :], preferred_element_type=F32)
        if c == 0:
            dv_acc[:nk, :] = dv
            dk_acc[:nk, :] = dk
        else:
            dv_acc[:nk, :] += dv
            dk_acc[:nk, :] += dk
        dqt = jnp.dot(kt[:, :nk], d_scr[:nk, lanes], preferred_element_type=F32)
        dq = (dqt.T * scale).astype(BF16)
        for h in range(per):
            head = c * per + h
            dq_ref[:, head * hd : (head + 1) * hd] = dq[h * BLK : (h + 1) * BLK, :]

    scores(0)
    for c in range(chunks):
        if c + 1 < chunks:
            scores(c + 1)
        if c > 0:
            gradients(c - 1)
        soften(c)
    gradients(chunks - 1)

    own_ref[parity * BLK : (parity + 1) * BLK, :hd] = dk_acc[:BLK, :] * scale
    own_ref[parity * BLK : (parity + 1) * BLK, hd:] = dv_acc[:BLK, :]
    dc_scr[:, :hd] += dk_acc[nsel:nk, :] * scale
    dc_scr[:, hd:] += dv_acc[nsel:nk, :]
    for n, (_, r) in enumerate(reach):
        at = slice((n + 1) * BLK, (n + 2) * BLK)
        dest = jnp.where(me >= r, me - r, me)
        send_ref[dest, :BLK, :] = (dk_acc[at, :] * scale).astype(BF16)
        send_ref[dest, BLK : 2 * BLK, :] = dv_acc[at, :].astype(BF16)


def add_homes(ranks, qb, lists, p, me, sel_ref, home_ref, acc):
    hd = home_ref.shape[2]
    for parity, reach in enumerate(lists):
        for j, r in reach:
            src = jnp.minimum(me + r, ranks - 1)
            named = sel_ref[j, src * qb + 2 * p + parity]
            local = jnp.clip(named - me * qb, 0, qb - 1)
            rows = pl.ds(pl.multiple_of(local * BLK, BLK), BLK)
            live = me + r < ranks
            acc[rows, :hd] += jnp.where(live, home_ref[src, :BLK, :].astype(F32), 0.0)
            acc[rows, hd:] += jnp.where(live, home_ref[src, BLK : 2 * BLK, :].astype(F32), 0.0)


def collect_kernel(ranks, qb, lists, rank_ref, sel_ref, own0_ref, own1_ref, home_ref, acc_ref):
    acc_ref[: 2 * BLK, :] = own0_ref[...]
    acc_ref[2 * BLK :, :] = own1_ref[...]
    add_homes(ranks, qb, lists, 0, rank_ref[0], sel_ref, home_ref, acc_ref)


def finish_kernel(ranks, qb, lists, rank_ref, sel_ref, part_ref, dc_ref, home_ref,
                  dk_ref, dv_ref, dck_ref, dcv_ref, acc):
    hd = dk_ref.shape[1]
    me = rank_ref[0]
    acc[...] = part_ref[...]
    add_homes(ranks, qb, lists, 1, me, sel_ref, home_ref, acc)
    dk_ref[...] = acc[:, :hd].astype(BF16)
    dv_ref[...] = acc[:, hd:].astype(BF16)

    def add(n, total):
        return total + home_ref[n, 2 * BLK :, :].astype(F32)

    total = lax.fori_loop(me + 1, ranks, add, jnp.zeros((2 * qb, hd), F32))
    dck_ref[...] = (total[:qb] + dc_ref[:qb, :hd]).astype(BF16)
    dcv_ref[...] = (total[qb:] + dc_ref[:qb, hd:]).astype(BF16)


def body(queries, keys, values, comp_keys, comp_values, selected, inputs, w_gate, d_out):
    tokens, width = queries.shape
    hd = keys.shape[1]
    heads = width // hd
    qb = tokens // BLK
    pair = qb // 2
    ranks = lax.axis_size("ctx")
    rank = lax.axis_index("ctx").astype(jnp.int32)
    me = rank.reshape(1)
    head = lax.axis_index("head")
    nblocks = ranks * qb
    lists = reach_lists(ranks)
    table = selected.T

    slot = 2 * BLK + 2 * qb

    def exchange(x):
        return lax.all_to_all(x, "ctx", split_axis=0, concat_axis=0, tiled=True)

    send = pl.pallas_call(
        functools.partial(pack_kernel, ranks, qb, lists),
        out_shape=jax.ShapeDtypeStruct((ranks, slot, hd), BF16),
        in_specs=[in_smem(), in_smem()] + [in_vmem()] * 4,
        out_specs=in_vmem(),
        compiler_params=params(ranks, 56),
        name="pack",
    )(me, table, keys, values, comp_keys, comp_values)
    fetched = exchange(send)

    gate = pl.pallas_call(
        functools.partial(gate_kernel, qb, heads),
        out_shape=jax.ShapeDtypeStruct((qb, 2, heads * BLK), F32),
        in_specs=[in_vmem()] * 4,
        out_specs=in_vmem(),
        compiler_params=params(ranks),
        cost_estimate=pl.CostEstimate(
            flops=2 * inputs.size * w_gate.shape[1], bytes_accessed=2 * inputs.size, transcendentals=0
        ),
        name="gate",
    )(inputs, w_gate.T, queries, d_out)
    half = w_gate.shape[0] // 2
    swap = [(0, 1), (1, 0)]
    w_send = lax.dynamic_slice_in_dim(w_gate, (1 - head) * half, half, 0)
    w_mine = lax.dynamic_slice_in_dim(w_gate, head * half, half, 0)
    w_other = lax.ppermute(w_send, "head", swap)

    nk = (1 + max(len(x) for x in lists)) * BLK + nblocks

    def attend(p, picks, previous):
        row = lambda i: (2 * p + i, 0)
        out_slot = slot if p else 2 * BLK
        args = [me, table, queries, d_out, keys, values, gate, fetched, picks] + previous
        in_specs = [
            in_smem(),
            in_smem(),
            pl.BlockSpec((BLK, width), row),
            pl.BlockSpec((BLK, width), row),
            in_vmem(),
            in_vmem(),
            pl.BlockSpec((1, 2, heads * BLK), lambda i: (2 * p + i, 0, 0)),
            pl.BlockSpec((ranks, 2 * qb, hd), lambda i: (0, 2 * BLK // (2 * qb), 0)),
            pl.BlockSpec((ranks, 2 * BLK, hd), lambda i: (0, 0, 0)),
        ]
        if previous:
            in_specs += [pl.BlockSpec(memory_space=pl.ANY), in_vmem(), in_vmem()]
        return pl.pallas_call(
            functools.partial(attend_kernel, ranks, qb, heads, lists, p),
            grid=(2,),
            out_shape=[
                jax.ShapeDtypeStruct(queries.shape, BF16),
                jax.ShapeDtypeStruct((2 * BLK, 2 * hd), F32),
                jax.ShapeDtypeStruct((2 * heads, tokens), F32),
                jax.ShapeDtypeStruct((nblocks, 2 * hd), F32),
                jax.ShapeDtypeStruct((ranks, out_slot, hd), BF16),
            ],
            in_specs=in_specs,
            out_specs=[pl.BlockSpec((BLK, width), row)] + [in_vmem()] * 4,
            scratch_shapes=[
                pltpu.VMEM((nk, hd), BF16),
                pltpu.VMEM((nk, hd), BF16),
                pltpu.VMEM((hd, nk), BF16),
                pltpu.VMEM((heads * BLK, hd), BF16),
                pltpu.VMEM((heads * BLK, hd), BF16),
                pltpu.VMEM((2, nk, LANES), F32),
                pltpu.VMEM((2, nk, LANES), F32),
                pltpu.VMEM((nk, heads * BLK), BF16),
                pltpu.VMEM((nk, heads * BLK), BF16),
                pltpu.VMEM((nk, hd), F32),
                pltpu.VMEM((nk, hd), F32),
                pltpu.VMEM((2, 2, heads * BLK), F32),
                pltpu.VMEM((nblocks, 2 * hd), F32),
            ],
            input_output_aliases={9: 0} if previous else {},
            compiler_params=params(ranks),
            cost_estimate=pl.CostEstimate(
                flops=10 * nk * heads * 2 * BLK * hd, bytes_accessed=4 << 20, transcendentals=0
            ),
            name=f"attend{p}",
        )(*args)

    dq, own0, dz, dc, send = attend(0, fetched, [])
    mixed = exchange(send)
    d_queries, own1, dz, dc, send = attend(1, mixed, [dq, dz, dc])
    home = exchange(send)

    part = pl.pallas_call(
        functools.partial(collect_kernel, ranks, qb, lists),
        out_shape=jax.ShapeDtypeStruct((tokens, 2 * hd), F32),
        in_specs=[in_smem(), in_smem()] + [in_vmem()] * 3,
        out_specs=in_vmem(),
        compiler_params=params(ranks),
        name="collect",
    )(me, table, own0, own1, mixed)
    d_keys, d_values, d_ck, d_cv = pl.pallas_call(
        functools.partial(finish_kernel, ranks, qb, lists),
        out_shape=[
            jax.ShapeDtypeStruct(x.shape, BF16) for x in (keys, values, comp_keys, comp_values)
        ],
        in_specs=[in_smem(), in_smem()] + [in_vmem()] * 3,
        out_specs=[in_vmem()] * 4,
        scratch_shapes=[pltpu.VMEM((tokens, 2 * hd), F32)],
        compiler_params=params(ranks),
        name="finish",
    )(me, table, part, dc, home)

    dz = dz.astype(BF16)
    dz_other = lax.ppermute(dz, "head", swap)
    tn = (((0,), (1,)), ((), ()))
    d_inputs = (
        lax.dot_general(dz, w_mine, tn, preferred_element_type=F32)
        + lax.dot_general(dz_other, w_other, tn, preferred_element_type=F32)
    ).astype(BF16)

    return d_queries, d_keys, d_values, d_ck, d_cv, d_inputs


def solution(mesh):
    split = P("ctx", "head")
    in_specs = (split,) * 5 + (P(), P("ctx", None), P(None, "head"), split)
    return jax.shard_map(
        body, mesh=mesh, in_specs=in_specs, out_specs=(split,) * 6, check_vma=False
    )
```

time: 81.3 us -> 82.7 us (1.017)
  blocking collectives: 0 us -> 18.5 us
  Pallas kernels: 27 us -> 18 us
  local copies, waits for them, and re-layouts: 14.4 us -> 8.55 us
  starting transfers between devices: 18.3 us -> 13.7 us
  waiting for transfers between devices: 18.4 us -> 20.9 us
    all_to_all x0 -> x1, blocking collectives: none -> 18.5 us  [exchange(): return lax.all_to_all(x, 'ctx', split_axis=0, concat_axis=0, tiled=True)]
    pallas_call x6 -> x3, Pallas kernels: 22.7 us -> 13.6 us  [the longest x2 13 us: attend(): pl.pallas_call(functools.partial(attend_kernel, ranks, qb, heads, lists,...]
    unnamed x50 -> x34, local copies, waits for them, and re-layouts: 14.4 us -> 8.53 us
    all_to_all x3 -> x2, starting transfers between devices: 16.1 us -> 11.6 us  [exchange(): return lax.all_to_all(x, 'ctx', split_axis=0, concat_axis=0, tiled=True)]
    ppermute x1, waiting for transfers between devices: 0.01 us -> 1.72 us  [body(): w_other = lax.ppermute(w_send, 'head', swap)]
    all_to_all x3 -> x2, waiting for transfers between devices: 18.4 us -> 18.9 us  [exchange(): return lax.all_to_all(x, 'ctx', split_axis=0, concat_axis=0, tiled=True)]
  transfers between devices with their start and end apart: 5 -> 4, of which waited for: 3 -> 4; matrix products, arithmetic and copies ran while one was open for 2% -> 2% of each run, Pallas kernels for 12% -> 2%
where the time goes in v3:
time: 82.7 us; the launch traced here: 82 us
  waiting for transfers between devices  20.9 us (25%)
  blocking collectives  18.5 us (22%)
  Pallas kernels  18 us (22%)
  starting transfers between devices  13.7 us (17%)
  local copies, waits for them, and re-layouts  8.55 us (10%)
  matrix products  1.54 us (2%)
    all_to_all x2, waiting for transfers between devices, exchange(): return lax.all_to_all(x, 'ctx', split_axis=0, concat_axis=0, tiled=True)  18.9 us
    all_to_all x1, blocking collectives, exchange(): return lax.all_to_all(x, 'ctx', split_axis=0, concat_axis=0, tiled=True)  18.5 us
    pallas_call x2, Pallas kernels, attend(): pl.pallas_call(functools.partial(attend_kernel, ranks, qb, heads, lists,...  13 us
    all_to_all x2, starting transfers between devices, exchange(): return lax.all_to_all(x, 'ctx', split_axis=0, concat_axis=0, tiled=True)  11.6 us
    unnamed x34, local copies, waits for them, and re-layouts  8.53 us
    pallas_call x1, Pallas kernels, body(): pl.pallas_call(functools.partial(pack_kernel, ranks, qb, lists), out_shap...  1.99 us
    ppermute x1, waiting for transfers between devices, body(): w_other = lax.ppermute(w_send, 'head', swap)  1.72 us
  transfers between devices with their start and end apart: 4, of which 4 were waited for; matrix products, arithmetic and copies ran while one was open for 2% of the time, Pallas kernels for 2%

profile of v3, /device:TPU:0, one launch (start us, length us, event | category | flops | bytes accessed | tf_op | source)
XLA Modules:
  0.0 82.0 jit_solution(2941137363210974168)
XLA Ops:
  0.6 0.0 copy-start
  0.6 2.0 %pack.1 = bf16[16,136,128]{2,1,0:T(8,128)(2,1)} custom-call(s32[1]{0:T(128)} %bitcast.rank_ref.refs_0_, s32[15,64]{1,0:T(8,128)} %bitcast.7, bf16[256,128]{1,0:T(8,128)(2,1)} %refs_4_.3, bf16[256,128]{1,0:T(8,128)(2,1)} %refs_5_.3, bf16[4,128]{1,0:T(4,128)(2,1)} %ck_ref.1, bf16[4,128]{1,0:T(4,128)(2,1)} %cv_ref.1), custom_call_target="tpu_custom_call" | custom-call | tf_op jit(solution)/shard_map/pack/pallas_call | solution.py:315
  2.6 7.4 %all-to-all-start = ((bf16[16,136,128]{2,1,0:T(8,128)(2,1)}), bf16[16,136,128]{2,1,0:T(8,128)(2,1)}, u32[]{:S(2)}, u32[]{:S(2)}) async-start(bf16[16,136,128]{2,1,0:T(8,128)(2,1)} %pack.1), calls=%async_computation | async-start | bytes 1114112 | tf_op jit(solution)/shard_map/all_to_all | solution.py:313
  10.0 0.0 copy-done
  10.1 0.0 copy-start.1
  10.1 1.2 %copy-done.1 = bf16[256,2048]{1,0:T(8,128)(2,1)S(1)} copy-done((bf16[256,2048]{1,0:T(8,128)(2,1)S(1)}, bf16[256,2048]{1,0:T(8,128)(2,1)}, u32[]{:S(2)}) %copy-start.1) | copy-done | bytes 1048600
  11.3 0.0 copy-start.3
  11.3 1.2 %copy-done.3 = bf16[256,2048]{1,0:T(8,128)(2,1)S(1)} copy-done((bf16[256,2048]{1,0:T(8,128)(2,1)S(1)}, bf16[256,2048]{1,0:T(8,128)(2,1)}, u32[]{:S(2)}) %copy-start.3) | copy-done | bytes 1048600
  12.5 0.9 %copy-done.5 = bf16[2560,32]{0,1:T(8,128)(2,1)S(1)} copy-done((bf16[2560,32]{0,1:T(8,128)(2,1)S(1)}, bf16[2560,32]{0,1:T(8,128)(2,1)}, u32[]{:S(2)}) %copy-start.5) | copy-done | bytes 163864
  13.4 0.0 copy-start.2
  13.4 0.0 copy-start.4
  13.4 0.0 copy-start.10
  13.4 0.6 gate.1.refs_6_
  14.1 0.0 copy-start.15
  14.1 0.6 copy-done.15
  14.7 10.5 %all-to-all-done.refs_7_.refs_8_ = bf16[16,136,128]{2,1,0:T(8,128)(2,1)} async-done(((bf16[16,136,128]{2,1,0:T(8,128)(2,1)}), bf16[16,136,128]{2,1,0:T(8,128)(2,1)}, u32[]{:S(2)}, u32[]{:S(2)}) %all-to-all-start) | async-done | bytes 557088 | tf_op jit(solution)/shard_map/all_to_all | solution.py:313
  25.1 0.0 copy-done.2
  25.1 0.0 copy-done.4
  25.1 0.0 copy-done.10
  25.1 0.0 copy-start.11
  25.2 0.8 %copy-done.11 = bf16[256,128]{1,0:T(8,128)(2,1)S(1)} copy-done((bf16[256,128]{1,0:T(8,128)(2,1)S(1)}, bf16[256,128]{1,0:T(8,128)(2,1)}, u32[]{:S(2)}) %copy-start.11) | copy-done | bytes 65560
  26.0 0.0 copy-start.12
  26.0 0.8 %copy-done.12 = bf16[256,128]{1,0:T(8,128)(2,1)S(1)} copy-done((bf16[256,128]{1,0:T(8,128)(2,1)S(1)}, bf16[256,128]{1,0:T(8,128)(2,1)}, u32[]{:S(2)}) %copy-start.12) | copy-done | bytes 65560
  26.8 0.0 copy-start.16
  26.8 0.8 copy-done.16
  27.6 6.6 %attend0.1 = (bf16[256,2048]{1,0:T(8,128)(2,1)}, f32[128,256]{1,0:T(8,128)S(1)}, f32[32,256]{1,0:T(8,128)S(1)}, f32[64,256]{1,0:T(8,128)S(1)}, bf16[16,128,128]{2,1,0:T(8,128)(2,1)S(1)}) custom-call(s32[1]{0:T(128)} %bitcast.rank_ref.refs_0_, s32[15,64]{1,0:T(8,128)S(1)} %bitcast.8, bf16[256,2048]{1,0:T(8,128)(2,1)S(1)} %copy-done.2, ...), custom_call_target="tpu_custom_call" | custom-call | flops 1677721600 | bytes 4194304 | tf_op jit(solution)/shard_map/attend0/pallas_call | solution.py:361
  34.2 18.5 %all_to_all.15.refs_8_.home_ref = bf16[16,128,128]{2,1,0:T(8,128)(2,1)S(1)} all-to-all(bf16[16,128,128]{2,1,0:T(8,128)(2,1)S(1)} %get-tuple-element.20), channel_id=1, replica_groups=mesh['ctx'=16,'head'=2] {'ctx'}, dimensions={0} | all-to-all | bytes 1048576 | tf_op jit(solution)/shard_map/all_to_all | solution.py:313
  52.7 0.0 copy-start.6
  52.7 6.4 %attend1.1 = (bf16[256,2048]{1,0:T(8,128)(2,1)}, f32[128,256]{1,0:T(8,128)S(1)}, f32[32,256]{1,0:T(8,128)S(1)}, f32[64,256]{1,0:T(8,128)S(1)}, bf16[16,136,128]{2,1,0:T(8,128)(2,1)S(1)}) custom-call(s32[1]{0:T(128)} %bitcast.rank_ref.refs_0_, s32[15,64]{1,0:T(8,128)S(1)} %bitcast.9, ...), custom_call_target="tpu_custom_call", output_to_operand_aliasing={{0}: (9, {})} | custom-call | flops 1677721600 | bytes 4194304 | tf_op jit(solution)/shard_map/attend1/pallas_call | solution.py:361
  59.1 0.0 copy-start.7
  59.1 0.8 copy-done.7
  59.9 0.0 copy-start.8
  59.9 0.7 copy-done.8
  60.6 0.6 copy-done.13
  61.2 4.2 %all-to-all-start.2 = ((bf16[16,136,128]{2,1,0:T(8,128)(2,1)}), bf16[16,136,128]{2,1,0:T(8,128)(2,1)S(1)}, u32[]{:S(2)}, u32[]{:S(2)}) async-start(bf16[16,136,128]{2,1,0:T(8,128)(2,1)} %copy-done.7), calls=%async_computation.2 | async-start | bytes 1114112 | tf_op jit(solution)/shard_map/all_to_all | solution.py:313
  65.4 0.0 copy-done.6
  65.5 1.6 %collective-permute-start.1 = (bf16[1280,32]{0,1:T(8,128)(2,1)S(1)}, bf16[1280,32]{0,1:T(8,128)(2,1)S(1)}, u32[]{:S(2)}, u32[]{:S(2)}) collective-permute-start(bf16[1280,32]{0,1:T(8,128)(2,1)S(1)} %constant_dynamic-slice_fusion), channel_id=1, source_target_pairs={{0,1},{1,0},{2,3},{3,2},{4,5},{5,4},{6,7},{7,6},{8,9},{9,8},{10,11... | collective-permute-start | bytes 245768 | tf_op jit(solution)/shard_map/ppermute | solution.py:340
  67.1 0.5 collective-permute-start
  67.6 0.3 fusion.1
  67.9 0.0 copy-done.9
  67.9 0.0 copy-start.14
  68.0 0.8 collect.1.part_ref
  68.8 1.7 %collective-permute-done.1 = bf16[1280,32]{0,1:T(8,128)(2,1)S(1)} collective-permute-done((bf16[1280,32]{0,1:T(8,128)(2,1)S(1)}, bf16[1280,32]{0,1:T(8,128)(2,1)S(1)}, u32[]{:S(2)}, u32[]{:S(2)}) %collective-permute-start.1) | collective-permute-done | bytes 81952 | tf_op jit(solution)/shard_map/ppermute | solution.py:340
  70.5 0.3 collective-permute-done
  70.8 1.2 %fusion = bf16[256,1280]{1,0:T(8,128)(2,1)} fusion(f32[256,1280]{1,0:T(8,128)S(1)} %fusion.1, bf16[32,256]{1,0:T(8,128)(2,1)S(1)} %collective-permute-done, bf16[1280,32]{0,1:T(8,128)(2,1)S(1)} %collective-permute-done.1), kind=kOutput, calls=%fused_computation.1 | convolution fusion | flops 21626880 | bytes 2064384 | tf_op jit(solution)/shard_map/dot_general | solution.py:426
  72.0 8.5 %all-to-all-done.2.home_ref = bf16[16,136,128]{2,1,0:T(8,128)(2,1)S(1)} async-done(((bf16[16,136,128]{2,1,0:T(8,128)(2,1)}), bf16[16,136,128]{2,1,0:T(8,128)(2,1)S(1)}, u32[]{:S(2)}, u32[]{:S(2)}) %all-to-all-start.2) | async-done | bytes 557088 | tf_op jit(solution)/shard_map/all_to_all | solution.py:313
  80.5 0.0 copy-done.14
  80.5 1.6 %finish.1 = (bf16[256,128]{1,0:T(8,128)(2,1)}, bf16[256,128]{1,0:T(8,128)(2,1)}, bf16[4,128]{1,0:T(4,128)(2,1)}, bf16[4,128]{1,0:T(4,128)(2,1)}) custom-call(s32[1]{0:T(128)} %bitcast.rank_ref.refs_0_, s32[15,64]{1,0:T(8,128)S(1)} %bitcast.11, f32[256,256]{1,0:T(8,128)S(1)} %collect.1.part_ref, f32[64,256]{1,0:T(8,128)S(1)} %copy-done.14, ...), custom_call_target="tpu_custom_call" | custom-call | tf_op jit(solution)/shard_map/finish/pallas_call | solution.py:409
  (5 shorter events, 0.0 us)
Async XLA Ops:
  0.6 9.4 %copy-start = (bf16[256,2560]{1,0:T(8,128)(2,1)S(1)}, bf16[256,2560]{1,0:T(8,128)(2,1)}, u32[]{:S(2)}) copy-start(bf16[256,2560]{1,0:T(8,128)(2,1)} %x_ref.1) | copy-start | bytes 3932164
  2.6 22.5 %all-to-all-start = ((bf16[16,136,128]{2,1,0:T(8,128)(2,1)}), bf16[16,136,128]{2,1,0:T(8,128)(2,1)}, u32[]{:S(2)}, u32[]{:S(2)}) async-start(bf16[16,136,128]{2,1,0:T(8,128)(2,1)} %pack.1), calls=%async_computation | async-start | bytes 1114112 | tf_op jit(solution)/shard_map/all_to_all | solution.py:313
  10.1 1.2 %copy-start.1 = (bf16[256,2048]{1,0:T(8,128)(2,1)S(1)}, bf16[256,2048]{1,0:T(8,128)(2,1)}, u32[]{:S(2)}) copy-start(bf16[256,2048]{1,0:T(8,128)(2,1)} %refs_2_.3) | copy-start | bytes 3145732
  11.3 1.2 %copy-start.3 = (bf16[256,2048]{1,0:T(8,128)(2,1)S(1)}, bf16[256,2048]{1,0:T(8,128)(2,1)}, u32[]{:S(2)}) copy-start(bf16[256,2048]{1,0:T(8,128)(2,1)} %refs_3_.3) | copy-start | bytes 3145732
  12.5 0.9 %copy-start.5 = (bf16[2560,32]{0,1:T(8,128)(2,1)S(1)}, bf16[2560,32]{0,1:T(8,128)(2,1)}, u32[]{:S(2)}) copy-start(bf16[2560,32]{0,1:T(8,128)(2,1)} %param.16) | copy-start | bytes 491524
  13.4 11.7 %copy-start.2 = (bf16[256,2048]{1,0:T(8,128)(2,1)S(1)}, bf16[256,2048]{1,0:T(8,128)(2,1)}, u32[]{:S(2)}) copy-start(bf16[256,2048]{1,0:T(8,128)(2,1)} %refs_2_.3) | copy-start | bytes 3145732
  13.4 11.7 %copy-start.4 = (bf16[256,2048]{1,0:T(8,128)(2,1)S(1)}, bf16[256,2048]{1,0:T(8,128)(2,1)}, u32[]{:S(2)}) copy-start(bf16[256,2048]{1,0:T(8,128)(2,1)} %refs_3_.3) | copy-start | bytes 3145732
  13.4 11.7 %copy-start.10 = (s32[64,15]{0,1:T(8,128)S(1)}, s32[64,15]{0,1:T(8,128)}, u32[]{:S(2)}) copy-start(s32[64,15]{0,1:T(8,128)} %param.14) | copy-start | bytes 11524
  14.1 0.6 copy-start.15
  25.1 0.8 %copy-start.11 = (bf16[256,128]{1,0:T(8,128)(2,1)S(1)}, bf16[256,128]{1,0:T(8,128)(2,1)}, u32[]{:S(2)}) copy-start(bf16[256,128]{1,0:T(8,128)(2,1)} %refs_4_.3) | copy-start | bytes 196612
  26.0 0.8 %copy-start.12 = (bf16[256,128]{1,0:T(8,128)(2,1)S(1)}, bf16[256,128]{1,0:T(8,128)(2,1)}, u32[]{:S(2)}) copy-start(bf16[256,128]{1,0:T(8,128)(2,1)} %refs_5_.3) | copy-start | bytes 196612
  26.8 0.8 copy-start.16
  52.7 12.8 %copy-start.6 = (bf16[2560,32]{0,1:T(8,128)(2,1)S(1)}, bf16[2560,32]{0,1:T(8,128)(2,1)}, u32[]{:S(2)}) copy-start(bf16[2560,32]{0,1:T(8,128)(2,1)} %param.16) | copy-start | bytes 491524
  59.1 0.8 %copy-start.7 = (bf16[16,136,128]{2,1,0:T(8,128)(2,1)}, bf16[16,136,128]{2,1,0:T(8,128)(2,1)S(1)}, u32[]{:S(2)}) copy-start(bf16[16,136,128]{2,1,0:T(8,128)(2,1)S(1)} %get-tuple-element.28) | copy-start | bytes 1671172
  59.9 0.7 copy-start.8
  60.6 0.6 copy-start.13
  61.2 6.7 %copy-start.9 = (f32[128,256]{1,0:T(8,128)S(1)}, f32[128,256]{1,0:T(8,128)}, u32[]{:S(2)}) copy-start(f32[128,256]{1,0:T(8,128)} %copy-done.8) | copy-start | bytes 393220
  61.2 19.3 %all-to-all-start.2 = ((bf16[16,136,128]{2,1,0:T(8,128)(2,1)}), bf16[16,136,128]{2,1,0:T(8,128)(2,1)S(1)}, u32[]{:S(2)}, u32[]{:S(2)}) async-start(bf16[16,136,128]{2,1,0:T(8,128)(2,1)} %copy-done.7), calls=%async_computation.2 | async-start | bytes 1114112 | tf_op jit(solution)/shard_map/all_to_all | solution.py:313
  65.5 5.0 %collective-permute-start.1 = (bf16[1280,32]{0,1:T(8,128)(2,1)S(1)}, bf16[1280,32]{0,1:T(8,128)(2,1)S(1)}, u32[]{:S(2)}, u32[]{:S(2)}) collective-permute-start(bf16[1280,32]{0,1:T(8,128)(2,1)S(1)} %constant_dynamic-slice_fusion), channel_id=1, source_target_pairs={{0,1},{1,0},{2,3},{3,2},{4,5},{5,4},{6,7},{7,6},{8,9},{9,8},{10,11... | collective-permute-start | bytes 245768 | tf_op jit(solution)/shard_map/ppermute | solution.py:340
  67.1 3.7 %collective-permute-start = (bf16[32,256]{1,0:T(8,128)(2,1)S(1)}, bf16[32,256]{1,0:T(8,128)(2,1)S(1)}, u32[]{:S(2)}, u32[]{:S(2)}) collective-permute-start(bf16[32,256]{1,0:T(8,128)(2,1)S(1)} %convert_element_type.6), channel_id=1, source_target_pairs={{0,1},{1,0},{2,3},{3,2},{4,5},{5,4},{6,7},{7,6},{8,9},{9,8},{10,11... | collective-permute-start | bytes 49160 | tf_op jit(solution)/shard_map/ppermute | solution.py:422
  67.9 12.5 %copy-start.14 = (f32[64,256]{1,0:T(8,128)S(1)}, f32[64,256]{1,0:T(8,128)}, u32[]{:S(2)}) copy-start(f32[64,256]{1,0:T(8,128)} %copy-done.13) | copy-start | bytes 196612

commit v4 on v3

--- a/solution.py
+++ b/solution.py
@@ -65,8 +65,7 @@
     fill_picks(ranks, qb, lists, 0, me, sel_ref, k_ref, v_ref, out_ref)
 
 
-def gate_kernel(qb, heads, x_ref, w_ref, q_ref, do_ref, out_ref):
-    del q_ref, do_ref
+def gate_kernel(qb, heads, x_ref, w_ref, out_ref):
     nt = (((1,), (1,)), ((), ()))
     z = lax.dot_general(w_ref[...], x_ref[...], nt, preferred_element_type=F32)
     zt = jax.nn.sigmoid(z)
@@ -116,7 +115,7 @@
     if p == 0:
         dq_ref, own_ref, dz_ref, dc_ref, send_ref, *scratch = refs[9:]
     else:
-        _, dz_in, dc_in, dq_ref, own_ref, dz_ref, dc_ref, send_ref, *scratch = refs[9:]
+        _, dz_in, dc_in, own_in, dq_ref, own_ref, dz_ref, dc_ref, send_ref, *scratch = refs[9:]
     hd = k_ref.shape[1]
     me = rank_ref[0]
     step = pl.program_id(0)
@@ -132,6 +131,9 @@
         else:
             dc_scr[...] = dc_in[...]
             dz_ref[...] = dz_in[...]
+            own_ref[: 2 * BLK, :] = own_in[...]
+            own_ref[2 * BLK :, :] = jnp.zeros((own_ref.shape[0] - 2 * BLK, own_ref.shape[1]), F32)
+            add_homes(ranks, qb, lists, 0, me, sel_ref, picks_ref, own_ref)
 
     for parity in range(2):
 
@@ -246,8 +248,13 @@
         soften(c)
     gradients(chunks - 1)
 
-    own_ref[parity * BLK : (parity + 1) * BLK, :hd] = dk_acc[:BLK, :] * scale
-    own_ref[parity * BLK : (parity + 1) * BLK, hd:] = dv_acc[:BLK, :]
+    own = slice(row * BLK, (row + 1) * BLK)
+    if row < 2:
+        own_ref[own, :hd] = dk_acc[:BLK, :] * scale
+        own_ref[own, hd:] = dv_acc[:BLK, :]
+    else:
+        own_ref[own, :hd] += dk_acc[:BLK, :] * scale
+        own_ref[own, hd:] += dv_acc[:BLK, :]
     dc_scr[:, :hd] += dk_acc[nsel:nk, :] * scale
     dc_scr[:, hd:] += dv_acc[nsel:nk, :]
     for n, (_, r) in enumerate(reach):
@@ -268,12 +275,6 @@
             live = me + r < ranks
             acc[rows, :hd] += jnp.where(live, home_ref[src, :BLK, :].astype(F32), 0.0)
             acc[rows, hd:] += jnp.where(live, home_ref[src, BLK : 2 * BLK, :].astype(F32), 0.0)
-
-
-def collect_kernel(ranks, qb, lists, rank_ref, sel_ref, own0_ref, own1_ref, home_ref, acc_ref):
-    acc_ref[: 2 * BLK, :] = own0_ref[...]
-    acc_ref[2 * BLK :, :] = own1_ref[...]
-    add_homes(ranks, qb, lists, 0, rank_ref[0], sel_ref, home_ref, acc_ref)
 
 
 def finish_kernel(ranks, qb, lists, rank_ref, sel_ref, part_ref, dc_ref, home_ref,
@@ -325,14 +326,14 @@
     gate = pl.pallas_call(
         functools.partial(gate_kernel, qb, heads),
         out_shape=jax.ShapeDtypeStruct((qb, 2, heads * BLK), F32),
-        in_specs=[in_vmem()] * 4,
+        in_specs=[in_vmem()] * 2,
         out_specs=in_vmem(),
-        compiler_params=params(ranks),
+        compiler_params=params(ranks, 60),
         cost_estimate=pl.CostEstimate(
             flops=2 * inputs.size * w_gate.shape[1], bytes_accessed=2 * inputs.size, transcendentals=0
         ),
         name="gate",
-    )(inputs, w_gate.T, queries, d_out)
+    )(inputs, w_gate.T)
     half = w_gate.shape[0] // 2
     swap = [(0, 1), (1, 0)]
     w_send = lax.dynamic_slice_in_dim(w_gate, (1 - head) * half, half, 0)
@@ -357,13 +358,13 @@
             pl.BlockSpec((ranks, 2 * BLK, hd), lambda i: (0, 0, 0)),
         ]
         if previous:
-            in_specs += [pl.BlockSpec(memory_space=pl.ANY), in_vmem(), in_vmem()]
+            in_specs += [pl.BlockSpec(memory_space=pl.ANY)] + [in_vmem()] * 3
         return pl.pallas_call(
             functools.partial(attend_kernel, ranks, qb, heads, lists, p),
             grid=(2,),
             out_shape=[
                 jax.ShapeDtypeStruct(queries.shape, BF16),
-                jax.ShapeDtypeStruct((2 * BLK, 2 * hd), F32),
+                jax.ShapeDtypeStruct((tokens if p else 2 * BLK, 2 * hd), F32),
                 jax.ShapeDtypeStruct((2 * heads, tokens), F32),
                 jax.ShapeDtypeStruct((nblocks, 2 * hd), F32),
                 jax.ShapeDtypeStruct((ranks, out_slot, hd), BF16),
@@ -395,17 +396,9 @@
 
     dq, own0, dz, dc, send = attend(0, fetched, [])
     mixed = exchange(send)
-    d_queries, own1, dz, dc, send = attend(1, mixed, [dq, dz, dc])
+    d_queries, part, dz, dc, send = attend(1, mixed, [dq, dz, dc, own0])
     home = exchange(send)
 
-    part = pl.pallas_call(
-        functools.partial(collect_kernel, ranks, qb, lists),
-        out_shape=jax.ShapeDtypeStruct((tokens, 2 * hd), F32),
-        in_specs=[in_smem(), in_smem()] + [in_vmem()] * 3,
-        out_specs=in_vmem(),
-        compiler_params=params(ranks),
-        name="collect",
-    )(me, table, own0, own1, mixed)
     d_keys, d_values, d_ck, d_cv = pl.pallas_call(
         functools.partial(finish_kernel, ranks, qb, lists),
         out_shape=[

time: 82.7 us -> 78.5 us (0.949)
  local copies, waits for them, and re-layouts: 8.55 us -> 0.79 us
  waiting for transfers between devices: 20.9 us -> 23.8 us
  Pallas kernels: 18 us -> 18.9 us
    unnamed x34 -> x14, local copies, waits for them, and re-layouts: 8.53 us -> 0.78 us
    all_to_all x2, waiting for transfers between devices: 18.9 us -> 20.9 us  [exchange(): return lax.all_to_all(x, 'ctx', split_axis=0, concat_axis=0, tiled=True)]
    pallas_call x1, Pallas kernels: 0.62 us -> 2.56 us  [body(): pl.pallas_call(functools.partial(gate_kernel, qb, heads), out_shape=jax.S...]
    ppermute x1, waiting for transfers between devices: 1.72 us -> 2.58 us  [body(): w_other = lax.ppermute(w_send, 'head', swap)]
  transfers between devices with their start and end apart: 4 -> 4, of which waited for: 4 -> 4; matrix products, arithmetic and copies ran while one was open for 2% -> 2% of each run, Pallas kernels for 2% -> 3%
where the time goes in v4:
time: 78.5 us; the launch traced here: 78 us
  waiting for transfers between devices  23.8 us (30%)
  Pallas kernels  18.9 us (24%)
  blocking collectives  18.5 us (24%)
  starting transfers between devices  13.7 us (17%)
  matrix products  1.53 us (2%)
  local copies, waits for them, and re-layouts  0.79 us (1%)
    all_to_all x2, waiting for transfers between devices, exchange(): return lax.all_to_all(x, 'ctx', split_axis=0, concat_axis=0, tiled=True)  20.9 us
    all_to_all x1, blocking collectives, exchange(): return lax.all_to_all(x, 'ctx', split_axis=0, concat_axis=0, tiled=True)  18.5 us
    pallas_call x2, Pallas kernels, attend(): pl.pallas_call(functools.partial(attend_kernel, ranks, qb, heads, lists,...  12.9 us
    all_to_all x2, starting transfers between devices, exchange(): return lax.all_to_all(x, 'ctx', split_axis=0, concat_axis=0, tiled=True)  11.6 us
    ppermute x1, waiting for transfers between devices, body(): w_other = lax.ppermute(w_send, 'head', swap)  2.58 us
    pallas_call x1, Pallas kernels, body(): pl.pallas_call(functools.partial(gate_kernel, qb, heads), out_shape=jax.S...  2.56 us
    pallas_call x1, Pallas kernels, body(): pl.pallas_call(functools.partial(pack_kernel, ranks, qb, lists), out_shap...  1.93 us
    ppermute x1, starting transfers between devices, body(): w_other = lax.ppermute(w_send, 'head', swap)  1.58 us
  transfers between devices with their start and end apart: 4, of which 4 were waited for; matrix products, arithmetic and copies ran while one was open for 2% of the time, Pallas kernels for 3%

profile of v4, /device:TPU:0, one launch (start us, length us, event | category | flops | bytes accessed | tf_op | source)
XLA Modules:
  0.0 78.0 jit_solution(589040415276929479)
XLA Ops:
  0.6 1.9 %pack.1 = bf16[16,136,128]{2,1,0:T(8,128)(2,1)} custom-call(s32[1]{0:T(128)} %bitcast.rank_ref.refs_0_, s32[15,64]{1,0:T(8,128)} %bitcast.6, bf16[256,128]{1,0:T(8,128)(2,1)} %refs_4_.3, bf16[256,128]{1,0:T(8,128)(2,1)} %refs_5_.3, bf16[4,128]{1,0:T(4,128)(2,1)} %ck_ref.1, bf16[4,128]{1,0:T(4,128)(2,1)} %cv_ref.1), custom_call_target="tpu_custom_call" | custom-call | tf_op jit(solution)/shard_map/pack/pallas_call | solution.py:316
  2.6 0.0 copy-start
  2.6 0.0 copy-start.1
  2.6 0.0 copy-start.2
  2.6 0.0 copy-start.4
  2.6 0.0 copy-start.5
  2.6 7.5 %all-to-all-start = ((bf16[16,136,128]{2,1,0:T(8,128)(2,1)}), bf16[16,136,128]{2,1,0:T(8,128)(2,1)S(1)}, u32[]{:S(2)}, u32[]{:S(2)}) async-start(bf16[16,136,128]{2,1,0:T(8,128)(2,1)} %pack.1), calls=%async_computation | async-start | bytes 1114112 | tf_op jit(solution)/shard_map/all_to_all | solution.py:314
  10.1 2.6 %gate.1.refs_6_ = f32[4,2,1024]{2,1,0:T(2,128)} custom-call(bf16[256,2560]{1,0:T(8,128)(2,1)} %x_ref.1, bf16[32,2560]{1,0:T(8,128)(2,1)} %bitcast.10), custom_call_target="tpu_custom_call" | custom-call | flops 41943040 | bytes 1310720 | tf_op jit(solution)/shard_map/gate/pallas_call | solution.py:326
  12.7 12.5 %all-to-all-done.refs_7_.refs_8_ = bf16[16,136,128]{2,1,0:T(8,128)(2,1)S(1)} async-done(((bf16[16,136,128]{2,1,0:T(8,128)(2,1)}), bf16[16,136,128]{2,1,0:T(8,128)(2,1)S(1)}, u32[]{:S(2)}, u32[]{:S(2)}) %all-to-all-start) | async-done | bytes 557088 | tf_op jit(solution)/shard_map/all_to_all | solution.py:314
  25.1 0.0 copy-done
  25.1 0.0 copy-done.1
  25.1 0.0 copy-done.2
  25.1 0.0 copy-done.4
  25.2 0.0 copy-done.5
  25.2 0.0 copy-start.3
  25.2 0.7 copy-done.3
  25.9 6.2 %attend0.1 = (bf16[256,2048]{1,0:T(8,128)(2,1)}, f32[128,256]{1,0:T(8,128)S(1)}, f32[32,256]{1,0:T(8,128)S(1)}, f32[64,256]{1,0:T(8,128)S(1)}, bf16[16,128,128]{2,1,0:T(8,128)(2,1)S(1)}) custom-call(s32[1]{0:T(128)} %bitcast.rank_ref.refs_0_, s32[15,64]{1,0:T(8,128)S(1)} %bitcast.7, bf16[256,2048]{1,0:T(8,128)(2,1)S(1)} %copy-done.4, ...), custom_call_target="tpu_custom_call" | custom-call | flops 1677721600 | bytes 4194304 | tf_op jit(solution)/shard_map/attend0/pallas_call | solution.py:362
  32.2 18.5 %all_to_all.15.refs_8_ = bf16[16,128,128]{2,1,0:T(8,128)(2,1)S(1)} all-to-all(bf16[16,128,128]{2,1,0:T(8,128)(2,1)S(1)} %get-tuple-element.20), channel_id=1, replica_groups=mesh['ctx'=16,'head'=2] {'ctx'}, dimensions={0} | all-to-all | bytes 1048576 | tf_op jit(solution)/shard_map/all_to_all | solution.py:314
  50.7 0.0 copy-start.6
  50.7 6.6 %attend1.1 = (bf16[256,2048]{1,0:T(8,128)(2,1)}, f32[256,256]{1,0:T(8,128)S(1)}, f32[32,256]{1,0:T(8,128)S(1)}, f32[64,256]{1,0:T(8,128)S(1)}, bf16[16,136,128]{2,1,0:T(8,128)(2,1)}) custom-call(s32[1]{0:T(128)} %bitcast.rank_ref.refs_0_, s32[15,64]{1,0:T(8,128)S(1)} %bitcast.8, bf16[256,2048]{1,0:T(8,128)(2,1)S(1)} %copy-done.4, ...), custom_call_target="tpu_custom_call", output_to_operand_aliasing={{0}: (9, {})} | custom-call | flops 1677721600 | bytes 4194304 | tf_op jit(solution)/shard_map/attend1/pallas_call | solution.py:362
  57.3 4.1 %all-to-all-start.2 = ((bf16[16,136,128]{2,1,0:T(8,128)(2,1)}), bf16[16,136,128]{2,1,0:T(8,128)(2,1)S(1)}, u32[]{:S(2)}, u32[]{:S(2)}) async-start(bf16[16,136,128]{2,1,0:T(8,128)(2,1)} %get-tuple-element.28), calls=%async_computation.2 | async-start | bytes 1114112 | tf_op jit(solution)/shard_map/all_to_all | solution.py:314
  61.4 0.0 copy-done.6
  61.4 1.6 %collective-permute-start.1 = (bf16[1280,32]{0,1:T(8,128)(2,1)S(1)}, bf16[1280,32]{0,1:T(8,128)(2,1)S(1)}, u32[]{:S(2)}, u32[]{:S(2)}) collective-permute-start(bf16[1280,32]{0,1:T(8,128)(2,1)S(1)} %constant_dynamic-slice_fusion), channel_id=1, source_target_pairs={{0,1},{1,0},{2,3},{3,2},{4,5},{5,4},{6,7},{7,6},{8,9},{9,8},{10,11... | collective-permute-start | bytes 245768 | tf_op jit(solution)/shard_map/ppermute | solution.py:341
  63.0 0.5 collective-permute-start
  63.5 0.3 fusion.1
  63.9 2.6 %collective-permute-done.1 = bf16[1280,32]{0,1:T(8,128)(2,1)S(1)} collective-permute-done((bf16[1280,32]{0,1:T(8,128)(2,1)S(1)}, bf16[1280,32]{0,1:T(8,128)(2,1)S(1)}, u32[]{:S(2)}, u32[]{:S(2)}) %collective-permute-start.1) | collective-permute-done | bytes 81952 | tf_op jit(solution)/shard_map/ppermute | solution.py:341
  66.5 0.3 collective-permute-done
  66.8 1.2 %fusion = bf16[256,1280]{1,0:T(8,128)(2,1)} fusion(f32[256,1280]{1,0:T(8,128)S(1)} %fusion.1, bf16[32,256]{1,0:T(8,128)(2,1)S(1)} %collective-permute-done, bf16[1280,32]{0,1:T(8,128)(2,1)S(1)} %collective-permute-done.1), kind=kOutput, calls=%fused_computation.1 | convolution fusion | flops 21626880 | bytes 2064384 | tf_op jit(solution)/shard_map/dot_general | solution.py:419
  68.0 8.5 %all-to-all-done.2.home_ref = bf16[16,136,128]{2,1,0:T(8,128)(2,1)S(1)} async-done(((bf16[16,136,128]{2,1,0:T(8,128)(2,1)}), bf16[16,136,128]{2,1,0:T(8,128)(2,1)S(1)}, u32[]{:S(2)}, u32[]{:S(2)}) %all-to-all-start.2) | async-done | bytes 557088 | tf_op jit(solution)/shard_map/all_to_all | solution.py:314
  76.4 1.6 %finish.1 = (bf16[256,128]{1,0:T(8,128)(2,1)}, bf16[256,128]{1,0:T(8,128)(2,1)}, bf16[4,128]{1,0:T(4,128)(2,1)}, bf16[4,128]{1,0:T(4,128)(2,1)}) custom-call(s32[1]{0:T(128)} %bitcast.rank_ref.refs_0_, s32[15,64]{1,0:T(8,128)S(1)} %bitcast.9, f32[256,256]{1,0:T(8,128)S(1)} %get-tuple-element.26.part_ref, f32[64,256]{1,0:T(8,128)S(1)} %get-tuple-element.27.dc_ref, ...), custom_call_target="tpu_custom_call" | custom-call | tf_op jit(solution)/shard_map/finish/pallas_call | solution.py:402
  (2 shorter events, 0.0 us)
Async XLA Ops:
  2.6 22.6 %copy-start = (bf16[256,128]{1,0:T(8,128)(2,1)S(1)}, bf16[256,128]{1,0:T(8,128)(2,1)}, u32[]{:S(2)}) copy-start(bf16[256,128]{1,0:T(8,128)(2,1)} %refs_4_.3) | copy-start | bytes 196612
  2.6 22.6 %copy-start.1 = (bf16[256,128]{1,0:T(8,128)(2,1)S(1)}, bf16[256,128]{1,0:T(8,128)(2,1)}, u32[]{:S(2)}) copy-start(bf16[256,128]{1,0:T(8,128)(2,1)} %refs_5_.3) | copy-start | bytes 196612
  2.6 22.6 %copy-start.2 = (s32[64,15]{0,1:T(8,128)S(1)}, s32[64,15]{0,1:T(8,128)}, u32[]{:S(2)}) copy-start(s32[64,15]{0,1:T(8,128)} %param.14) | copy-start | bytes 11524
  2.6 22.6 %copy-start.4 = (bf16[256,2048]{1,0:T(8,128)(2,1)S(1)}, bf16[256,2048]{1,0:T(8,128)(2,1)}, u32[]{:S(2)}) copy-start(bf16[256,2048]{1,0:T(8,128)(2,1)} %refs_2_.3) | copy-start | bytes 3145732
  2.6 22.6 %copy-start.5 = (bf16[256,2048]{1,0:T(8,128)(2,1)S(1)}, bf16[256,2048]{1,0:T(8,128)(2,1)}, u32[]{:S(2)}) copy-start(bf16[256,2048]{1,0:T(8,128)(2,1)} %refs_3_.3) | copy-start | bytes 3145732
  2.6 22.5 %all-to-all-start = ((bf16[16,136,128]{2,1,0:T(8,128)(2,1)}), bf16[16,136,128]{2,1,0:T(8,128)(2,1)S(1)}, u32[]{:S(2)}, u32[]{:S(2)}) async-start(bf16[16,136,128]{2,1,0:T(8,128)(2,1)} %pack.1), calls=%async_computation | async-start | bytes 1114112 | tf_op jit(solution)/shard_map/all_to_all | solution.py:314
  25.2 0.8 copy-start.3
  50.7 10.7 %copy-start.6 = (bf16[2560,32]{0,1:T(8,128)(2,1)S(1)}, bf16[2560,32]{0,1:T(8,128)(2,1)}, u32[]{:S(2)}) copy-start(bf16[2560,32]{0,1:T(8,128)(2,1)} %param.16) | copy-start | bytes 491524
  57.3 19.1 %all-to-all-start.2 = ((bf16[16,136,128]{2,1,0:T(8,128)(2,1)}), bf16[16,136,128]{2,1,0:T(8,128)(2,1)S(1)}, u32[]{:S(2)}, u32[]{:S(2)}) async-start(bf16[16,136,128]{2,1,0:T(8,128)(2,1)} %get-tuple-element.28), calls=%async_computation.2 | async-start | bytes 1114112 | tf_op jit(solution)/shard_map/all_to_all | solution.py:314
  61.4 5.0 %collective-permute-start.1 = (bf16[1280,32]{0,1:T(8,128)(2,1)S(1)}, bf16[1280,32]{0,1:T(8,128)(2,1)S(1)}, u32[]{:S(2)}, u32[]{:S(2)}) collective-permute-start(bf16[1280,32]{0,1:T(8,128)(2,1)S(1)} %constant_dynamic-slice_fusion), channel_id=1, source_target_pairs={{0,1},{1,0},{2,3},{3,2},{4,5},{5,4},{6,7},{7,6},{8,9},{9,8},{10,11... | collective-permute-start | bytes 245768 | tf_op jit(solution)/shard_map/ppermute | solution.py:341
  63.0 3.7 %collective-permute-start = (bf16[32,256]{1,0:T(8,128)(2,1)S(1)}, bf16[32,256]{1,0:T(8,128)(2,1)S(1)}, u32[]{:S(2)}, u32[]{:S(2)}) collective-permute-start(bf16[32,256]{1,0:T(8,128)(2,1)S(1)} %convert_element_type.6), channel_id=1, source_target_pairs={{0,1},{1,0},{2,3},{3,2},{4,5},{5,4},{6,7},{7,6},{8,9},{9,8},{10,11... | collective-permute-start | bytes 49160 | tf_op jit(solution)/shard_map/ppermute | solution.py:415

commit v5 on v4

--- a/solution.py
+++ b/solution.py
@@ -65,7 +65,10 @@
     fill_picks(ranks, qb, lists, 0, me, sel_ref, k_ref, v_ref, out_ref)
 
 
-def gate_kernel(qb, heads, x_ref, w_ref, out_ref):
+def gate_kernel(qb, heads, x_hbm, w_ref, out_ref, x_ref, sem):
+    copy = pltpu.make_async_copy(x_hbm, x_ref, sem)
+    copy.start()
+    copy.wait()
     nt = (((1,), (1,)), ((), ()))
     z = lax.dot_general(w_ref[...], x_ref[...], nt, preferred_element_type=F32)
     zt = jax.nn.sigmoid(z)
@@ -165,7 +168,7 @@
 
 
 def attend_row(ranks, qb, heads, reach, me, row, parity, q_ref, do_ref, k_ref, v_ref, gate_ref,
-               comp_ref, picks_ref, dq_ref, own_ref, send_ref, kcat, vcat, kt, qs, ds,
+               comp_ref, picks_ref, dq_ref, own_ref, send_ref, kcat, vcat, qs, ds,
                s_scr, u_scr, w_scr, d_scr, dv_acc, dk_acc, dg_scr, dc_scr):
     npick = len(reach)
     hd = k_ref.shape[1]
@@ -186,7 +189,6 @@
         src = jnp.where(me >= r, me - r, me)
         kcat[(n + 1) * BLK : (n + 2) * BLK, :] = picks_ref[src, :BLK, :]
         vcat[(n + 1) * BLK : (n + 2) * BLK, :] = picks_ref[src, BLK : 2 * BLK, :]
-    kt[:, :nk] = kcat[:nk, :].astype(F32).T.astype(BF16)
     for h in range(heads):
         qs[h * BLK : (h + 1) * BLK, :] = q_ref[:, h * hd : (h + 1) * hd]
         ds[h * BLK : (h + 1) * BLK, :] = do_ref[:, h * hd : (h + 1) * hd]
@@ -233,8 +235,9 @@
         else:
             dv_acc[:nk, :] += dv
             dk_acc[:nk, :] += dk
-        dqt = jnp.dot(kt[:, :nk], d_scr[:nk, lanes], preferred_element_type=F32)
-        dq = (dqt.T * scale).astype(BF16)
+        tn = (((0,), (0,)), ((), ()))
+        dq = lax.dot_general(d_scr[:nk, lanes], kcat[:nk, :], tn, preferred_element_type=F32)
+        dq = (dq * scale).astype(BF16)
         for h in range(per):
             head = c * per + h
             dq_ref[:, head * hd : (head + 1) * hd] = dq[h * BLK : (h + 1) * BLK, :]
@@ -326,9 +329,10 @@
     gate = pl.pallas_call(
         functools.partial(gate_kernel, qb, heads),
         out_shape=jax.ShapeDtypeStruct((qb, 2, heads * BLK), F32),
-        in_specs=[in_vmem()] * 2,
+        in_specs=[pl.BlockSpec(memory_space=pl.ANY), in_vmem()],
         out_specs=in_vmem(),
-        compiler_params=params(ranks, 60),
+        scratch_shapes=[pltpu.VMEM(inputs.shape, BF16), pltpu.SemaphoreType.DMA],
+        compiler_params=params(ranks),
         cost_estimate=pl.CostEstimate(
             flops=2 * inputs.size * w_gate.shape[1], bytes_accessed=2 * inputs.size, transcendentals=0
         ),
@@ -374,7 +378,6 @@
             scratch_shapes=[
                 pltpu.VMEM((nk, hd), BF16),
                 pltpu.VMEM((nk, hd), BF16),
-                pltpu.VMEM((hd, nk), BF16),
                 pltpu.VMEM((heads * BLK, hd), BF16),
                 pltpu.VMEM((heads * BLK, hd), BF16),
                 pltpu.VMEM((2, nk, LANES), F32),

time: 78.5 us -> 80.4 us (1.024)
  waiting for transfers between devices: 23.8 us -> 25.6 us
    pallas_call x1, Pallas kernels: 2.56 us -> 0.72 us  [body(): pl.pallas_call(functools.partial(gate_kernel, qb, heads), out_shape=jax.S...]
    all_to_all x2, waiting for transfers between devices: 20.9 us -> 22.7 us  [exchange(): return lax.all_to_all(x, 'ctx', split_axis=0, concat_axis=0, tiled=True)]
    pallas_call x2, Pallas kernels: 12.9 us -> 14.3 us  [attend(): pl.pallas_call(functools.partial(attend_kernel, ranks, qb, heads, lists,...]
  transfers between devices with their start and end apart: 4 -> 4, of which waited for: 4 -> 4; matrix products, arithmetic and copies ran while one was open for 2% -> 2% of each run, Pallas kernels for 3% -> 1%
where the time goes in v5:
time: 80.4 us; the launch traced here: 80 us
  waiting for transfers between devices  25.6 us (32%)
  Pallas kernels  18.6 us (23%)
  blocking collectives  18.5 us (23%)
  starting transfers between devices  13.7 us (17%)
  matrix products  1.55 us (2%)
  local copies, waits for them, and re-layouts  1.26 us (2%)
    all_to_all x2, waiting for transfers between devices, exchange(): return lax.all_to_all(x, 'ctx', split_axis=0, concat_axis=0, tiled=True)  22.7 us
    all_to_all x1, blocking collectives, exchange(): return lax.all_to_all(x, 'ctx', split_axis=0, concat_axis=0, tiled=True)  18.5 us
    pallas_call x2, Pallas kernels, attend(): pl.pallas_call(functools.partial(attend_kernel, ranks, qb, heads, lists,...  14.3 us
    all_to_all x2, starting transfers between devices, exchange(): return lax.all_to_all(x, 'ctx', split_axis=0, concat_axis=0, tiled=True)  11.6 us
    ppermute x1, waiting for transfers between devices, body(): w_other = lax.ppermute(w_send, 'head', swap)  2.5 us
    pallas_call x1, Pallas kernels, body(): pl.pallas_call(functools.partial(pack_kernel, ranks, qb, lists), out_shap...  2 us
    ppermute x1, starting transfers between devices, body(): w_other = lax.ppermute(w_send, 'head', swap)  1.62 us
  transfers between devices with their start and end apart: 4, of which 4 were waited for; matrix products, arithmetic and copies ran while one was open for 2% of the time, Pallas kernels for 1%

profile of v5, /device:TPU:0, one launch (start us, length us, event | category | flops | bytes accessed | tf_op | source)
XLA Modules:
  0.0 80.0 jit_solution(5021987426919046430)
XLA Ops:
  0.6 0.0 copy-start.1
  0.6 0.0 copy-start
  0.7 2.0 %pack.1 = bf16[16,136,128]{2,1,0:T(8,128)(2,1)} custom-call(s32[1]{0:T(128)} %bitcast.rank_ref.refs_0_, s32[15,64]{1,0:T(8,128)} %bitcast.7, bf16[256,128]{1,0:T(8,128)(2,1)} %refs_4_.3, bf16[256,128]{1,0:T(8,128)(2,1)} %refs_5_.3, bf16[4,128]{1,0:T(4,128)(2,1)} %ck_ref.1, bf16[4,128]{1,0:T(4,128)(2,1)} %cv_ref.1), custom_call_target="tpu_custom_call" | custom-call | tf_op jit(solution)/shard_map/pack/pallas_call | solution.py:319
  2.7 0.0 copy-start.2
  2.7 0.0 copy-start.3
  2.7 0.0 copy-start.4
  2.7 0.0 copy-start.5
  2.7 7.5 %all-to-all-start = ((bf16[16,136,128]{2,1,0:T(8,128)(2,1)}), bf16[16,136,128]{2,1,0:T(8,128)(2,1)S(1)}, u32[]{:S(2)}, u32[]{:S(2)}) async-start(bf16[16,136,128]{2,1,0:T(8,128)(2,1)} %pack.1), calls=%async_computation | async-start | bytes 1114112 | tf_op jit(solution)/shard_map/all_to_all | solution.py:317
  10.2 0.0 copy-done.1
  10.2 0.0 copy-done
  10.2 0.7 gate.1.refs_6_
  10.9 14.3 %all-to-all-done.refs_7_.refs_8_ = bf16[16,136,128]{2,1,0:T(8,128)(2,1)S(1)} async-done(((bf16[16,136,128]{2,1,0:T(8,128)(2,1)}), bf16[16,136,128]{2,1,0:T(8,128)(2,1)S(1)}, u32[]{:S(2)}, u32[]{:S(2)}) %all-to-all-start) | async-done | bytes 557088 | tf_op jit(solution)/shard_map/all_to_all | solution.py:317
  25.2 0.0 copy-done.2
  25.2 0.0 copy-done.3
  25.2 0.0 copy-done.4
  25.2 0.0 copy-done.5
  25.2 0.0 copy-start.6
  25.2 1.2 %copy-done.6 = bf16[256,2048]{1,0:T(8,128)(2,1)S(1)} copy-done((bf16[256,2048]{1,0:T(8,128)(2,1)S(1)}, bf16[256,2048]{1,0:T(8,128)(2,1)}, u32[]{:S(2)}) %copy-start.6) | copy-done | bytes 1048600
  26.5 6.9 %attend0.1 = (bf16[256,2048]{1,0:T(8,128)(2,1)}, f32[128,256]{1,0:T(8,128)S(1)}, f32[32,256]{1,0:T(8,128)S(1)}, f32[64,256]{1,0:T(8,128)S(1)}, bf16[16,128,128]{2,1,0:T(8,128)(2,1)S(1)}) custom-call(s32[1]{0:T(128)} %bitcast.rank_ref.refs_0_, s32[15,64]{1,0:T(8,128)S(1)} %bitcast.8, bf16[256,2048]{1,0:T(8,128)(2,1)S(1)} %copy-done.5, ...), custom_call_target="tpu_custom_call" | custom-call | flops 1677721600 | bytes 4194304 | tf_op jit(solution)/shard_map/attend0/pallas_call | solution.py:366
  33.4 18.5 %all_to_all.15.refs_8_ = bf16[16,128,128]{2,1,0:T(8,128)(2,1)S(1)} all-to-all(bf16[16,128,128]{2,1,0:T(8,128)(2,1)S(1)} %get-tuple-element.20), channel_id=1, replica_groups=mesh['ctx'=16,'head'=2] {'ctx'}, dimensions={0} | all-to-all | bytes 1048576 | tf_op jit(solution)/shard_map/all_to_all | solution.py:317
  51.9 7.4 %attend1.1 = (bf16[256,2048]{1,0:T(8,128)(2,1)}, f32[256,256]{1,0:T(8,128)S(1)}, f32[32,256]{1,0:T(8,128)S(1)}, f32[64,256]{1,0:T(8,128)S(1)}, bf16[16,136,128]{2,1,0:T(8,128)(2,1)}) custom-call(s32[1]{0:T(128)} %bitcast.rank_ref.refs_0_, s32[15,64]{1,0:T(8,128)S(1)} %bitcast.9, bf16[256,2048]{1,0:T(8,128)(2,1)S(1)} %copy-done.5, ...), custom_call_target="tpu_custom_call", output_to_operand_aliasing={{0}: (9, {})} | custom-call | flops 1677721600 | bytes 4194304 | tf_op jit(solution)/shard_map/attend1/pallas_call | solution.py:366
  59.3 4.1 %all-to-all-start.2 = ((bf16[16,136,128]{2,1,0:T(8,128)(2,1)}), bf16[16,136,128]{2,1,0:T(8,128)(2,1)S(1)}, u32[]{:S(2)}, u32[]{:S(2)}) async-start(bf16[16,136,128]{2,1,0:T(8,128)(2,1)} %get-tuple-element.28), calls=%async_computation.2 | async-start | bytes 1114112 | tf_op jit(solution)/shard_map/all_to_all | solution.py:317
  63.4 1.6 %collective-permute-start.1 = (bf16[1280,32]{0,1:T(8,128)(2,1)S(1)}, bf16[1280,32]{0,1:T(8,128)(2,1)S(1)}, u32[]{:S(2)}, u32[]{:S(2)}) collective-permute-start(bf16[1280,32]{0,1:T(8,128)(2,1)S(1)} %constant_dynamic-slice_fusion), channel_id=1, source_target_pairs={{0,1},{1,0},{2,3},{3,2},{4,5},{5,4},{6,7},{7,6},{8,9},{9,8},{10,11... | collective-permute-start | bytes 245768 | tf_op jit(solution)/shard_map/ppermute | solution.py:345
  65.0 0.5 collective-permute-start
  65.5 0.3 fusion.1
  65.9 2.5 %collective-permute-done.1 = bf16[1280,32]{0,1:T(8,128)(2,1)S(1)} collective-permute-done((bf16[1280,32]{0,1:T(8,128)(2,1)S(1)}, bf16[1280,32]{0,1:T(8,128)(2,1)S(1)}, u32[]{:S(2)}, u32[]{:S(2)}) %collective-permute-start.1) | collective-permute-done | bytes 81952 | tf_op jit(solution)/shard_map/ppermute | solution.py:345
  68.4 0.4 collective-permute-done
  68.8 1.2 %fusion = bf16[256,1280]{1,0:T(8,128)(2,1)} fusion(f32[256,1280]{1,0:T(8,128)S(1)} %fusion.1, bf16[32,256]{1,0:T(8,128)(2,1)S(1)} %collective-permute-done, bf16[1280,32]{0,1:T(8,128)(2,1)S(1)} %collective-permute-done.1), kind=kOutput, calls=%fused_computation.1 | convolution fusion | flops 21626880 | bytes 2064384 | tf_op jit(solution)/shard_map/dot_general | solution.py:422
  70.0 8.4 %all-to-all-done.2.home_ref = bf16[16,136,128]{2,1,0:T(8,128)(2,1)S(1)} async-done(((bf16[16,136,128]{2,1,0:T(8,128)(2,1)}), bf16[16,136,128]{2,1,0:T(8,128)(2,1)S(1)}, u32[]{:S(2)}, u32[]{:S(2)}) %all-to-all-start.2) | async-done | bytes 557088 | tf_op jit(solution)/shard_map/all_to_all | solution.py:317
  78.4 1.6 %finish.1 = (bf16[256,128]{1,0:T(8,128)(2,1)}, bf16[256,128]{1,0:T(8,128)(2,1)}, bf16[4,128]{1,0:T(4,128)(2,1)}, bf16[4,128]{1,0:T(4,128)(2,1)}) custom-call(s32[1]{0:T(128)} %bitcast.rank_ref.refs_0_, s32[15,64]{1,0:T(8,128)S(1)} %bitcast.10, f32[256,256]{1,0:T(8,128)S(1)} %get-tuple-element.26.part_ref, f32[64,256]{1,0:T(8,128)S(1)} %get-tuple-element.27.dc_ref, ...), custom_call_target="tpu_custom_call" | custom-call | tf_op jit(solution)/shard_map/finish/pallas_call | solution.py:405
  (2 shorter events, 0.0 us)
Async XLA Ops:
  0.6 9.6 %copy-start.1 = (bf16[2560,32]{0,1:T(8,128)(2,1)S(1)}, bf16[2560,32]{0,1:T(8,128)(2,1)}, u32[]{:S(2)}) copy-start(bf16[2560,32]{0,1:T(8,128)(2,1)} %param.16) | copy-start | bytes 491524
  0.6 9.6 %copy-start = (bf16[256,2560]{1,0:T(8,128)(2,1)S(1)}, bf16[256,2560]{1,0:T(8,128)(2,1)}, u32[]{:S(2)}) copy-start(bf16[256,2560]{1,0:T(8,128)(2,1)} %x_hbm.1) | copy-start | bytes 3932164
  2.7 22.6 %copy-start.2 = (bf16[256,128]{1,0:T(8,128)(2,1)S(1)}, bf16[256,128]{1,0:T(8,128)(2,1)}, u32[]{:S(2)}) copy-start(bf16[256,128]{1,0:T(8,128)(2,1)} %refs_4_.3) | copy-start | bytes 196612
  2.7 22.6 %copy-start.3 = (bf16[256,128]{1,0:T(8,128)(2,1)S(1)}, bf16[256,128]{1,0:T(8,128)(2,1)}, u32[]{:S(2)}) copy-start(bf16[256,128]{1,0:T(8,128)(2,1)} %refs_5_.3) | copy-start | bytes 196612
  2.7 22.6 %copy-start.4 = (s32[64,15]{0,1:T(8,128)S(1)}, s32[64,15]{0,1:T(8,128)}, u32[]{:S(2)}) copy-start(s32[64,15]{0,1:T(8,128)} %param.14) | copy-start | bytes 11524
  2.7 22.6 %copy-start.5 = (bf16[256,2048]{1,0:T(8,128)(2,1)S(1)}, bf16[256,2048]{1,0:T(8,128)(2,1)}, u32[]{:S(2)}) copy-start(bf16[256,2048]{1,0:T(8,128)(2,1)} %refs_2_.3) | copy-start | bytes 3145732
  2.7 22.5 %all-to-all-start = ((bf16[16,136,128]{2,1,0:T(8,128)(2,1)}), bf16[16,136,128]{2,1,0:T(8,128)(2,1)S(1)}, u32[]{:S(2)}, u32[]{:S(2)}) async-start(bf16[16,136,128]{2,1,0:T(8,128)(2,1)} %pack.1), calls=%async_computation | async-start | bytes 1114112 | tf_op jit(solution)/shard_map/all_to_all | solution.py:317
  25.2 1.2 %copy-start.6 = (bf16[256,2048]{1,0:T(8,128)(2,1)S(1)}, bf16[256,2048]{1,0:T(8,128)(2,1)}, u32[]{:S(2)}) copy-start(bf16[256,2048]{1,0:T(8,128)(2,1)} %refs_3_.3) | copy-start | bytes 3145732
  59.3 19.1 %all-to-all-start.2 = ((bf16[16,136,128]{2,1,0:T(8,128)(2,1)}), bf16[16,136,128]{2,1,0:T(8,128)(2,1)S(1)}, u32[]{:S(2)}, u32[]{:S(2)}) async-start(bf16[16,136,128]{2,1,0:T(8,128)(2,1)} %get-tuple-element.28), calls=%async_computation.2 | async-start | bytes 1114112 | tf_op jit(solution)/shard_map/all_to_all | solution.py:317
  63.4 5.0 %collective-permute-start.1 = (bf16[1280,32]{0,1:T(8,128)(2,1)S(1)}, bf16[1280,32]{0,1:T(8,128)(2,1)S(1)}, u32[]{:S(2)}, u32[]{:S(2)}) collective-permute-start(bf16[1280,32]{0,1:T(8,128)(2,1)S(1)} %constant_dynamic-slice_fusion), channel_id=1, source_target_pairs={{0,1},{1,0},{2,3},{3,2},{4,5},{5,4},{6,7},{7,6},{8,9},{9,8},{10,11... | collective-permute-start | bytes 245768 | tf_op jit(solution)/shard_map/ppermute | solution.py:345
  65.0 3.7 %collective-permute-start = (bf16[32,256]{1,0:T(8,128)(2,1)S(1)}, bf16[32,256]{1,0:T(8,128)(2,1)S(1)}, u32[]{:S(2)}, u32[]{:S(2)}) collective-permute-start(bf16[32,256]{1,0:T(8,128)(2,1)S(1)} %convert_element_type.6), channel_id=1, source_target_pairs={{0,1},{1,0},{2,3},{3,2},{4,5},{5,4},{6,7},{7,6},{8,9},{9,8},{10,11... | collective-permute-start | bytes 49160 | tf_op jit(solution)/shard_map/ppermute | solution.py:418

commit v6 on v4

--- a/solution.py
+++ b/solution.py
@@ -113,9 +113,10 @@
 def attend_kernel(ranks, qb, heads, lists, p, *refs):
     (rank_ref, sel_ref, q_ref, do_ref, k_ref, v_ref, gate_ref, comp_ref, picks_ref) = refs[:9]
     if p == 0:
-        dq_ref, own_ref, dz_ref, dc_ref, send_ref, *scratch = refs[9:]
+        dq_ref, own_ref, dz_ref, dc_ref, send_ref, ckv_ref, *scratch = refs[9:]
     else:
-        _, dz_in, dc_in, own_in, dq_ref, own_ref, dz_ref, dc_ref, send_ref, *scratch = refs[9:]
+        dz_in, dc_in, own_in, own_ref, dz_ref, dc_ref, send_ref, *scratch = refs[9:]
+        dq_ref, ckv_ref = None, None
     hd = k_ref.shape[1]
     me = rank_ref[0]
     step = pl.program_id(0)
@@ -140,7 +141,7 @@
         @pl.when(step == parity)
         def _(parity=parity):
             attend_row(ranks, qb, heads, lists[parity], me, 2 * p + parity, parity, q_ref, do_ref, k_ref, v_ref,
-                       gate_ref, comp_ref, picks_ref, dq_ref, own_ref, send_ref, *scratch)
+                       gate_ref, comp_ref, picks_ref, dq_ref, own_ref, send_ref, ckv_ref, *scratch)
 
     @pl.when(step == 1)
     def _():
@@ -164,8 +165,20 @@
                     ]
 
 
+def tail_kernel(ranks, qb, heads, lists, rank_ref, q_ref, do_ref, k_ref, v_ref, gate_ref, ckv_ref,
+                picks_ref, _, dq_ref, *scratch):
+    me = rank_ref[0]
+    step = pl.program_id(0)
+    for parity in range(2):
+
+        @pl.when(step == parity)
+        def _(parity=parity):
+            attend_row(ranks, qb, heads, lists[parity], me, 2 + parity, parity, q_ref, do_ref, k_ref, v_ref,
+                       gate_ref, ckv_ref, picks_ref, dq_ref, None, None, None, *scratch)
+
+
 def attend_row(ranks, qb, heads, reach, me, row, parity, q_ref, do_ref, k_ref, v_ref, gate_ref,
-               comp_ref, picks_ref, dq_ref, own_ref, send_ref, kcat, vcat, kt, qs, ds,
+               comp_ref, picks_ref, dq_ref, own_ref, send_ref, ckv_ref, kcat, vcat, kt, qs, ds,
                s_scr, u_scr, w_scr, d_scr, dv_acc, dk_acc, dg_scr, dc_scr):
     npick = len(reach)
     hd = k_ref.shape[1]
@@ -175,18 +188,25 @@
     per = LANES // BLK
     scale = hd ** -0.5
 
-    pieces = []
-    for r in range(ranks):
-        pieces.append(comp_ref[jnp.maximum(me - r, 0)].astype(F32))
-    kcat[nsel:nk, :] = jnp.concatenate([x[:qb] for x in pieces], axis=0).astype(BF16)
-    vcat[nsel:nk, :] = jnp.concatenate([x[qb:] for x in pieces], axis=0).astype(BF16)
+    if len(comp_ref.shape) == 3:
+        pieces = []
+        for r in range(ranks):
+            pieces.append(comp_ref[jnp.maximum(me - r, 0)].astype(F32))
+        kcat[nsel:nk, :] = jnp.concatenate([x[:qb] for x in pieces], axis=0).astype(BF16)
+        vcat[nsel:nk, :] = jnp.concatenate([x[qb:] for x in pieces], axis=0).astype(BF16)
+        ckv_ref[:, :hd] = kcat[nsel:nk, :]
+        ckv_ref[:, hd:] = vcat[nsel:nk, :]
+    else:
+        kcat[nsel:nk, :] = comp_ref[:, :hd]
+        vcat[nsel:nk, :] = comp_ref[:, hd:]
     kcat[:BLK, :] = k_ref[row * BLK : (row + 1) * BLK, :]
     vcat[:BLK, :] = v_ref[row * BLK : (row + 1) * BLK, :]
     for n, (_, r) in enumerate(reach):
         src = jnp.where(me >= r, me - r, me)
         kcat[(n + 1) * BLK : (n + 2) * BLK, :] = picks_ref[src, :BLK, :]
         vcat[(n + 1) * BLK : (n + 2) * BLK, :] = picks_ref[src, BLK : 2 * BLK, :]
-    kt[:, :nk] = kcat[:nk, :].astype(F32).T.astype(BF16)
+    if dq_ref is not None:
+        kt[:, :nk] = kcat[:nk, :].astype(F32).T.astype(BF16)
     for h in range(heads):
         qs[h * BLK : (h + 1) * BLK, :] = q_ref[:, h * hd : (h + 1) * hd]
         ds[h * BLK : (h + 1) * BLK, :] = do_ref[:, h * hd : (h + 1) * hd]
@@ -225,19 +245,21 @@
 
     def gradients(c):
         lanes = lanes_of(c)
-        dv = jnp.dot(w_scr[:nk, lanes], ds[lanes, :], preferred_element_type=F32)
-        dk = jnp.dot(d_scr[:nk, lanes], qs[lanes, :], preferred_element_type=F32)
-        if c == 0:
-            dv_acc[:nk, :] = dv
-            dk_acc[:nk, :] = dk
-        else:
-            dv_acc[:nk, :] += dv
-            dk_acc[:nk, :] += dk
-        dqt = jnp.dot(kt[:, :nk], d_scr[:nk, lanes], preferred_element_type=F32)
-        dq = (dqt.T * scale).astype(BF16)
-        for h in range(per):
-            head = c * per + h
-            dq_ref[:, head * hd : (head + 1) * hd] = dq[h * BLK : (h + 1) * BLK, :]
+        if send_ref is not None:
+            dv = jnp.dot(w_scr[:nk, lanes], ds[lanes, :], preferred_element_type=F32)
+            dk = jnp.dot(d_scr[:nk, lanes], qs[lanes, :], preferred_element_type=F32)
+            if c == 0:
+                dv_acc[:nk, :] = dv
+                dk_acc[:nk, :] = dk
+            else:
+                dv_acc[:nk, :] += dv
+                dk_acc[:nk, :] += dk
+        if dq_ref is not None:
+            dqt = jnp.dot(kt[:, :nk], d_scr[:nk, lanes], preferred_element_type=F32)
+            dq = (dqt.T * scale).astype(BF16)
+            for h in range(per):
+                head = c * per + h
+                dq_ref[:, head * hd : (head + 1) * hd] = dq[h * BLK : (h + 1) * BLK, :]
 
     scores(0)
     for c in range(chunks):
@@ -247,6 +269,8 @@
             gradients(c - 1)
         soften(c)
     gradients(chunks - 1)
+    if send_ref is None:
+        return
 
     own = slice(row * BLK, (row + 1) * BLK)
     if row < 2:
@@ -342,62 +366,83 @@
 
     nk = (1 + max(len(x) for x in lists)) * BLK + nblocks
 
-    def attend(p, picks, previous):
+    def row_specs(p):
         row = lambda i: (2 * p + i, 0)
-        out_slot = slot if p else 2 * BLK
-        args = [me, table, queries, d_out, keys, values, gate, fetched, picks] + previous
-        in_specs = [
-            in_smem(),
-            in_smem(),
+        return [
             pl.BlockSpec((BLK, width), row),
             pl.BlockSpec((BLK, width), row),
             in_vmem(),
             in_vmem(),
             pl.BlockSpec((1, 2, heads * BLK), lambda i: (2 * p + i, 0, 0)),
-            pl.BlockSpec((ranks, 2 * qb, hd), lambda i: (0, 2 * BLK // (2 * qb), 0)),
-            pl.BlockSpec((ranks, 2 * BLK, hd), lambda i: (0, 0, 0)),
         ]
-        if previous:
-            in_specs += [pl.BlockSpec(memory_space=pl.ANY)] + [in_vmem()] * 3
+
+    scratch = [
+        pltpu.VMEM((nk, hd), BF16),
+        pltpu.VMEM((nk, hd), BF16),
+        pltpu.VMEM((hd, nk), BF16),
+        pltpu.VMEM((heads * BLK, hd), BF16),
+        pltpu.VMEM((heads * BLK, hd), BF16),
+        pltpu.VMEM((2, nk, LANES), F32),
+        pltpu.VMEM((2, nk, LANES), F32),
+        pltpu.VMEM((nk, heads * BLK), BF16),
+        pltpu.VMEM((nk, heads * BLK), BF16),
+        pltpu.VMEM((nk, hd), F32),
+        pltpu.VMEM((nk, hd), F32),
+        pltpu.VMEM((2, 2, heads * BLK), F32),
+        pltpu.VMEM((nblocks, 2 * hd), F32),
+    ]
+    cost = pl.CostEstimate(
+        flops=10 * nk * heads * 2 * BLK * hd, bytes_accessed=4 << 20, transcendentals=0
+    )
+    pick_spec = pl.BlockSpec((ranks, 2 * BLK, hd), lambda i: (0, 0, 0))
+
+    def attend(p, comp, picks, previous):
+        out_slot = slot if p else 2 * BLK
+        comp_spec = in_vmem()
+        out_shape = [
+            jax.ShapeDtypeStruct((tokens if p else 2 * BLK, 2 * hd), F32),
+            jax.ShapeDtypeStruct((2 * heads, tokens), F32),
+            jax.ShapeDtypeStruct((nblocks, 2 * hd), F32),
+            jax.ShapeDtypeStruct((ranks, out_slot, hd), BF16),
+        ]
+        out_specs = [in_vmem()] * 4
+        if p == 0:
+            comp_spec = pl.BlockSpec((ranks, 2 * qb, hd), lambda i: (0, 2 * BLK // (2 * qb), 0))
+            out_shape = (
+                [jax.ShapeDtypeStruct(queries.shape, BF16)]
+                + out_shape
+                + [jax.ShapeDtypeStruct((nblocks, 2 * hd), BF16)]
+            )
+            out_specs = [pl.BlockSpec((BLK, width), lambda i: (i, 0))] + out_specs + [in_vmem()]
         return pl.pallas_call(
             functools.partial(attend_kernel, ranks, qb, heads, lists, p),
             grid=(2,),
-            out_shape=[
-                jax.ShapeDtypeStruct(queries.shape, BF16),
-                jax.ShapeDtypeStruct((tokens if p else 2 * BLK, 2 * hd), F32),
-                jax.ShapeDtypeStruct((2 * heads, tokens), F32),
-                jax.ShapeDtypeStruct((nblocks, 2 * hd), F32),
-                jax.ShapeDtypeStruct((ranks, out_slot, hd), BF16),
-            ],
-            in_specs=in_specs,
-            out_specs=[pl.BlockSpec((BLK, width), row)] + [in_vmem()] * 4,
-            scratch_shapes=[
-                pltpu.VMEM((nk, hd), BF16),
-                pltpu.VMEM((nk, hd), BF16),
-                pltpu.VMEM((hd, nk), BF16),
-                pltpu.VMEM((heads * BLK, hd), BF16),
-                pltpu.VMEM((heads * BLK, hd), BF16),
-                pltpu.VMEM((2, nk, LANES), F32),
-                pltpu.VMEM((2, nk, LANES), F32),
-                pltpu.VMEM((nk, heads * BLK), BF16),
-                pltpu.VMEM((nk, heads * BLK), BF16),
-                pltpu.VMEM((nk, hd), F32),
-                pltpu.VMEM((nk, hd), F32),
-                pltpu.VMEM((2, 2, heads * BLK), F32),
-                pltpu.VMEM((nblocks, 2 * hd), F32),
-            ],
-            input_output_aliases={9: 0} if previous else {},
+            out_shape=out_shape,
+            in_specs=[in_smem(), in_smem()] + row_specs(p) + [comp_spec, pick_spec]
+            + [in_vmem()] * len(previous),
+            out_specs=out_specs,
+            scratch_shapes=scratch,
             compiler_params=params(ranks),
-            cost_estimate=pl.CostEstimate(
-                flops=10 * nk * heads * 2 * BLK * hd, bytes_accessed=4 << 20, transcendentals=0
-            ),
+            cost_estimate=cost,
             name=f"attend{p}",
-        )(*args)
-
-    dq, own0, dz, dc, send = attend(0, fetched, [])
+        )(me, table, queries, d_out, keys, values, gate, comp, picks, *previous)
+
+    dq, own0, dz, dc, send, ckv = attend(0, fetched, fetched, [])
     mixed = exchange(send)
-    d_queries, part, dz, dc, send = attend(1, mixed, [dq, dz, dc, own0])
+    part, dz, dc, send = attend(1, ckv, mixed, [dz, dc, own0])
     home = exchange(send)
+    d_queries = pl.pallas_call(
+        functools.partial(tail_kernel, ranks, qb, heads, lists),
+        grid=(2,),
+        out_shape=jax.ShapeDtypeStruct(queries.shape, BF16),
+        in_specs=[in_smem()] + row_specs(1) + [in_vmem(), pick_spec, pl.BlockSpec(memory_space=pl.ANY)],
+        out_specs=pl.BlockSpec((BLK, width), lambda i: (2 + i, 0)),
+        scratch_shapes=scratch,
+        input_output_aliases={8: 0},
+        compiler_params=params(ranks),
+        cost_estimate=cost,
+        name="tail",
+    )(me, queries, d_out, keys, values, gate, ckv, mixed, dq)
 
     d_keys, d_values, d_ck, d_cv = pl.pallas_call(
         functools.partial(finish_kernel, ranks, qb, lists),

time: 78.5 us -> 79.2 us (level)
  waiting for transfers between devices: 23.8 us -> 18.6 us
  Pallas kernels: 18.9 us -> 23 us
  local copies, waits for them, and re-layouts: 0.79 us -> 2.37 us
    pallas_call x0 -> x1, Pallas kernels: none -> 4.8 us  [body(): pl.pallas_call(functools.partial(tail_kernel, ranks, qb, heads, lists), g...]
    ppermute x1, waiting for transfers between devices: 2.58 us -> 0.01 us  [body(): w_other = lax.ppermute(w_send, 'head', swap)]
    all_to_all x2, waiting for transfers between devices: 20.9 us -> 18.6 us  [exchange(): return lax.all_to_all(x, 'ctx', split_axis=0, concat_axis=0, tiled=True)]
    unnamed x14 -> x18, local copies, waits for them, and re-layouts: 0.78 us -> 2.35 us
  transfers between devices with their start and end apart: 4 -> 4, of which waited for: 4 -> 2; matrix products, arithmetic and copies ran while one was open for 2% -> 2% of each run, Pallas kernels for 3% -> 9%
where the time goes in v6:
time: 79.2 us; the launch traced here: 78.6 us
  Pallas kernels  23 us (29%)
  waiting for transfers between devices  18.6 us (23%)
  blocking collectives  18.5 us (23%)
  starting transfers between devices  13.9 us (18%)
  local copies, waits for them, and re-layouts  2.37 us (3%)
  matrix products  1.55 us (2%)
    all_to_all x2, waiting for transfers between devices, exchange(): return lax.all_to_all(x, 'ctx', split_axis=0, concat_axis=0, tiled=True)  18.6 us
    all_to_all x1, blocking collectives, exchange(): return lax.all_to_all(x, 'ctx', split_axis=0, concat_axis=0, tiled=True)  18.5 us
    pallas_call x2, Pallas kernels, attend(): pl.pallas_call(functools.partial(attend_kernel, ranks, qb, heads, lists,...  12.1 us
    all_to_all x2, starting transfers between devices, exchange(): return lax.all_to_all(x, 'ctx', split_axis=0, concat_axis=0, tiled=True)  11.7 us
    pallas_call x1, Pallas kernels, body(): pl.pallas_call(functools.partial(tail_kernel, ranks, qb, heads, lists), g...  4.8 us
    pallas_call x1, Pallas kernels, body(): pl.pallas_call(functools.partial(gate_kernel, qb, heads), out_shape=jax.S...  2.56 us
    unnamed x18, local copies, waits for them, and re-layouts  2.35 us
    pallas_call x1, Pallas kernels, body(): pl.pallas_call(functools.partial(pack_kernel, ranks, qb, lists), out_shap...  1.93 us
  transfers between devices with their start and end apart: 4, of which 2 were waited for; matrix products, arithmetic and copies ran while one was open for 2% of the time, Pallas kernels for 9%

profile of v6, /device:TPU:0, one launch (start us, length us, event | category | flops | bytes accessed | tf_op | source)
XLA Modules:
  0.0 78.6 jit_solution(2072583182417336406)
XLA Ops:
  0.6 1.9 %pack.1 = bf16[16,136,128]{2,1,0:T(8,128)(2,1)} custom-call(s32[1]{0:T(128)} %bitcast.rank_ref.refs_0_, s32[15,64]{1,0:T(8,128)} %bitcast.6, bf16[256,128]{1,0:T(8,128)(2,1)} %refs_4_.3, bf16[256,128]{1,0:T(8,128)(2,1)} %refs_5_.3, bf16[4,128]{1,0:T(4,128)(2,1)} %ck_ref.1, bf16[4,128]{1,0:T(4,128)(2,1)} %cv_ref.1), custom_call_target="tpu_custom_call" | custom-call | tf_op jit(solution)/shard_map/pack/pallas_call | solution.py:340
  2.6 0.0 copy-start
  2.6 0.0 copy-start.1
  2.6 0.0 copy-start.2
  2.6 0.0 copy-start.5
  2.6 7.5 %all-to-all-start = ((bf16[16,136,128]{2,1,0:T(8,128)(2,1)}), bf16[16,136,128]{2,1,0:T(8,128)(2,1)S(1)}, u32[]{:S(2)}, u32[]{:S(2)}) async-start(bf16[16,136,128]{2,1,0:T(8,128)(2,1)} %pack.1), calls=%async_computation | async-start | bytes 1114112 | tf_op jit(solution)/shard_map/all_to_all | solution.py:338
  10.1 2.6 %gate.1.refs_6_.gate_ref = f32[4,2,1024]{2,1,0:T(2,128)} custom-call(bf16[256,2560]{1,0:T(8,128)(2,1)} %x_ref.1, bf16[32,2560]{1,0:T(8,128)(2,1)} %bitcast.10), custom_call_target="tpu_custom_call" | custom-call | flops 41943040 | bytes 1310720 | tf_op jit(solution)/shard_map/gate/pallas_call | solution.py:350
  12.7 12.5 %all-to-all-done.refs_7_.refs_8_ = bf16[16,136,128]{2,1,0:T(8,128)(2,1)S(1)} async-done(((bf16[16,136,128]{2,1,0:T(8,128)(2,1)}), bf16[16,136,128]{2,1,0:T(8,128)(2,1)S(1)}, u32[]{:S(2)}, u32[]{:S(2)}) %all-to-all-start) | async-done | bytes 557088 | tf_op jit(solution)/shard_map/all_to_all | solution.py:338
  25.1 0.0 copy-done
  25.1 0.0 copy-done.1
  25.1 0.0 copy-done.2
  25.1 0.0 copy-done.5
  25.1 0.0 copy-start.3
  25.2 0.7 copy-done.3
  25.9 0.0 copy-start.6
  25.9 1.2 %copy-done.6 = bf16[256,2048]{1,0:T(8,128)(2,1)S(1)} copy-done((bf16[256,2048]{1,0:T(8,128)(2,1)S(1)}, bf16[256,2048]{1,0:T(8,128)(2,1)}, u32[]{:S(2)}) %copy-start.6) | copy-done | bytes 1048600
  27.1 6.2 %attend0.1 = (bf16[256,2048]{1,0:T(8,128)(2,1)}, f32[128,256]{1,0:T(8,128)S(1)}, f32[32,256]{1,0:T(8,128)S(1)}, f32[64,256]{1,0:T(8,128)S(1)}, bf16[16,128,128]{...) custom-call(s32[1]{0:T(128)} %bitcast.rank_ref.refs_0_, s32[15,64]{1,0:T(8,128)S(1)} %bitcast.7, ...), custom_call_target="tpu_custom_call" | custom-call | flops 1677721600 | bytes 4194304 | tf_op jit(solution)/shard_map/attend0/pallas_call | solution.py:417
  33.4 18.5 %all_to_all.15.picks_ref.refs_8_ = bf16[16,128,128]{2,1,0:T(8,128)(2,1)S(1)} all-to-all(bf16[16,128,128]{2,1,0:T(8,128)(2,1)S(1)} %get-tuple-element.21), channel_id=1, replica_groups=mesh['ctx'=16,'head'=2] {'ctx'}, dimensions={0} | all-to-all | bytes 1048576 | tf_op jit(solution)/shard_map/all_to_all | solution.py:338
  51.9 0.0 copy-start.8
  51.9 5.9 %attend1.1 = (f32[256,256]{1,0:T(8,128)S(1)}, f32[32,256]{1,0:T(8,128)S(1)}, f32[64,256]{1,0:T(8,128)S(1)}, bf16[16,136,128]{2,1,0:T(8,128)(2,1)}) custom-call(s32[1]{0:T(128)} %bitcast.rank_ref.refs_0_, s32[15,64]{1,0:T(8,128)S(1)} %bitcast.8, bf16[256,2048]{1,0:T(8,128)(2,1)S(1)} %copy-done.5, bf16[256,2048]{1,0:T(8,128)(2,1)S(1)} %copy-done.6, ...), custom_call_target="tpu_custom_call" | custom-call | flops 1677721600 | bytes 4194304 | tf_op jit(solution)/shard_map/attend1/pallas_call | solution.py:417
  57.8 0.0 copy-start.4
  57.8 4.2 %all-to-all-start.2 = ((bf16[16,136,128]{2,1,0:T(8,128)(2,1)}), bf16[16,136,128]{2,1,0:T(8,128)(2,1)S(1)}, u32[]{:S(2)}, u32[]{:S(2)}) async-start(bf16[16,136,128]{2,1,0:T(8,128)(2,1)} %get-tuple-element.28), calls=%async_computation.2 | async-start | bytes 1114112 | tf_op jit(solution)/shard_map/all_to_all | solution.py:338
  62.0 0.0 copy-done.8
  62.1 1.6 %collective-permute-start.1 = (bf16[1280,32]{0,1:T(8,128)(2,1)S(1)}, bf16[1280,32]{0,1:T(8,128)(2,1)S(1)}, u32[]{:S(2)}, u32[]{:S(2)}) collective-permute-start(bf16[1280,32]{0,1:T(8,128)(2,1)S(1)} %constant_dynamic-slice_fusion), channel_id=1, source_target_pairs={{0,1},{1,0},{2,3},{3,2},{4,5},{5,4},{6,7},{7,6},{8,9},{9,8},{10,11... | collective-permute-start | bytes 245768 | tf_op jit(solution)/shard_map/ppermute | solution.py:365
  63.7 0.0 copy-start.7
  63.7 0.5 collective-permute-start
  64.2 0.3 fusion.1
  64.5 0.0 copy-done.4
  64.5 0.4 copy-done.7
  64.9 4.8 %tail.1 = bf16[256,2048]{1,0:T(8,128)(2,1)} custom-call(s32[1]{0:T(128)} %bitcast.rank_ref.refs_0_, bf16[256,2048]{1,0:T(8,128)(2,1)S(1)} %copy-done.5, bf16[256,2048]{1,0:T(8,128)(2,1)S(1)} %copy-done.7, bf16[256,128]{1,0:T(8,128)(2,1)S(1)} %copy-done, bf16[256,128]{1,0:T(8,128)(2,1)S(1)} %copy-done.1, ...), custom_call_target="tpu_custom_call", output_to_operand_aliasing={{}: (8, {})} | custom-call | flops 1677721600 | bytes 4194304 | tf_op jit(solution)/shard_map/tail/pallas_call | solution.py:434
  69.7 0.0 collective-permute-done.1
  69.7 0.0 collective-permute-done
  69.7 1.2 %fusion = bf16[256,1280]{1,0:T(8,128)(2,1)} fusion(f32[256,1280]{1,0:T(8,128)S(1)} %fusion.1, bf16[32,256]{1,0:T(8,128)(2,1)S(1)} %collective-permute-done, bf16[1280,32]{0,1:T(8,128)(2,1)S(1)} %collective-permute-done.1), kind=kOutput, calls=%fused_computation.1 | convolution fusion | flops 21626880 | bytes 2064384 | tf_op jit(solution)/shard_map/dot_general | solution.py:464
  70.9 6.1 %all-to-all-done.2.home_ref = bf16[16,136,128]{2,1,0:T(8,128)(2,1)S(1)} async-done(((bf16[16,136,128]{2,1,0:T(8,128)(2,1)}), bf16[16,136,128]{2,1,0:T(8,128)(2,1)S(1)}, u32[]{:S(2)}, u32[]{:S(2)}) %all-to-all-start.2) | async-done | bytes 557088 | tf_op jit(solution)/shard_map/all_to_all | solution.py:338
  77.0 1.6 %finish.1 = (bf16[256,128]{1,0:T(8,128)(2,1)}, bf16[256,128]{1,0:T(8,128)(2,1)}, bf16[4,128]{1,0:T(4,128)(2,1)}, bf16[4,128]{1,0:T(4,128)(2,1)}) custom-call(s32[1]{0:T(128)} %bitcast.rank_ref.refs_0_, s32[15,64]{1,0:T(8,128)S(1)} %bitcast.9, f32[256,256]{1,0:T(8,128)S(1)} %get-tuple-element.26.part_ref, f32[64,256]{1,0:T(8,128)S(1)} %get-tuple-element.27.dc_ref, ...), custom_call_target="tpu_custom_call" | custom-call | tf_op jit(solution)/shard_map/finish/pallas_call | solution.py:447
  (2 shorter events, 0.0 us)
Async XLA Ops:
  2.6 22.6 %copy-start = (bf16[256,128]{1,0:T(8,128)(2,1)S(1)}, bf16[256,128]{1,0:T(8,128)(2,1)}, u32[]{:S(2)}) copy-start(bf16[256,128]{1,0:T(8,128)(2,1)} %refs_4_.3) | copy-start | bytes 196612
  2.6 22.6 %copy-start.1 = (bf16[256,128]{1,0:T(8,128)(2,1)S(1)}, bf16[256,128]{1,0:T(8,128)(2,1)}, u32[]{:S(2)}) copy-start(bf16[256,128]{1,0:T(8,128)(2,1)} %refs_5_.3) | copy-start | bytes 196612
  2.6 22.6 %copy-start.2 = (s32[64,15]{0,1:T(8,128)S(1)}, s32[64,15]{0,1:T(8,128)}, u32[]{:S(2)}) copy-start(s32[64,15]{0,1:T(8,128)} %param.14) | copy-start | bytes 11524
  2.6 22.6 %copy-start.5 = (bf16[256,2048]{1,0:T(8,128)(2,1)S(1)}, bf16[256,2048]{1,0:T(8,128)(2,1)}, u32[]{:S(2)}) copy-start(bf16[256,2048]{1,0:T(8,128)(2,1)} %refs_2_.3) | copy-start | bytes 3145732
  2.6 22.5 %all-to-all-start = ((bf16[16,136,128]{2,1,0:T(8,128)(2,1)}), bf16[16,136,128]{2,1,0:T(8,128)(2,1)S(1)}, u32[]{:S(2)}, u32[]{:S(2)}) async-start(bf16[16,136,128]{2,1,0:T(8,128)(2,1)} %pack.1), calls=%async_computation | async-start | bytes 1114112 | tf_op jit(solution)/shard_map/all_to_all | solution.py:338
  25.1 0.8 copy-start.3
  25.9 1.2 %copy-start.6 = (bf16[256,2048]{1,0:T(8,128)(2,1)S(1)}, bf16[256,2048]{1,0:T(8,128)(2,1)}, u32[]{:S(2)}) copy-start(bf16[256,2048]{1,0:T(8,128)(2,1)} %refs_3_.3) | copy-start | bytes 3145732
  51.9 10.2 %copy-start.8 = (bf16[2560,32]{0,1:T(8,128)(2,1)S(1)}, bf16[2560,32]{0,1:T(8,128)(2,1)}, u32[]{:S(2)}) copy-start(bf16[2560,32]{0,1:T(8,128)(2,1)} %param.16) | copy-start | bytes 491524
  57.8 6.8 %copy-start.4 = (f32[4,2,1024]{2,1,0:T(2,128)S(1)}, f32[4,2,1024]{2,1,0:T(2,128)}, u32[]{:S(2)}) copy-start(f32[4,2,1024]{2,1,0:T(2,128)} %gate.1.refs_6_.gate_ref) | copy-start | bytes 98308
  57.8 19.3 %all-to-all-start.2 = ((bf16[16,136,128]{2,1,0:T(8,128)(2,1)}), bf16[16,136,128]{2,1,0:T(8,128)(2,1)S(1)}, u32[]{:S(2)}, u32[]{:S(2)}) async-start(bf16[16,136,128]{2,1,0:T(8,128)(2,1)} %get-tuple-element.28), calls=%async_computation.2 | async-start | bytes 1114112 | tf_op jit(solution)/shard_map/all_to_all | solution.py:338
  62.1 7.6 %collective-permute-start.1 = (bf16[1280,32]{0,1:T(8,128)(2,1)S(1)}, bf16[1280,32]{0,1:T(8,128)(2,1)S(1)}, u32[]{:S(2)}, u32[]{:S(2)}) collective-permute-start(bf16[1280,32]{0,1:T(8,128)(2,1)S(1)} %constant_dynamic-slice_fusion), channel_id=1, source_target_pairs={{0,1},{1,0},{2,3},{3,2},{4,5},{5,4},{6,7},{7,6},{8,9},{9,8},{10,11... | collective-permute-start | bytes 245768 | tf_op jit(solution)/shard_map/ppermute | solution.py:365
  63.7 1.2 %copy-start.7 = (bf16[256,2048]{1,0:T(8,128)(2,1)S(1)}, bf16[256,2048]{1,0:T(8,128)(2,1)}, u32[]{:S(2)}) copy-start(bf16[256,2048]{1,0:T(8,128)(2,1)} %refs_3_.3) | copy-start | bytes 3145732
  63.7 6.0 %collective-permute-start = (bf16[32,256]{1,0:T(8,128)(2,1)S(1)}, bf16[32,256]{1,0:T(8,128)(2,1)S(1)}, u32[]{:S(2)}, u32[]{:S(2)}) collective-permute-start(bf16[32,256]{1,0:T(8,128)(2,1)S(1)} %convert_element_type.6), channel_id=1, source_target_pairs={{0,1},{1,0},{2,3},{3,2},{4,5},{5,4},{6,7},{7,6},{8,9},{9,8},{10,11... | collective-permute-start | bytes 49160 | tf_op jit(solution)/shard_map/ppermute | solution.py:460

commit v7 on v6

--- a/solution.py
+++ b/solution.py
@@ -439,7 +439,7 @@
         out_specs=pl.BlockSpec((BLK, width), lambda i: (2 + i, 0)),
         scratch_shapes=scratch,
         input_output_aliases={8: 0},
-        compiler_params=params(ranks),
+        compiler_params=params(ranks, 60),
         cost_estimate=cost,
         name="tail",
     )(me, queries, d_out, keys, values, gate, ckv, mixed, dq)

time: 79.2 us -> 79.1 us (level)
  Pallas kernels: 23 us -> 24.4 us
  waiting for transfers between devices: 18.6 us -> 17.6 us
    pallas_call x1, Pallas kernels: 4.8 us -> 6.2 us  [body(): pl.pallas_call(functools.partial(tail_kernel, ranks, qb, heads, lists), g...]
    all_to_all x2, waiting for transfers between devices: 18.6 us -> 17.6 us  [exchange(): return lax.all_to_all(x, 'ctx', split_axis=0, concat_axis=0, tiled=True)]
  transfers between devices with their start and end apart: 4 -> 4, of which waited for: 2 -> 2; matrix products, arithmetic and copies ran while one was open for 2% -> 2% of each run, Pallas kernels for 9% -> 11%
where the time goes in v7:
time: 79.1 us; the launch traced here: 78.5 us
  Pallas kernels  24.4 us (31%)
  blocking collectives  18.5 us (23%)
  waiting for transfers between devices  17.6 us (22%)
  starting transfers between devices  13.7 us (17%)
  local copies, waits for them, and re-layouts  2.02 us (3%)
  matrix products  1.54 us (2%)
    all_to_all x1, blocking collectives, exchange(): return lax.all_to_all(x, 'ctx', split_axis=0, concat_axis=0, tiled=True)  18.5 us
    all_to_all x2, waiting for transfers between devices, exchange(): return lax.all_to_all(x, 'ctx', split_axis=0, concat_axis=0, tiled=True)  17.6 us
    pallas_call x2, Pallas kernels, attend(): pl.pallas_call(functools.partial(attend_kernel, ranks, qb, heads, lists,...  12.1 us
    all_to_all x2, starting transfers between devices, exchange(): return lax.all_to_all(x, 'ctx', split_axis=0, concat_axis=0, tiled=True)  11.6 us
    pallas_call x1, Pallas kernels, body(): pl.pallas_call(functools.partial(tail_kernel, ranks, qb, heads, lists), g...  6.2 us
    pallas_call x1, Pallas kernels, body(): pl.pallas_call(functools.partial(gate_kernel, qb, heads), out_shape=jax.S...  2.56 us
    unnamed x18, local copies, waits for them, and re-layouts  2.01 us
    pallas_call x1, Pallas kernels, body(): pl.pallas_call(functools.partial(pack_kernel, ranks, qb, lists), out_shap...  1.93 us
  transfers between devices with their start and end apart: 4, of which 2 were waited for; matrix products, arithmetic and copies ran while one was open for 2% of the time, Pallas kernels for 11%

profile of v7, /device:TPU:0, one launch (start us, length us, event | category | flops | bytes accessed | tf_op | source)
XLA Modules:
  0.0 78.5 jit_solution(12497467492930287834)
XLA Ops:
  0.6 1.9 %pack.1 = bf16[16,136,128]{2,1,0:T(8,128)(2,1)} custom-call(s32[1]{0:T(128)} %bitcast.rank_ref.refs_0_, s32[15,64]{1,0:T(8,128)} %bitcast.6, bf16[256,128]{1,0:T(8,128)(2,1)} %refs_4_.3, bf16[256,128]{1,0:T(8,128)(2,1)} %refs_5_.3, bf16[4,128]{1,0:T(4,128)(2,1)} %ck_ref.1, bf16[4,128]{1,0:T(4,128)(2,1)} %cv_ref.1), custom_call_target="tpu_custom_call" | custom-call | tf_op jit(solution)/shard_map/pack/pallas_call | solution.py:340
  2.6 0.0 copy-start.1
  2.6 0.0 copy-start.2
  2.6 0.0 copy-start.3
  2.6 0.0 copy-start.5
  2.6 7.5 %all-to-all-start = ((bf16[16,136,128]{2,1,0:T(8,128)(2,1)}), bf16[16,136,128]{2,1,0:T(8,128)(2,1)S(1)}, u32[]{:S(2)}, u32[]{:S(2)}) async-start(bf16[16,136,128]{2,1,0:T(8,128)(2,1)} %pack.1), calls=%async_computation | async-start | bytes 1114112 | tf_op jit(solution)/shard_map/all_to_all | solution.py:338
  10.1 2.6 %gate.1.refs_6_.gate_ref = f32[4,2,1024]{2,1,0:T(2,128)} custom-call(bf16[256,2560]{1,0:T(8,128)(2,1)} %x_ref.1, bf16[32,2560]{1,0:T(8,128)(2,1)} %bitcast.10), custom_call_target="tpu_custom_call" | custom-call | flops 41943040 | bytes 1310720 | tf_op jit(solution)/shard_map/gate/pallas_call | solution.py:350
  12.7 12.5 %all-to-all-done.refs_7_.refs_8_ = bf16[16,136,128]{2,1,0:T(8,128)(2,1)S(1)} async-done(((bf16[16,136,128]{2,1,0:T(8,128)(2,1)}), bf16[16,136,128]{2,1,0:T(8,128)(2,1)S(1)}, u32[]{:S(2)}, u32[]{:S(2)}) %all-to-all-start) | async-done | bytes 557088 | tf_op jit(solution)/shard_map/all_to_all | solution.py:338
  25.1 0.0 copy-done.1
  25.1 0.0 copy-done.2
  25.1 0.0 copy-done.3
  25.1 0.0 copy-done.5
  25.1 0.0 copy-start.4
  25.2 0.7 copy-done.4
  25.9 0.0 copy-start.6
  25.9 1.2 %copy-done.6 = bf16[256,2048]{1,0:T(8,128)(2,1)S(1)} copy-done((bf16[256,2048]{1,0:T(8,128)(2,1)S(1)}, bf16[256,2048]{1,0:T(8,128)(2,1)}, u32[]{:S(2)}) %copy-start.6) | copy-done | bytes 1048600
  27.1 6.2 %attend0.1 = (bf16[256,2048]{1,0:T(8,128)(2,1)}, f32[128,256]{1,0:T(8,128)S(1)}, f32[32,256]{1,0:T(8,128)S(1)}, f32[64,256]{1,0:T(8,128)S(1)}, bf16[16,128,128]{...) custom-call(s32[1]{0:T(128)} %bitcast.rank_ref.refs_0_, s32[15,64]{1,0:T(8,128)S(1)} %bitcast.7, ...), custom_call_target="tpu_custom_call" | custom-call | flops 1677721600 | bytes 4194304 | tf_op jit(solution)/shard_map/attend0/pallas_call | solution.py:417
  33.4 0.0 copy-start.7
  33.4 18.5 %all_to_all.15.picks_ref.refs_8_ = bf16[16,128,128]{2,1,0:T(8,128)(2,1)S(1)} all-to-all(bf16[16,128,128]{2,1,0:T(8,128)(2,1)S(1)} %get-tuple-element.21), channel_id=1, replica_groups=mesh['ctx'=16,'head'=2] {'ctx'}, dimensions={0} | all-to-all | bytes 1048576 | tf_op jit(solution)/shard_map/all_to_all | solution.py:338
  51.9 0.0 copy-start
  51.9 0.0 copy-start.8
  51.9 5.9 %attend1.1 = (f32[256,256]{1,0:T(8,128)S(1)}, f32[32,256]{1,0:T(8,128)S(1)}, f32[64,256]{1,0:T(8,128)S(1)}, bf16[16,136,128]{2,1,0:T(8,128)(2,1)}) custom-call(s32[1]{0:T(128)} %bitcast.rank_ref.refs_0_, s32[15,64]{1,0:T(8,128)S(1)} %bitcast.8, bf16[256,2048]{1,0:T(8,128)(2,1)S(1)} %copy-done.5, bf16[256,2048]{1,0:T(8,128)(2,1)S(1)} %copy-done.6, ...), custom_call_target="tpu_custom_call" | custom-call | flops 1677721600 | bytes 4194304 | tf_op jit(solution)/shard_map/attend1/pallas_call | solution.py:417
  57.8 0.0 copy-done.7
  57.8 0.0 copy-done
  57.8 4.1 %all-to-all-start.2 = ((bf16[16,136,128]{2,1,0:T(8,128)(2,1)}), bf16[16,136,128]{2,1,0:T(8,128)(2,1)S(1)}, u32[]{:S(2)}, u32[]{:S(2)}) async-start(bf16[16,136,128]{2,1,0:T(8,128)(2,1)} %get-tuple-element.28), calls=%async_computation.2 | async-start | bytes 1114112 | tf_op jit(solution)/shard_map/all_to_all | solution.py:338
  61.9 0.0 copy-done.8
  61.9 1.6 %collective-permute-start.1 = (bf16[1280,32]{0,1:T(8,128)(2,1)S(1)}, bf16[1280,32]{0,1:T(8,128)(2,1)S(1)}, u32[]{:S(2)}, u32[]{:S(2)}) collective-permute-start(bf16[1280,32]{0,1:T(8,128)(2,1)S(1)} %constant_dynamic-slice_fusion), channel_id=1, source_target_pairs={{0,1},{1,0},{2,3},{3,2},{4,5},{5,4},{6,7},{7,6},{8,9},{9,8},{10,11... | collective-permute-start | bytes 245768 | tf_op jit(solution)/shard_map/ppermute | solution.py:365
  63.6 0.5 collective-permute-start
  64.1 0.3 fusion.1
  64.4 6.2 %tail.1 = bf16[256,2048]{1,0:T(8,128)(2,1)} custom-call(s32[1]{0:T(128)} %bitcast.rank_ref.refs_0_, bf16[256,2048]{1,0:T(8,128)(2,1)} %refs_2_.3, bf16[256,2048]{1,0:T(8,128)(2,1)} %refs_3_.3, bf16[256,128]{1,0:T(8,128)(2,1)} %refs_4_.3, bf16[256,128]{1,0:T(8,128)(2,1)} %refs_5_.3, ...), custom_call_target="tpu_custom_call", output_to_operand_aliasing={{}: (8, {})} | custom-call | flops 1677721600 | bytes 4194304 | tf_op jit(solution)/shard_map/tail/pallas_call | solution.py:434
  70.6 0.0 collective-permute-done.1
  70.6 0.0 collective-permute-done
  70.6 1.2 %fusion = bf16[256,1280]{1,0:T(8,128)(2,1)} fusion(f32[256,1280]{1,0:T(8,128)S(1)} %fusion.1, bf16[32,256]{1,0:T(8,128)(2,1)S(1)} %collective-permute-done, bf16[1280,32]{0,1:T(8,128)(2,1)S(1)} %collective-permute-done.1), kind=kOutput, calls=%fused_computation.1 | convolution fusion | flops 21626880 | bytes 2064384 | tf_op jit(solution)/shard_map/dot_general | solution.py:464
  71.8 5.1 %all-to-all-done.2.home_ref = bf16[16,136,128]{2,1,0:T(8,128)(2,1)S(1)} async-done(((bf16[16,136,128]{2,1,0:T(8,128)(2,1)}), bf16[16,136,128]{2,1,0:T(8,128)(2,1)S(1)}, u32[]{:S(2)}, u32[]{:S(2)}) %all-to-all-start.2) | async-done | bytes 557088 | tf_op jit(solution)/shard_map/all_to_all | solution.py:338
  76.9 1.6 %finish.1 = (bf16[256,128]{1,0:T(8,128)(2,1)}, bf16[256,128]{1,0:T(8,128)(2,1)}, bf16[4,128]{1,0:T(4,128)(2,1)}, bf16[4,128]{1,0:T(4,128)(2,1)}) custom-call(s32[1]{0:T(128)} %bitcast.rank_ref.refs_0_, s32[15,64]{1,0:T(8,128)S(1)} %bitcast.9, f32[256,256]{1,0:T(8,128)S(1)} %get-tuple-element.26.part_ref, f32[64,256]{1,0:T(8,128)S(1)} %get-tuple-element.27.dc_ref, ...), custom_call_target="tpu_custom_call" | custom-call | tf_op jit(solution)/shard_map/finish/pallas_call | solution.py:447
  (2 shorter events, 0.0 us)
Async XLA Ops:
  2.6 22.6 %copy-start.1 = (bf16[256,128]{1,0:T(8,128)(2,1)S(1)}, bf16[256,128]{1,0:T(8,128)(2,1)}, u32[]{:S(2)}) copy-start(bf16[256,128]{1,0:T(8,128)(2,1)} %refs_4_.3) | copy-start | bytes 196612
  2.6 22.6 %copy-start.2 = (bf16[256,128]{1,0:T(8,128)(2,1)S(1)}, bf16[256,128]{1,0:T(8,128)(2,1)}, u32[]{:S(2)}) copy-start(bf16[256,128]{1,0:T(8,128)(2,1)} %refs_5_.3) | copy-start | bytes 196612
  2.6 22.6 %copy-start.3 = (s32[64,15]{0,1:T(8,128)S(1)}, s32[64,15]{0,1:T(8,128)}, u32[]{:S(2)}) copy-start(s32[64,15]{0,1:T(8,128)} %param.14) | copy-start | bytes 11524
  2.6 22.6 %copy-start.5 = (bf16[256,2048]{1,0:T(8,128)(2,1)S(1)}, bf16[256,2048]{1,0:T(8,128)(2,1)}, u32[]{:S(2)}) copy-start(bf16[256,2048]{1,0:T(8,128)(2,1)} %refs_2_.3) | copy-start | bytes 3145732
  2.6 22.5 %all-to-all-start = ((bf16[16,136,128]{2,1,0:T(8,128)(2,1)}), bf16[16,136,128]{2,1,0:T(8,128)(2,1)S(1)}, u32[]{:S(2)}, u32[]{:S(2)}) async-start(bf16[16,136,128]{2,1,0:T(8,128)(2,1)} %pack.1), calls=%async_computation | async-start | bytes 1114112 | tf_op jit(solution)/shard_map/all_to_all | solution.py:338
  25.1 0.8 copy-start.4
  25.9 1.2 %copy-start.6 = (bf16[256,2048]{1,0:T(8,128)(2,1)S(1)}, bf16[256,2048]{1,0:T(8,128)(2,1)}, u32[]{:S(2)}) copy-start(bf16[256,2048]{1,0:T(8,128)(2,1)} %refs_3_.3) | copy-start | bytes 3145732
  33.4 24.4 %copy-start.7 = (bf16[64,256]{1,0:T(8,128)(2,1)}, bf16[64,256]{1,0:T(8,128)(2,1)S(1)}, u32[]{:S(2)}) copy-start(bf16[64,256]{1,0:T(8,128)(2,1)S(1)} %get-tuple-element.20.ckv_ref.refs_7_) | copy-start | bytes 98308
  51.9 5.9 %copy-start = (bf16[16,128,128]{2,1,0:T(8,128)(2,1)}, bf16[16,128,128]{2,1,0:T(8,128)(2,1)S(1)}, u32[]{:S(2)}) copy-start(bf16[16,128,128]{2,1,0:T(8,128)(2,1)S(1)} %all_to_all.15.picks_ref.refs_8_) | copy-start | bytes 1572868
  51.9 10.0 %copy-start.8 = (bf16[2560,32]{0,1:T(8,128)(2,1)S(1)}, bf16[2560,32]{0,1:T(8,128)(2,1)}, u32[]{:S(2)}) copy-start(bf16[2560,32]{0,1:T(8,128)(2,1)} %param.16) | copy-start | bytes 491524
  57.8 19.1 %all-to-all-start.2 = ((bf16[16,136,128]{2,1,0:T(8,128)(2,1)}), bf16[16,136,128]{2,1,0:T(8,128)(2,1)S(1)}, u32[]{:S(2)}, u32[]{:S(2)}) async-start(bf16[16,136,128]{2,1,0:T(8,128)(2,1)} %get-tuple-element.28), calls=%async_computation.2 | async-start | bytes 1114112 | tf_op jit(solution)/shard_map/all_to_all | solution.py:338
  61.9 8.7 %collective-permute-start.1 = (bf16[1280,32]{0,1:T(8,128)(2,1)S(1)}, bf16[1280,32]{0,1:T(8,128)(2,1)S(1)}, u32[]{:S(2)}, u32[]{:S(2)}) collective-permute-start(bf16[1280,32]{0,1:T(8,128)(2,1)S(1)} %constant_dynamic-slice_fusion), channel_id=1, source_target_pairs={{0,1},{1,0},{2,3},{3,2},{4,5},{5,4},{6,7},{7,6},{8,9},{9,8},{10,11... | collective-permute-start | bytes 245768 | tf_op jit(solution)/shard_map/ppermute | solution.py:365
  63.6 7.1 %collective-permute-start = (bf16[32,256]{1,0:T(8,128)(2,1)S(1)}, bf16[32,256]{1,0:T(8,128)(2,1)S(1)}, u32[]{:S(2)}, u32[]{:S(2)}) collective-permute-start(bf16[32,256]{1,0:T(8,128)(2,1)S(1)} %convert_element_type.6), channel_id=1, source_target_pairs={{0,1},{1,0},{2,3},{3,2},{4,5},{5,4},{6,7},{7,6},{8,9},{9,8},{10,11... | collective-permute-start | bytes 49160 | tf_op jit(solution)/shard_map/ppermute | solution.py:460

commit v8 on v7

--- a/solution.py
+++ b/solution.py
@@ -113,10 +113,10 @@
 def attend_kernel(ranks, qb, heads, lists, p, *refs):
     (rank_ref, sel_ref, q_ref, do_ref, k_ref, v_ref, gate_ref, comp_ref, picks_ref) = refs[:9]
     if p == 0:
-        dq_ref, own_ref, dz_ref, dc_ref, send_ref, ckv_ref, *scratch = refs[9:]
+        dq_ref, own_ref, dz_ref, dc_ref, send_ref, *scratch = refs[9:]
     else:
         dz_in, dc_in, own_in, own_ref, dz_ref, dc_ref, send_ref, *scratch = refs[9:]
-        dq_ref, ckv_ref = None, None
+        dq_ref = None
     hd = k_ref.shape[1]
     me = rank_ref[0]
     step = pl.program_id(0)
@@ -141,7 +141,7 @@
         @pl.when(step == parity)
         def _(parity=parity):
             attend_row(ranks, qb, heads, lists[parity], me, 2 * p + parity, parity, q_ref, do_ref, k_ref, v_ref,
-                       gate_ref, comp_ref, picks_ref, dq_ref, own_ref, send_ref, ckv_ref, *scratch)
+                       gate_ref, comp_ref, picks_ref, dq_ref, own_ref, send_ref, *scratch)
 
     @pl.when(step == 1)
     def _():
@@ -165,7 +165,7 @@
                     ]
 
 
-def tail_kernel(ranks, qb, heads, lists, rank_ref, q_ref, do_ref, k_ref, v_ref, gate_ref, ckv_ref,
+def tail_kernel(ranks, qb, heads, lists, rank_ref, q_ref, do_ref, k_ref, v_ref, gate_ref, comp_ref,
                 picks_ref, _, dq_ref, *scratch):
     me = rank_ref[0]
     step = pl.program_id(0)
@@ -174,11 +174,11 @@
         @pl.when(step == parity)
         def _(parity=parity):
             attend_row(ranks, qb, heads, lists[parity], me, 2 + parity, parity, q_ref, do_ref, k_ref, v_ref,
-                       gate_ref, ckv_ref, picks_ref, dq_ref, None, None, None, *scratch)
+                       gate_ref, comp_ref, picks_ref, dq_ref, None, None, *scratch)
 
 
 def attend_row(ranks, qb, heads, reach, me, row, parity, q_ref, do_ref, k_ref, v_ref, gate_ref,
-               comp_ref, picks_ref, dq_ref, own_ref, send_ref, ckv_ref, kcat, vcat, kt, qs, ds,
+               comp_ref, picks_ref, dq_ref, own_ref, send_ref, kcat, vcat, kt, qs, ds,
                s_scr, u_scr, w_scr, d_scr, dv_acc, dk_acc, dg_scr, dc_scr):
     npick = len(reach)
     hd = k_ref.shape[1]
@@ -188,17 +188,11 @@
     per = LANES // BLK
     scale = hd ** -0.5
 
-    if len(comp_ref.shape) == 3:
-        pieces = []
-        for r in range(ranks):
-            pieces.append(comp_ref[jnp.maximum(me - r, 0)].astype(F32))
-        kcat[nsel:nk, :] = jnp.concatenate([x[:qb] for x in pieces], axis=0).astype(BF16)
-        vcat[nsel:nk, :] = jnp.concatenate([x[qb:] for x in pieces], axis=0).astype(BF16)
-        ckv_ref[:, :hd] = kcat[nsel:nk, :]
-        ckv_ref[:, hd:] = vcat[nsel:nk, :]
-    else:
-        kcat[nsel:nk, :] = comp_ref[:, :hd]
-        vcat[nsel:nk, :] = comp_ref[:, hd:]
+    pieces = []
+    for r in range(ranks):
+        pieces.append(comp_ref[jnp.maximum(me - r, 0)].astype(F32))
+    kcat[nsel:nk, :] = jnp.concatenate([x[:qb] for x in pieces], axis=0).astype(BF16)
+    vcat[nsel:nk, :] = jnp.concatenate([x[qb:] for x in pieces], axis=0).astype(BF16)
     kcat[:BLK, :] = k_ref[row * BLK : (row + 1) * BLK, :]
     vcat[:BLK, :] = v_ref[row * BLK : (row + 1) * BLK, :]
     for n, (_, r) in enumerate(reach):
@@ -395,10 +389,10 @@
         flops=10 * nk * heads * 2 * BLK * hd, bytes_accessed=4 << 20, transcendentals=0
     )
     pick_spec = pl.BlockSpec((ranks, 2 * BLK, hd), lambda i: (0, 0, 0))
-
-    def attend(p, comp, picks, previous):
+    comp_spec = pl.BlockSpec((ranks, 2 * qb, hd), lambda i: (0, 2 * BLK // (2 * qb), 0))
+
+    def attend(p, picks, previous):
         out_slot = slot if p else 2 * BLK
-        comp_spec = in_vmem()
         out_shape = [
             jax.ShapeDtypeStruct((tokens if p else 2 * BLK, 2 * hd), F32),
             jax.ShapeDtypeStruct((2 * heads, tokens), F32),
@@ -407,13 +401,8 @@
         ]
         out_specs = [in_vmem()] * 4
         if p == 0:
-            comp_spec = pl.BlockSpec((ranks, 2 * qb, hd), lambda i: (0, 2 * BLK // (2 * qb), 0))
-            out_shape = (
-                [jax.ShapeDtypeStruct(queries.shape, BF16)]
-                + out_shape
-                + [jax.ShapeDtypeStruct((nblocks, 2 * hd), BF16)]
-            )
-            out_specs = [pl.BlockSpec((BLK, width), lambda i: (i, 0))] + out_specs + [in_vmem()]
+            out_shape = [jax.ShapeDtypeStruct(queries.shape, BF16)] + out_shape
+            out_specs = [pl.BlockSpec((BLK, width), lambda i: (i, 0))] + out_specs
         return pl.pallas_call(
             functools.partial(attend_kernel, ranks, qb, heads, lists, p),
             grid=(2,),
@@ -425,24 +414,24 @@
             compiler_params=params(ranks),
             cost_estimate=cost,
             name=f"attend{p}",
-        )(me, table, queries, d_out, keys, values, gate, comp, picks, *previous)
-
-    dq, own0, dz, dc, send, ckv = attend(0, fetched, fetched, [])
+        )(me, table, queries, d_out, keys, values, gate, fetched, picks, *previous)
+
+    dq, own0, dz, dc, send = attend(0, fetched, [])
     mixed = exchange(send)
-    part, dz, dc, send = attend(1, ckv, mixed, [dz, dc, own0])
+    part, dz, dc, send = attend(1, mixed, [dz, dc, own0])
     home = exchange(send)
     d_queries = pl.pallas_call(
         functools.partial(tail_kernel, ranks, qb, heads, lists),
         grid=(2,),
         out_shape=jax.ShapeDtypeStruct(queries.shape, BF16),
-        in_specs=[in_smem()] + row_specs(1) + [in_vmem(), pick_spec, pl.BlockSpec(memory_space=pl.ANY)],
+        in_specs=[in_smem()] + row_specs(1) + [comp_spec, pick_spec, pl.BlockSpec(memory_space=pl.ANY)],
         out_specs=pl.BlockSpec((BLK, width), lambda i: (2 + i, 0)),
         scratch_shapes=scratch,
         input_output_aliases={8: 0},
         compiler_params=params(ranks, 60),
         cost_estimate=cost,
         name="tail",
-    )(me, queries, d_out, keys, values, gate, ckv, mixed, dq)
+    )(me, queries, d_out, keys, values, gate, fetched, mixed, dq)
 
     d_keys, d_values, d_ck, d_cv = pl.pallas_call(
         functools.partial(finish_kernel, ranks, qb, lists),

time: 79.1 us -> 79.1 us (level)
  no operation moved by 1% of the time
where the time goes in v8:
time: 79.1 us; the launch traced here: 78.5 us
  Pallas kernels  24.4 us (31%)
  blocking collectives  18.5 us (23%)
  waiting for transfers between devices  17.6 us (22%)
  starting transfers between devices  13.7 us (17%)
  local copies, waits for them, and re-layouts  2.02 us (3%)
  matrix products  1.54 us (2%)
    all_to_all x1, blocking collectives, exchange(): return lax.all_to_all(x, 'ctx', split_axis=0, concat_axis=0, tiled=True)  18.5 us
    all_to_all x2, waiting for transfers between devices, exchange(): return lax.all_to_all(x, 'ctx', split_axis=0, concat_axis=0, tiled=True)  17.6 us
    pallas_call x2, Pallas kernels, attend(): pl.pallas_call(functools.partial(attend_kernel, ranks, qb, heads, lists,...  12.2 us
    all_to_all x2, starting transfers between devices, exchange(): return lax.all_to_all(x, 'ctx', split_axis=0, concat_axis=0, tiled=True)  11.6 us
    pallas_call x1, Pallas kernels, body(): pl.pallas_call(functools.partial(tail_kernel, ranks, qb, heads, lists), g...  6.19 us
    pallas_call x1, Pallas kernels, body(): pl.pallas_call(functools.partial(gate_kernel, qb, heads), out_shape=jax.S...  2.56 us
    unnamed x18, local copies, waits for them, and re-layouts  2.01 us
    pallas_call x1, Pallas kernels, body(): pl.pallas_call(functools.partial(pack_kernel, ranks, qb, lists), out_shap...  1.93 us
  transfers between devices with their start and end apart: 4, of which 2 were waited for; matrix products, arithmetic and copies ran while one was open for 2% of the time, Pallas kernels for 11%

profile of v8, /device:TPU:0, one launch (start us, length us, event | category | flops | bytes accessed | tf_op | source)
XLA Modules:
  0.0 78.5 jit_solution(12427062916822394868)
XLA Ops:
  0.6 1.9 %pack.1 = bf16[16,136,128]{2,1,0:T(8,128)(2,1)} custom-call(s32[1]{0:T(128)} %bitcast.rank_ref.refs_0_, s32[15,64]{1,0:T(8,128)} %bitcast.6, bf16[256,128]{1,0:T(8,128)(2,1)} %refs_4_.3, bf16[256,128]{1,0:T(8,128)(2,1)} %refs_5_.3, bf16[4,128]{1,0:T(4,128)(2,1)} %ck_ref.1, bf16[4,128]{1,0:T(4,128)(2,1)} %cv_ref.1), custom_call_target="tpu_custom_call" | custom-call | tf_op jit(solution)/shard_map/pack/pallas_call | solution.py:334
  2.6 0.0 copy-start.2
  2.6 0.0 copy-start.3
  2.6 0.0 copy-start.4
  2.6 0.0 copy-start.6
  2.6 7.5 %all-to-all-start = ((bf16[16,136,128]{2,1,0:T(8,128)(2,1)}), bf16[16,136,128]{2,1,0:T(8,128)(2,1)S(1)}, u32[]{:S(2)}, u32[]{:S(2)}) async-start(bf16[16,136,128]{2,1,0:T(8,128)(2,1)} %pack.1), calls=%async_computation | async-start | bytes 1114112 | tf_op jit(solution)/shard_map/all_to_all | solution.py:332
  10.1 2.6 %gate.1.refs_6_.gate_ref = f32[4,2,1024]{2,1,0:T(2,128)} custom-call(bf16[256,2560]{1,0:T(8,128)(2,1)} %x_ref.1, bf16[32,2560]{1,0:T(8,128)(2,1)} %bitcast.10), custom_call_target="tpu_custom_call" | custom-call | flops 41943040 | bytes 1310720 | tf_op jit(solution)/shard_map/gate/pallas_call | solution.py:344
  12.7 12.5 %all-to-all-done.refs_7_.refs_8_.comp_ref = bf16[16,136,128]{2,1,0:T(8,128)(2,1)S(1)} async-done(((bf16[16,136,128]{2,1,0:T(8,128)(2,1)}), bf16[16,136,128]{2,1,0:T(8,128)(2,1)S(1)}, u32[]{:S(2)}, u32[]{:S(2)}) %all-to-all-start) | async-done | bytes 557088 | tf_op jit(solution)/shard_map/all_to_all | solution.py:332
  25.1 0.0 copy-done.2
  25.1 0.0 copy-done.3
  25.1 0.0 copy-done.4
  25.1 0.0 copy-done.6
  25.1 0.0 copy-start.5
  25.2 0.7 copy-done.5
  25.9 0.0 copy-start.7
  25.9 1.2 %copy-done.7 = bf16[256,2048]{1,0:T(8,128)(2,1)S(1)} copy-done((bf16[256,2048]{1,0:T(8,128)(2,1)S(1)}, bf16[256,2048]{1,0:T(8,128)(2,1)}, u32[]{:S(2)}) %copy-start.7) | copy-done | bytes 1048600
  27.1 0.0 copy-start
  27.1 6.2 %attend0.1 = (bf16[256,2048]{1,0:T(8,128)(2,1)}, f32[128,256]{1,0:T(8,128)S(1)}, f32[32,256]{1,0:T(8,128)S(1)}, f32[64,256]{1,0:T(8,128)S(1)}, bf16[16,128,128]{2,1,0:T(8,128)(2,1)S(1)}) custom-call(s32[1]{0:T(128)} %bitcast.rank_ref.refs_0_, s32[15,64]{1,0:T(8,128)S(1)} %bitcast.7, bf16[256,2048]{1,0:T(8,128)(2,1)S(1)} %copy-done.6, ...), custom_call_target="tpu_custom_call" | custom-call | flops 1677721600 | bytes 4194304 | tf_op jit(solution)/shard_map/attend0/pallas_call | solution.py:406
  33.4 18.5 %all_to_all.15.picks_ref.refs_8_ = bf16[16,128,128]{2,1,0:T(8,128)(2,1)S(1)} all-to-all(bf16[16,128,128]{2,1,0:T(8,128)(2,1)S(1)} %get-tuple-element.19), channel_id=1, replica_groups=mesh['ctx'=16,'head'=2] {'ctx'}, dimensions={0} | all-to-all | bytes 1048576 | tf_op jit(solution)/shard_map/all_to_all | solution.py:332
  51.9 0.0 copy-start.1
  51.9 0.0 copy-done
  51.9 0.0 copy-start.8
  51.9 5.9 %attend1.1 = (f32[256,256]{1,0:T(8,128)S(1)}, f32[32,256]{1,0:T(8,128)S(1)}, f32[64,256]{1,0:T(8,128)S(1)}, bf16[16,136,128]{2,1,0:T(8,128)(2,1)}) custom-call(s32[1]{0:T(128)} %bitcast.rank_ref.refs_0_, s32[15,64]{1,0:T(8,128)S(1)} %bitcast.8, bf16[256,2048]{1,0:T(8,128)(2,1)S(1)} %copy-done.6, bf16[256,2048]{1,0:T(8,128)(2,1)S(1)} %copy-done.7, ...), custom_call_target="tpu_custom_call" | custom-call | flops 1677721600 | bytes 4194304 | tf_op jit(solution)/shard_map/attend1/pallas_call | solution.py:406
  57.8 0.0 copy-done.1
  57.8 4.1 %all-to-all-start.2 = ((bf16[16,136,128]{2,1,0:T(8,128)(2,1)}), bf16[16,136,128]{2,1,0:T(8,128)(2,1)S(1)}, u32[]{:S(2)}, u32[]{:S(2)}) async-start(bf16[16,136,128]{2,1,0:T(8,128)(2,1)} %get-tuple-element.26), calls=%async_computation.2 | async-start | bytes 1114112 | tf_op jit(solution)/shard_map/all_to_all | solution.py:332
  61.9 0.0 copy-done.8
  62.0 1.6 %collective-permute-start.1 = (bf16[1280,32]{0,1:T(8,128)(2,1)S(1)}, bf16[1280,32]{0,1:T(8,128)(2,1)S(1)}, u32[]{:S(2)}, u32[]{:S(2)}) collective-permute-start(bf16[1280,32]{0,1:T(8,128)(2,1)S(1)} %constant_dynamic-slice_fusion), channel_id=1, source_target_pairs={{0,1},{1,0},{2,3},{3,2},{4,5},{5,4},{6,7},{7,6},{8,9},{9,8},{10,11... | collective-permute-start | bytes 245768 | tf_op jit(solution)/shard_map/ppermute | solution.py:359
  63.6 0.5 collective-permute-start
  64.1 0.3 fusion.1
  64.4 6.2 %tail.1 = bf16[256,2048]{1,0:T(8,128)(2,1)} custom-call(s32[1]{0:T(128)} %bitcast.rank_ref.refs_0_, bf16[256,2048]{1,0:T(8,128)(2,1)} %refs_2_.3, bf16[256,2048]{1,0:T(8,128)(2,1)} %refs_3_.3, bf16[256,128]{1,0:T(8,128)(2,1)} %refs_4_.3, bf16[256,128]{1,0:T(8,128)(2,1)} %refs_5_.3, ...), custom_call_target="tpu_custom_call", output_to_operand_aliasing={{}: (8, {})} | custom-call | flops 1677721600 | bytes 4194304 | tf_op jit(solution)/shard_map/tail/pallas_call | solution.py:423
  70.6 0.0 collective-permute-done.1
  70.6 0.0 collective-permute-done
  70.6 1.2 %fusion = bf16[256,1280]{1,0:T(8,128)(2,1)} fusion(f32[256,1280]{1,0:T(8,128)S(1)} %fusion.1, bf16[32,256]{1,0:T(8,128)(2,1)S(1)} %collective-permute-done, bf16[1280,32]{0,1:T(8,128)(2,1)S(1)} %collective-permute-done.1), kind=kOutput, calls=%fused_computation.1 | convolution fusion | flops 21626880 | bytes 2064384 | tf_op jit(solution)/shard_map/dot_general | solution.py:453
  71.8 5.1 %all-to-all-done.2.home_ref = bf16[16,136,128]{2,1,0:T(8,128)(2,1)S(1)} async-done(((bf16[16,136,128]{2,1,0:T(8,128)(2,1)}), bf16[16,136,128]{2,1,0:T(8,128)(2,1)S(1)}, u32[]{:S(2)}, u32[]{:S(2)}) %all-to-all-start.2) | async-done | bytes 557088 | tf_op jit(solution)/shard_map/all_to_all | solution.py:332
  76.9 1.6 %finish.1 = (bf16[256,128]{1,0:T(8,128)(2,1)}, bf16[256,128]{1,0:T(8,128)(2,1)}, bf16[4,128]{1,0:T(4,128)(2,1)}, bf16[4,128]{1,0:T(4,128)(2,1)}) custom-call(s32[1]{0:T(128)} %bitcast.rank_ref.refs_0_, s32[15,64]{1,0:T(8,128)S(1)} %bitcast.9, f32[256,256]{1,0:T(8,128)S(1)} %get-tuple-element.24.part_ref, f32[64,256]{1,0:T(8,128)S(1)} %get-tuple-element.25.dc_ref, ...), custom_call_target="tpu_custom_call" | custom-call | tf_op jit(solution)/shard_map/finish/pallas_call | solution.py:436
  (2 shorter events, 0.0 us)
Async XLA Ops:
  2.6 22.6 %copy-start.2 = (bf16[256,128]{1,0:T(8,128)(2,1)S(1)}, bf16[256,128]{1,0:T(8,128)(2,1)}, u32[]{:S(2)}) copy-start(bf16[256,128]{1,0:T(8,128)(2,1)} %refs_4_.3) | copy-start | bytes 196612
  2.6 22.6 %copy-start.3 = (bf16[256,128]{1,0:T(8,128)(2,1)S(1)}, bf16[256,128]{1,0:T(8,128)(2,1)}, u32[]{:S(2)}) copy-start(bf16[256,128]{1,0:T(8,128)(2,1)} %refs_5_.3) | copy-start | bytes 196612
  2.6 22.6 %copy-start.4 = (s32[64,15]{0,1:T(8,128)S(1)}, s32[64,15]{0,1:T(8,128)}, u32[]{:S(2)}) copy-start(s32[64,15]{0,1:T(8,128)} %param.14) | copy-start | bytes 11524
  2.6 22.6 %copy-start.6 = (bf16[256,2048]{1,0:T(8,128)(2,1)S(1)}, bf16[256,2048]{1,0:T(8,128)(2,1)}, u32[]{:S(2)}) copy-start(bf16[256,2048]{1,0:T(8,128)(2,1)} %refs_2_.3) | copy-start | bytes 3145732
  2.6 22.5 %all-to-all-start = ((bf16[16,136,128]{2,1,0:T(8,128)(2,1)}), bf16[16,136,128]{2,1,0:T(8,128)(2,1)S(1)}, u32[]{:S(2)}, u32[]{:S(2)}) async-start(bf16[16,136,128]{2,1,0:T(8,128)(2,1)} %pack.1), calls=%async_computation | async-start | bytes 1114112 | tf_op jit(solution)/shard_map/all_to_all | solution.py:332
  25.1 0.8 copy-start.5
  25.9 1.2 %copy-start.7 = (bf16[256,2048]{1,0:T(8,128)(2,1)S(1)}, bf16[256,2048]{1,0:T(8,128)(2,1)}, u32[]{:S(2)}) copy-start(bf16[256,2048]{1,0:T(8,128)(2,1)} %refs_3_.3) | copy-start | bytes 3145732
  27.1 24.7 %copy-start = (bf16[16,136,128]{2,1,0:T(8,128)(2,1)}, bf16[16,136,128]{2,1,0:T(8,128)(2,1)S(1)}, u32[]{:S(2)}) copy-start(bf16[16,136,128]{2,1,0:T(8,128)(2,1)S(1)} %all-to-all-done.refs_7_.refs_8_.comp_ref) | copy-start | bytes 1671172
  51.9 5.9 %copy-start.1 = (bf16[16,128,128]{2,1,0:T(8,128)(2,1)}, bf16[16,128,128]{2,1,0:T(8,128)(2,1)S(1)}, u32[]{:S(2)}) copy-start(bf16[16,128,128]{2,1,0:T(8,128)(2,1)S(1)} %all_to_all.15.picks_ref.refs_8_) | copy-start | bytes 1572868
  51.9 10.1 %copy-start.8 = (bf16[2560,32]{0,1:T(8,128)(2,1)S(1)}, bf16[2560,32]{0,1:T(8,128)(2,1)}, u32[]{:S(2)}) copy-start(bf16[2560,32]{0,1:T(8,128)(2,1)} %param.16) | copy-start | bytes 491524
  57.8 19.1 %all-to-all-start.2 = ((bf16[16,136,128]{2,1,0:T(8,128)(2,1)}), bf16[16,136,128]{2,1,0:T(8,128)(2,1)S(1)}, u32[]{:S(2)}, u32[]{:S(2)}) async-start(bf16[16,136,128]{2,1,0:T(8,128)(2,1)} %get-tuple-element.26), calls=%async_computation.2 | async-start | bytes 1114112 | tf_op jit(solution)/shard_map/all_to_all | solution.py:332
  62.0 8.7 %collective-permute-start.1 = (bf16[1280,32]{0,1:T(8,128)(2,1)S(1)}, bf16[1280,32]{0,1:T(8,128)(2,1)S(1)}, u32[]{:S(2)}, u32[]{:S(2)}) collective-permute-start(bf16[1280,32]{0,1:T(8,128)(2,1)S(1)} %constant_dynamic-slice_fusion), channel_id=1, source_target_pairs={{0,1},{1,0},{2,3},{3,2},{4,5},{5,4},{6,7},{7,6},{8,9},{9,8},{10,11... | collective-permute-start | bytes 245768 | tf_op jit(solution)/shard_map/ppermute | solution.py:359
  63.6 7.1 %collective-permute-start = (bf16[32,256]{1,0:T(8,128)(2,1)S(1)}, bf16[32,256]{1,0:T(8,128)(2,1)S(1)}, u32[]{:S(2)}, u32[]{:S(2)}) collective-permute-start(bf16[32,256]{1,0:T(8,128)(2,1)S(1)} %convert_element_type.6), channel_id=1, source_target_pairs={{0,1},{1,0},{2,3},{3,2},{4,5},{5,4},{6,7},{7,6},{8,9},{9,8},{10,11... | collective-permute-start | bytes 49160 | tf_op jit(solution)/shard_map/ppermute | solution.py:449

commit v9 on v7

--- a/solution.py
+++ b/solution.py
@@ -352,7 +352,7 @@
         out_shape=jax.ShapeDtypeStruct((qb, 2, heads * BLK), F32),
         in_specs=[in_vmem()] * 2,
         out_specs=in_vmem(),
-        compiler_params=params(ranks, 60),
+        compiler_params=params(ranks),
         cost_estimate=pl.CostEstimate(
             flops=2 * inputs.size * w_gate.shape[1], bytes_accessed=2 * inputs.size, transcendentals=0
         ),

time: 79.1 us -> 78.3 us (0.990)
  Pallas kernels: 24.4 us -> 22.5 us
  waiting for transfers between devices: 17.6 us -> 19.5 us
    pallas_call x1, Pallas kernels: 2.56 us -> 0.62 us  [body(): pl.pallas_call(functools.partial(gate_kernel, qb, heads), out_shape=jax.S...]
    all_to_all x2, waiting for transfers between devices: 17.6 us -> 19.5 us  [exchange(): return lax.all_to_all(x, 'ctx', split_axis=0, concat_axis=0, tiled=True)]
    unnamed x18 -> x20, local copies, waits for them, and re-layouts: 2.01 us -> 1.26 us
  transfers between devices with their start and end apart: 4 -> 4, of which waited for: 2 -> 2; matrix products, arithmetic and copies ran while one was open for 2% -> 2% of each run, Pallas kernels for 11% -> 9%
where the time goes in v9:
time: 78.3 us; the launch traced here: 77.8 us
  Pallas kernels  22.5 us (29%)
  waiting for transfers between devices  19.5 us (25%)
  blocking collectives  18.5 us (24%)
  starting transfers between devices  13.7 us (17%)
  matrix products  1.54 us (2%)
  local copies, waits for them, and re-layouts  1.27 us (2%)
    all_to_all x2, waiting for transfers between devices, exchange(): return lax.all_to_all(x, 'ctx', split_axis=0, concat_axis=0, tiled=True)  19.5 us
    all_to_all x1, blocking collectives, exchange(): return lax.all_to_all(x, 'ctx', split_axis=0, concat_axis=0, tiled=True)  18.5 us
    pallas_call x2, Pallas kernels, attend(): pl.pallas_call(functools.partial(attend_kernel, ranks, qb, heads, lists,...  12.1 us
    all_to_all x2, starting transfers between devices, exchange(): return lax.all_to_all(x, 'ctx', split_axis=0, concat_axis=0, tiled=True)  11.6 us
    pallas_call x1, Pallas kernels, body(): pl.pallas_call(functools.partial(tail_kernel, ranks, qb, heads, lists), g...  6.2 us
    pallas_call x1, Pallas kernels, body(): pl.pallas_call(functools.partial(pack_kernel, ranks, qb, lists), out_shap...  2 us
    ppermute x1, starting transfers between devices, body(): w_other = lax.ppermute(w_send, 'head', swap)  1.61 us
  transfers between devices with their start and end apart: 4, of which 2 were waited for; matrix products, arithmetic and copies ran while one was open for 2% of the time, Pallas kernels for 9%

profile of v9, /device:TPU:0, one launch (start us, length us, event | category | flops | bytes accessed | tf_op | source)
XLA Modules:
  0.0 77.8 jit_solution(3486321034052662439)
XLA Ops:
  0.6 0.0 copy-start.1
  0.6 0.0 copy-start
  0.7 2.0 %pack.1 = bf16[16,136,128]{2,1,0:T(8,128)(2,1)} custom-call(s32[1]{0:T(128)} %bitcast.rank_ref.refs_0_, s32[15,64]{1,0:T(8,128)} %bitcast.7, bf16[256,128]{1,0:T(8,128)(2,1)} %refs_4_.3, bf16[256,128]{1,0:T(8,128)(2,1)} %refs_5_.3, bf16[4,128]{1,0:T(4,128)(2,1)} %ck_ref.1, bf16[4,128]{1,0:T(4,128)(2,1)} %cv_ref.1), custom_call_target="tpu_custom_call" | custom-call | tf_op jit(solution)/shard_map/pack/pallas_call | solution.py:340
  2.7 0.0 copy-start.3
  2.7 0.0 copy-start.4
  2.7 0.0 copy-start.5
  2.7 0.0 copy-start.7
  2.7 7.5 %all-to-all-start = ((bf16[16,136,128]{2,1,0:T(8,128)(2,1)}), bf16[16,136,128]{2,1,0:T(8,128)(2,1)S(1)}, u32[]{:S(2)}, u32[]{:S(2)}) async-start(bf16[16,136,128]{2,1,0:T(8,128)(2,1)} %pack.1), calls=%async_computation | async-start | bytes 1114112 | tf_op jit(solution)/shard_map/all_to_all | solution.py:338
  10.2 0.0 copy-done.1
  10.2 0.0 copy-done
  10.2 0.6 gate.1.refs_6_.gate_ref
  10.8 0.0 copy-start.6
  10.8 14.4 %all-to-all-done.refs_7_.refs_8_ = bf16[16,136,128]{2,1,0:T(8,128)(2,1)S(1)} async-done(((bf16[16,136,128]{2,1,0:T(8,128)(2,1)}), bf16[16,136,128]{2,1,0:T(8,128)(2,1)S(1)}, u32[]{:S(2)}, u32[]{:S(2)}) %all-to-all-start) | async-done | bytes 557088 | tf_op jit(solution)/shard_map/all_to_all | solution.py:338
  25.2 0.0 copy-done.3
  25.2 0.0 copy-done.4
  25.2 0.0 copy-done.5
  25.2 0.0 copy-done.7
  25.2 0.0 copy-start.8
  25.2 1.2 %copy-done.8 = bf16[256,2048]{1,0:T(8,128)(2,1)S(1)} copy-done((bf16[256,2048]{1,0:T(8,128)(2,1)S(1)}, bf16[256,2048]{1,0:T(8,128)(2,1)}, u32[]{:S(2)}) %copy-start.8) | copy-done | bytes 1048600
  26.5 6.2 %attend0.1 = (bf16[256,2048]{1,0:T(8,128)(2,1)}, f32[128,256]{1,0:T(8,128)S(1)}, f32[32,256]{1,0:T(8,128)S(1)}, f32[64,256]{1,0:T(8,128)S(1)}, bf16[16,128,128]{...) custom-call(s32[1]{0:T(128)} %bitcast.rank_ref.refs_0_, s32[15,64]{1,0:T(8,128)S(1)} %bitcast.8, ...), custom_call_target="tpu_custom_call" | custom-call | flops 1677721600 | bytes 4194304 | tf_op jit(solution)/shard_map/attend0/pallas_call | solution.py:417
  32.7 0.0 copy-start.9
  32.7 18.5 %all_to_all.15.picks_ref.refs_8_ = bf16[16,128,128]{2,1,0:T(8,128)(2,1)S(1)} all-to-all(bf16[16,128,128]{2,1,0:T(8,128)(2,1)S(1)} %get-tuple-element.21), channel_id=1, replica_groups=mesh['ctx'=16,'head'=2] {'ctx'}, dimensions={0} | all-to-all | bytes 1048576 | tf_op jit(solution)/shard_map/all_to_all | solution.py:338
  51.2 0.0 copy-start.2
  51.2 0.0 copy-done.6
  51.2 5.9 %attend1.1 = (f32[256,256]{1,0:T(8,128)S(1)}, f32[32,256]{1,0:T(8,128)S(1)}, f32[64,256]{1,0:T(8,128)S(1)}, bf16[16,136,128]{2,1,0:T(8,128)(2,1)}) custom-call(s32[1]{0:T(128)} %bitcast.rank_ref.refs_0_, s32[15,64]{1,0:T(8,128)S(1)} %bitcast.9, bf16[256,2048]{1,0:T(8,128)(2,1)S(1)} %copy-done.7, bf16[256,2048]{1,0:T(8,128)(2,1)S(1)} %copy-done.8, ...), custom_call_target="tpu_custom_call" | custom-call | flops 1677721600 | bytes 4194304 | tf_op jit(solution)/shard_map/attend1/pallas_call | solution.py:417
  57.1 0.0 copy-done.9
  57.1 0.0 copy-done.2
  57.1 4.1 %all-to-all-start.2 = ((bf16[16,136,128]{2,1,0:T(8,128)(2,1)}), bf16[16,136,128]{2,1,0:T(8,128)(2,1)S(1)}, u32[]{:S(2)}, u32[]{:S(2)}) async-start(bf16[16,136,128]{2,1,0:T(8,128)(2,1)} %get-tuple-element.28), calls=%async_computation.2 | async-start | bytes 1114112 | tf_op jit(solution)/shard_map/all_to_all | solution.py:338
  61.3 1.6 %collective-permute-start.1 = (bf16[1280,32]{0,1:T(8,128)(2,1)S(1)}, bf16[1280,32]{0,1:T(8,128)(2,1)S(1)}, u32[]{:S(2)}, u32[]{:S(2)}) collective-permute-start(bf16[1280,32]{0,1:T(8,128)(2,1)S(1)} %constant_dynamic-slice_fusion), channel_id=1, source_target_pairs={{0,1},{1,0},{2,3},{3,2},{4,5},{5,4},{6,7},{7,6},{8,9},{9,8},{10,11... | collective-permute-start | bytes 245768 | tf_op jit(solution)/shard_map/ppermute | solution.py:365
  62.9 0.5 collective-permute-start
  63.4 0.3 fusion.1
  63.7 6.2 %tail.1 = bf16[256,2048]{1,0:T(8,128)(2,1)} custom-call(s32[1]{0:T(128)} %bitcast.rank_ref.refs_0_, bf16[256,2048]{1,0:T(8,128)(2,1)} %refs_2_.3, bf16[256,2048]{1,0:T(8,128)(2,1)} %refs_3_.3, bf16[256,128]{1,0:T(8,128)(2,1)} %refs_4_.3, bf16[256,128]{1,0:T(8,128)(2,1)} %refs_5_.3, f32[4,2,1024]{2,1,0:T(2,128)} %copy-done.6, ...), custom_call_target="tpu_custom_call", output_to_operand_aliasing={{}: (8, {})} | custom-call | flops 1677721600 | bytes 4194304 | tf_op jit(solution)/shard_map/tail/pallas_call | solution.py:434
  69.9 0.0 collective-permute-done.1
  69.9 0.0 collective-permute-done
  69.9 1.2 %fusion = bf16[256,1280]{1,0:T(8,128)(2,1)} fusion(f32[256,1280]{1,0:T(8,128)S(1)} %fusion.1, bf16[32,256]{1,0:T(8,128)(2,1)S(1)} %collective-permute-done, bf16[1280,32]{0,1:T(8,128)(2,1)S(1)} %collective-permute-done.1), kind=kOutput, calls=%fused_computation.1 | convolution fusion | flops 21626880 | bytes 2064384 | tf_op jit(solution)/shard_map/dot_general | solution.py:464
  71.1 5.1 %all-to-all-done.2.home_ref = bf16[16,136,128]{2,1,0:T(8,128)(2,1)S(1)} async-done(((bf16[16,136,128]{2,1,0:T(8,128)(2,1)}), bf16[16,136,128]{2,1,0:T(8,128)(2,1)S(1)}, u32[]{:S(2)}, u32[]{:S(2)}) %all-to-all-start.2) | async-done | bytes 557088 | tf_op jit(solution)/shard_map/all_to_all | solution.py:338
  76.2 1.6 %finish.1 = (bf16[256,128]{1,0:T(8,128)(2,1)}, bf16[256,128]{1,0:T(8,128)(2,1)}, bf16[4,128]{1,0:T(4,128)(2,1)}, bf16[4,128]{1,0:T(4,128)(2,1)}) custom-call(s32[1]{0:T(128)} %bitcast.rank_ref.refs_0_, s32[15,64]{1,0:T(8,128)S(1)} %bitcast.10, f32[256,256]{1,0:T(8,128)S(1)} %get-tuple-element.26.part_ref, f32[64,256]{1,0:T(8,128)S(1)} %get-tuple-element.27.dc_ref, ...), custom_call_target="tpu_custom_call" | custom-call | tf_op jit(solution)/shard_map/finish/pallas_call | solution.py:447
  (2 shorter events, 0.0 us)
Async XLA Ops:
  0.6 9.6 %copy-start.1 = (bf16[2560,32]{0,1:T(8,128)(2,1)S(1)}, bf16[2560,32]{0,1:T(8,128)(2,1)}, u32[]{:S(2)}) copy-start(bf16[2560,32]{0,1:T(8,128)(2,1)} %param.16) | copy-start | bytes 491524
  0.6 9.6 %copy-start = (bf16[256,2560]{1,0:T(8,128)(2,1)S(1)}, bf16[256,2560]{1,0:T(8,128)(2,1)}, u32[]{:S(2)}) copy-start(bf16[256,2560]{1,0:T(8,128)(2,1)} %x_ref.1) | copy-start | bytes 3932164
  2.7 22.6 %copy-start.3 = (bf16[256,128]{1,0:T(8,128)(2,1)S(1)}, bf16[256,128]{1,0:T(8,128)(2,1)}, u32[]{:S(2)}) copy-start(bf16[256,128]{1,0:T(8,128)(2,1)} %refs_4_.3) | copy-start | bytes 196612
  2.7 22.6 %copy-start.4 = (bf16[256,128]{1,0:T(8,128)(2,1)S(1)}, bf16[256,128]{1,0:T(8,128)(2,1)}, u32[]{:S(2)}) copy-start(bf16[256,128]{1,0:T(8,128)(2,1)} %refs_5_.3) | copy-start | bytes 196612
  2.7 22.6 %copy-start.5 = (s32[64,15]{0,1:T(8,128)S(1)}, s32[64,15]{0,1:T(8,128)}, u32[]{:S(2)}) copy-start(s32[64,15]{0,1:T(8,128)} %param.14) | copy-start | bytes 11524
  2.7 22.6 %copy-start.7 = (bf16[256,2048]{1,0:T(8,128)(2,1)S(1)}, bf16[256,2048]{1,0:T(8,128)(2,1)}, u32[]{:S(2)}) copy-start(bf16[256,2048]{1,0:T(8,128)(2,1)} %refs_2_.3) | copy-start | bytes 3145732
  2.7 22.5 %all-to-all-start = ((bf16[16,136,128]{2,1,0:T(8,128)(2,1)}), bf16[16,136,128]{2,1,0:T(8,128)(2,1)S(1)}, u32[]{:S(2)}, u32[]{:S(2)}) async-start(bf16[16,136,128]{2,1,0:T(8,128)(2,1)} %pack.1), calls=%async_computation | async-start | bytes 1114112 | tf_op jit(solution)/shard_map/all_to_all | solution.py:338
  10.8 40.4 %copy-start.6 = (f32[4,2,1024]{2,1,0:T(2,128)}, f32[4,2,1024]{2,1,0:T(2,128)S(1)}, u32[]{:S(2)}) copy-start(f32[4,2,1024]{2,1,0:T(2,128)S(1)} %gate.1.refs_6_.gate_ref) | copy-start | bytes 98308
  25.2 1.2 %copy-start.8 = (bf16[256,2048]{1,0:T(8,128)(2,1)S(1)}, bf16[256,2048]{1,0:T(8,128)(2,1)}, u32[]{:S(2)}) copy-start(bf16[256,2048]{1,0:T(8,128)(2,1)} %refs_3_.3) | copy-start | bytes 3145732
  32.7 24.4 %copy-start.9 = (bf16[64,256]{1,0:T(8,128)(2,1)}, bf16[64,256]{1,0:T(8,128)(2,1)S(1)}, u32[]{:S(2)}) copy-start(bf16[64,256]{1,0:T(8,128)(2,1)S(1)} %get-tuple-element.20.ckv_ref.refs_7_) | copy-start | bytes 98308
  51.2 5.9 %copy-start.2 = (bf16[16,128,128]{2,1,0:T(8,128)(2,1)}, bf16[16,128,128]{2,1,0:T(8,128)(2,1)S(1)}, u32[]{:S(2)}) copy-start(bf16[16,128,128]{2,1,0:T(8,128)(2,1)S(1)} %all_to_all.15.picks_ref.refs_8_) | copy-start | bytes 1572868
  57.1 19.1 %all-to-all-start.2 = ((bf16[16,136,128]{2,1,0:T(8,128)(2,1)}), bf16[16,136,128]{2,1,0:T(8,128)(2,1)S(1)}, u32[]{:S(2)}, u32[]{:S(2)}) async-start(bf16[16,136,128]{2,1,0:T(8,128)(2,1)} %get-tuple-element.28), calls=%async_computation.2 | async-start | bytes 1114112 | tf_op jit(solution)/shard_map/all_to_all | solution.py:338
  61.3 8.7 %collective-permute-start.1 = (bf16[1280,32]{0,1:T(8,128)(2,1)S(1)}, bf16[1280,32]{0,1:T(8,128)(2,1)S(1)}, u32[]{:S(2)}, u32[]{:S(2)}) collective-permute-start(bf16[1280,32]{0,1:T(8,128)(2,1)S(1)} %constant_dynamic-slice_fusion), channel_id=1, source_target_pairs={{0,1},{1,0},{2,3},{3,2},{4,5},{5,4},{6,7},{7,6},{8,9},{9,8},{10,11... | collective-permute-start | bytes 245768 | tf_op jit(solution)/shard_map/ppermute | solution.py:365
  62.9 7.1 %collective-permute-start = (bf16[32,256]{1,0:T(8,128)(2,1)S(1)}, bf16[32,256]{1,0:T(8,128)(2,1)S(1)}, u32[]{:S(2)}, u32[]{:S(2)}) collective-permute-start(bf16[32,256]{1,0:T(8,128)(2,1)S(1)} %convert_element_type.6), channel_id=1, source_target_pairs={{0,1},{1,0},{2,3},{3,2},{4,5},{5,4},{6,7},{7,6},{8,9},{9,8},{10,11... | collective-permute-start | bytes 49160 | tf_op jit(solution)/shard_map/ppermute | solution.py:460

commit v10 on v9

--- a/solution.py
+++ b/solution.py
@@ -65,7 +65,8 @@
     fill_picks(ranks, qb, lists, 0, me, sel_ref, k_ref, v_ref, out_ref)
 
 
-def gate_kernel(qb, heads, x_ref, w_ref, out_ref):
+def gate_kernel(qb, heads, x_ref, w_ref, do_ref, out_ref):
+    del do_ref
     nt = (((1,), (1,)), ((), ()))
     z = lax.dot_general(w_ref[...], x_ref[...], nt, preferred_element_type=F32)
     zt = jax.nn.sigmoid(z)
@@ -350,14 +351,14 @@
     gate = pl.pallas_call(
         functools.partial(gate_kernel, qb, heads),
         out_shape=jax.ShapeDtypeStruct((qb, 2, heads * BLK), F32),
-        in_specs=[in_vmem()] * 2,
+        in_specs=[in_vmem()] * 3,
         out_specs=in_vmem(),
         compiler_params=params(ranks),
         cost_estimate=pl.CostEstimate(
             flops=2 * inputs.size * w_gate.shape[1], bytes_accessed=2 * inputs.size, transcendentals=0
         ),
         name="gate",
-    )(inputs, w_gate.T)
+    )(inputs, w_gate.T, d_out)
     half = w_gate.shape[0] // 2
     swap = [(0, 1), (1, 0)]
     w_send = lax.dynamic_slice_in_dim(w_gate, (1 - head) * half, half, 0)

time: 78.3 us -> 78.1 us (level)
  waiting for transfers between devices: 19.5 us -> 17.1 us
  local copies, waits for them, and re-layouts: 1.27 us -> 2.49 us
  matrix products: 1.54 us -> 2.62 us
    all_to_all x2, waiting for transfers between devices: 19.5 us -> 17.1 us  [exchange(): return lax.all_to_all(x, 'ctx', split_axis=0, concat_axis=0, tiled=True)]
    unnamed x20 -> x24, local copies, waits for them, and re-layouts: 1.26 us -> 2.48 us
    dot_general x1, matrix products: 0.35 us -> 1.43 us  [body(): lax.dot_general(dz, w_mine, tn, preferred_element_type=F32)]
  transfers between devices with their start and end apart: 4 -> 4, of which waited for: 2 -> 2; matrix products, arithmetic and copies ran while one was open for 2% -> 3% of each run, Pallas kernels for 9% -> 9%
where the time goes in v10:
time: 78.1 us; the launch traced here: 77.7 us
  Pallas kernels  22.6 us (29%)
  blocking collectives  18.5 us (24%)
  waiting for transfers between devices  17.1 us (22%)
  starting transfers between devices  13.6 us (17%)
  matrix products  2.62 us (3%)
  local copies, waits for them, and re-layouts  2.49 us (3%)
    all_to_all x1, blocking collectives, exchange(): return lax.all_to_all(x, 'ctx', split_axis=0, concat_axis=0, tiled=True)  18.5 us
    all_to_all x2, waiting for transfers between devices, exchange(): return lax.all_to_all(x, 'ctx', split_axis=0, concat_axis=0, tiled=True)  17.1 us
    pallas_call x2, Pallas kernels, attend(): pl.pallas_call(functools.partial(attend_kernel, ranks, qb, heads, lists,...  12.1 us
    all_to_all x2, starting transfers between devices, exchange(): return lax.all_to_all(x, 'ctx', split_axis=0, concat_axis=0, tiled=True)  11.5 us
    pallas_call x1, Pallas kernels, body(): pl.pallas_call(functools.partial(tail_kernel, ranks, qb, heads, lists), g...  6.26 us
    unnamed x24, local copies, waits for them, and re-layouts  2.48 us
    pallas_call x1, Pallas kernels, body(): pl.pallas_call(functools.partial(pack_kernel, ranks, qb, lists), out_shap...  2 us
    ppermute x1, starting transfers between devices, body(): w_other = lax.ppermute(w_send, 'head', swap)  1.61 us
  transfers between devices with their start and end apart: 4, of which 2 were waited for; matrix products, arithmetic and copies ran while one was open for 3% of the time, Pallas kernels for 9%

profile of v10, /device:TPU:0, one launch (start us, length us, event | category | flops | bytes accessed | tf_op | source)
XLA Modules:
  0.0 77.7 jit_solution(7557654755075845307)
XLA Ops:
  0.6 0.0 copy-start.3
  0.6 0.0 copy-start
  0.7 2.0 %pack.1 = bf16[16,136,128]{2,1,0:T(8,128)(2,1)} custom-call(s32[1]{0:T(128)} %bitcast.rank_ref.refs_0_, s32[15,64]{1,0:T(8,128)} %bitcast.7, bf16[256,128]{1,0:T(8,128)(2,1)} %refs_4_.3, bf16[256,128]{1,0:T(8,128)(2,1)} %refs_5_.3, bf16[4,128]{1,0:T(4,128)(2,1)} %ck_ref.1, bf16[4,128]{1,0:T(4,128)(2,1)} %cv_ref.1), custom_call_target="tpu_custom_call" | custom-call | tf_op jit(solution)/shard_map/pack/pallas_call | solution.py:341
  2.7 7.4 %all-to-all-start = ((bf16[16,136,128]{2,1,0:T(8,128)(2,1)}), bf16[16,136,128]{2,1,0:T(8,128)(2,1)S(1)}, u32[]{:S(2)}, u32[]{:S(2)}) async-start(bf16[16,136,128]{2,1,0:T(8,128)(2,1)} %pack.1), calls=%async_computation | async-start | bytes 1114112 | tf_op jit(solution)/shard_map/all_to_all | solution.py:339
  10.0 0.0 copy-done.3
  10.0 0.0 copy-done
  10.0 0.0 copy-start.1
  10.1 1.2 %copy-done.1 = bf16[256,2048]{1,0:T(8,128)(2,1)S(1)} copy-done((bf16[256,2048]{1,0:T(8,128)(2,1)S(1)}, bf16[256,2048]{1,0:T(8,128)(2,1)}, u32[]{:S(2)}) %copy-start.1) | copy-done | bytes 1048600
  11.3 0.0 copy-start.2
  11.3 0.0 copy-start.5
  11.3 0.0 copy-start.6
  11.3 0.0 copy-start.8
  11.3 0.6 gate.1.refs_6_.gate_ref
  11.9 0.0 copy-start.7
  11.9 13.1 %all-to-all-done.refs_7_.refs_8_ = bf16[16,136,128]{2,1,0:T(8,128)(2,1)S(1)} async-done(((bf16[16,136,128]{2,1,0:T(8,128)(2,1)}), bf16[16,136,128]{2,1,0:T(8,128)(2,1)S(1)}, u32[]{:S(2)}, u32[]{:S(2)}) %all-to-all-start) | async-done | bytes 557088 | tf_op jit(solution)/shard_map/all_to_all | solution.py:339
  25.0 0.0 copy-done.2
  25.0 0.0 copy-done.5
  25.0 0.0 copy-done.6
  25.1 0.0 copy-done.8
  25.1 0.0 copy-start.9
  25.1 1.2 %copy-done.9 = bf16[256,2048]{1,0:T(8,128)(2,1)S(1)} copy-done((bf16[256,2048]{1,0:T(8,128)(2,1)S(1)}, bf16[256,2048]{1,0:T(8,128)(2,1)}, u32[]{:S(2)}) %copy-start.9) | copy-done | bytes 1048600
  26.3 6.2 %attend0.1 = (bf16[256,2048]{1,0:T(8,128)(2,1)}, f32[128,256]{1,0:T(8,128)S(1)}, f32[32,256]{1,0:T(8,128)S(1)}, f32[64,256]{1,0:T(8,128)S(1)}, bf16[16,128,128]{...) custom-call(s32[1]{0:T(128)} %bitcast.rank_ref.refs_0_, s32[15,64]{1,0:T(8,128)S(1)} %bitcast.8, ...), custom_call_target="tpu_custom_call" | custom-call | flops 1677721600 | bytes 4194304 | tf_op jit(solution)/shard_map/attend0/pallas_call | solution.py:418
  32.5 0.0 copy-start.10
  32.5 18.5 %all_to_all.15.picks_ref.refs_8_ = bf16[16,128,128]{2,1,0:T(8,128)(2,1)S(1)} all-to-all(bf16[16,128,128]{2,1,0:T(8,128)(2,1)S(1)} %get-tuple-element.21), channel_id=1, replica_groups=mesh['ctx'=16,'head'=2] {'ctx'}, dimensions={0} | all-to-all | bytes 1048576 | tf_op jit(solution)/shard_map/all_to_all | solution.py:339
  51.0 0.0 copy-start.4
  51.0 0.0 copy-done.7
  51.0 5.9 %attend1.1 = (f32[256,256]{1,0:T(8,128)S(1)}, f32[32,256]{1,0:T(8,128)S(1)}, f32[64,256]{1,0:T(8,128)S(1)}, bf16[16,136,128]{2,1,0:T(8,128)(2,1)}) custom-call(s32[1]{0:T(128)} %bitcast.rank_ref.refs_0_, s32[15,64]{1,0:T(8,128)S(1)} %bitcast.9, bf16[256,2048]{1,0:T(8,128)(2,1)S(1)} %copy-done.9, bf16[256,2048]{1,0:T(8,128)(2,1)S(1)} %copy-done.2, ...), custom_call_target="tpu_custom_call" | custom-call | flops 1677721600 | bytes 4194304 | tf_op jit(solution)/shard_map/attend1/pallas_call | solution.py:418
  56.9 0.0 copy-done.10
  56.9 0.0 copy-done.4
  56.9 4.1 %all-to-all-start.2 = ((bf16[16,136,128]{2,1,0:T(8,128)(2,1)}), bf16[16,136,128]{2,1,0:T(8,128)(2,1)S(1)}, u32[]{:S(2)}, u32[]{:S(2)}) async-start(bf16[16,136,128]{2,1,0:T(8,128)(2,1)} %get-tuple-element.28), calls=%async_computation.2 | async-start | bytes 1114112 | tf_op jit(solution)/shard_map/all_to_all | solution.py:339
  61.1 1.6 %collective-permute-start.1 = (bf16[1280,32]{0,1:T(8,128)(2,1)S(1)}, bf16[1280,32]{0,1:T(8,128)(2,1)S(1)}, u32[]{:S(2)}, u32[]{:S(2)}) collective-permute-start(bf16[1280,32]{0,1:T(8,128)(2,1)S(1)} %constant_dynamic-slice_fusion), channel_id=1, source_target_pairs={{0,1},{1,0},{2,3},{3,2},{4,5},{5,4},{6,7},{7,6},{8,9},{9,8},{10,11... | collective-permute-start | bytes 245768 | tf_op jit(solution)/shard_map/ppermute | solution.py:366
  62.7 0.5 collective-permute-start
  63.2 1.4 %fusion.1 = f32[256,1280]{1,0:T(8,128)} fusion(bf16[32,256]{1,0:T(8,128)(2,1)S(1)} %convert_element_type.6, bf16[2560,32]{0,1:T(8,128)(2,1)S(1)} %copy-done.3, s32[]{:T(128)S(6)} %select_n.6), kind=kOutput, calls=%fused_computation.2 | convolution fusion | flops 20971520 | bytes 1409028 | tf_op jit(solution)/shard_map/dot_general | solution.py:464
  64.7 0.0 copy-start.11
  64.7 6.3 %tail.1 = bf16[256,2048]{1,0:T(8,128)(2,1)} custom-call(s32[1]{0:T(128)} %bitcast.rank_ref.refs_0_, bf16[256,2048]{1,0:T(8,128)(2,1)} %refs_2_.3, bf16[256,2048]{1,0:T(8,128)(2,1)} %refs_3_.3, bf16[256,128]{1,0:T(8,128)(2,1)} %refs_4_.3, bf16[256,128]{1,0:T(8,128)(2,1)} %refs_5_.3, f32[4,2,1024]{2,1,0:T(2,128)} %copy-done.7, ...), custom_call_target="tpu_custom_call", output_to_operand_aliasing={{}: (8, {})} | custom-call | flops 1677721600 | bytes 4194304 | tf_op jit(solution)/shard_map/tail/pallas_call | solution.py:435
  70.9 0.0 collective-permute-done.1
  70.9 0.0 collective-permute-done
  70.9 0.0 copy-done.11
  70.9 1.2 %fusion = bf16[256,1280]{1,0:T(8,128)(2,1)} fusion(f32[256,1280]{1,0:T(8,128)S(1)} %copy-done.11, bf16[32,256]{1,0:T(8,128)(2,1)S(1)} %collective-permute-done, bf16[1280,32]{0,1:T(8,128)(2,1)S(1)} %collective-permute-done.1), kind=kOutput, calls=%fused_computation.1 | convolution fusion | flops 21626880 | bytes 2064384 | tf_op jit(solution)/shard_map/dot_general | solution.py:465
  72.1 4.0 %all-to-all-done.2.home_ref = bf16[16,136,128]{2,1,0:T(8,128)(2,1)S(1)} async-done(((bf16[16,136,128]{2,1,0:T(8,128)(2,1)}), bf16[16,136,128]{2,1,0:T(8,128)(2,1)S(1)}, u32[]{:S(2)}, u32[]{:S(2)}) %all-to-all-start.2) | async-done | bytes 557088 | tf_op jit(solution)/shard_map/all_to_all | solution.py:339
  76.1 1.6 %finish.1 = (bf16[256,128]{1,0:T(8,128)(2,1)}, bf16[256,128]{1,0:T(8,128)(2,1)}, bf16[4,128]{1,0:T(4,128)(2,1)}, bf16[4,128]{1,0:T(4,128)(2,1)}) custom-call(s32[1]{0:T(128)} %bitcast.rank_ref.refs_0_, s32[15,64]{1,0:T(8,128)S(1)} %bitcast.10, f32[256,256]{1,0:T(8,128)S(1)} %get-tuple-element.26.part_ref, f32[64,256]{1,0:T(8,128)S(1)} %get-tuple-element.27.dc_ref, ...), custom_call_target="tpu_custom_call" | custom-call | tf_op jit(solution)/shard_map/finish/pallas_call | solution.py:448
  (2 shorter events, 0.0 us)
Async XLA Ops:
  0.6 9.4 %copy-start.3 = (bf16[2560,32]{0,1:T(8,128)(2,1)S(1)}, bf16[2560,32]{0,1:T(8,128)(2,1)}, u32[]{:S(2)}) copy-start(bf16[2560,32]{0,1:T(8,128)(2,1)} %param.16) | copy-start | bytes 491524
  0.6 9.4 %copy-start = (bf16[256,2560]{1,0:T(8,128)(2,1)S(1)}, bf16[256,2560]{1,0:T(8,128)(2,1)}, u32[]{:S(2)}) copy-start(bf16[256,2560]{1,0:T(8,128)(2,1)} %x_ref.1) | copy-start | bytes 3932164
  2.7 22.4 %all-to-all-start = ((bf16[16,136,128]{2,1,0:T(8,128)(2,1)}), bf16[16,136,128]{2,1,0:T(8,128)(2,1)S(1)}, u32[]{:S(2)}, u32[]{:S(2)}) async-start(bf16[16,136,128]{2,1,0:T(8,128)(2,1)} %pack.1), calls=%async_computation | async-start | bytes 1114112 | tf_op jit(solution)/shard_map/all_to_all | solution.py:339
  10.0 1.2 %copy-start.1 = (bf16[256,2048]{1,0:T(8,128)(2,1)S(1)}, bf16[256,2048]{1,0:T(8,128)(2,1)}, u32[]{:S(2)}) copy-start(bf16[256,2048]{1,0:T(8,128)(2,1)} %refs_3_.3) | copy-start | bytes 3145732
  11.3 13.8 %copy-start.2 = (bf16[256,2048]{1,0:T(8,128)(2,1)S(1)}, bf16[256,2048]{1,0:T(8,128)(2,1)}, u32[]{:S(2)}) copy-start(bf16[256,2048]{1,0:T(8,128)(2,1)} %refs_3_.3) | copy-start | bytes 3145732
  11.3 13.8 %copy-start.5 = (bf16[256,128]{1,0:T(8,128)(2,1)S(1)}, bf16[256,128]{1,0:T(8,128)(2,1)}, u32[]{:S(2)}) copy-start(bf16[256,128]{1,0:T(8,128)(2,1)} %refs_4_.3) | copy-start | bytes 196612
  11.3 13.8 %copy-start.6 = (bf16[256,128]{1,0:T(8,128)(2,1)S(1)}, bf16[256,128]{1,0:T(8,128)(2,1)}, u32[]{:S(2)}) copy-start(bf16[256,128]{1,0:T(8,128)(2,1)} %refs_5_.3) | copy-start | bytes 196612
  11.3 13.8 %copy-start.8 = (s32[64,15]{0,1:T(8,128)S(1)}, s32[64,15]{0,1:T(8,128)}, u32[]{:S(2)}) copy-start(s32[64,15]{0,1:T(8,128)} %param.14) | copy-start | bytes 11524
  11.9 39.1 %copy-start.7 = (f32[4,2,1024]{2,1,0:T(2,128)}, f32[4,2,1024]{2,1,0:T(2,128)S(1)}, u32[]{:S(2)}) copy-start(f32[4,2,1024]{2,1,0:T(2,128)S(1)} %gate.1.refs_6_.gate_ref) | copy-start | bytes 98308
  25.1 1.2 %copy-start.9 = (bf16[256,2048]{1,0:T(8,128)(2,1)S(1)}, bf16[256,2048]{1,0:T(8,128)(2,1)}, u32[]{:S(2)}) copy-start(bf16[256,2048]{1,0:T(8,128)(2,1)} %refs_2_.3) | copy-start | bytes 3145732
  32.5 24.4 %copy-start.10 = (bf16[64,256]{1,0:T(8,128)(2,1)}, bf16[64,256]{1,0:T(8,128)(2,1)S(1)}, u32[]{:S(2)}) copy-start(bf16[64,256]{1,0:T(8,128)(2,1)S(1)} %get-tuple-element.20.ckv_ref.refs_7_) | copy-start | bytes 98308
  51.0 5.9 %copy-start.4 = (bf16[16,128,128]{2,1,0:T(8,128)(2,1)}, bf16[16,128,128]{2,1,0:T(8,128)(2,1)S(1)}, u32[]{:S(2)}) copy-start(bf16[16,128,128]{2,1,0:T(8,128)(2,1)S(1)} %all_to_all.15.picks_ref.refs_8_) | copy-start | bytes 1572868
  56.9 19.1 %all-to-all-start.2 = ((bf16[16,136,128]{2,1,0:T(8,128)(2,1)}), bf16[16,136,128]{2,1,0:T(8,128)(2,1)S(1)}, u32[]{:S(2)}, u32[]{:S(2)}) async-start(bf16[16,136,128]{2,1,0:T(8,128)(2,1)} %get-tuple-element.28), calls=%async_computation.2 | async-start | bytes 1114112 | tf_op jit(solution)/shard_map/all_to_all | solution.py:339
  61.1 9.8 %collective-permute-start.1 = (bf16[1280,32]{0,1:T(8,128)(2,1)S(1)}, bf16[1280,32]{0,1:T(8,128)(2,1)S(1)}, u32[]{:S(2)}, u32[]{:S(2)}) collective-permute-start(bf16[1280,32]{0,1:T(8,128)(2,1)S(1)} %constant_dynamic-slice_fusion), channel_id=1, source_target_pairs={{0,1},{1,0},{2,3},{3,2},{4,5},{5,4},{6,7},{7,6},{8,9},{9,8},{10,11... | collective-permute-start | bytes 245768 | tf_op jit(solution)/shard_map/ppermute | solution.py:366
  62.7 8.2 %collective-permute-start = (bf16[32,256]{1,0:T(8,128)(2,1)S(1)}, bf16[32,256]{1,0:T(8,128)(2,1)S(1)}, u32[]{:S(2)}, u32[]{:S(2)}) collective-permute-start(bf16[32,256]{1,0:T(8,128)(2,1)S(1)} %convert_element_type.6), channel_id=1, source_target_pairs={{0,1},{1,0},{2,3},{3,2},{4,5},{5,4},{6,7},{7,6},{8,9},{9,8},{10,11... | collective-permute-start | bytes 49160 | tf_op jit(solution)/shard_map/ppermute | solution.py:461
  64.7 6.3 %copy-start.11 = (f32[256,1280]{1,0:T(8,128)S(1)}, f32[256,1280]{1,0:T(8,128)}, u32[]{:S(2)}) copy-start(f32[256,1280]{1,0:T(8,128)} %fusion.1) | copy-start | bytes 3932164

commit v11 on v10

--- a/solution.py
+++ b/solution.py
@@ -206,8 +206,6 @@
         src = jnp.where(me >= r, me - r, me)
         kcat[(n + 1) * BLK : (n + 2) * BLK, :] = picks_ref[src, :BLK, :]
         vcat[(n + 1) * BLK : (n + 2) * BLK, :] = picks_ref[src, BLK : 2 * BLK, :]
-    if dq_ref is not None:
-        kt[:, :nk] = kcat[:nk, :].astype(F32).T.astype(BF16)
     for h in range(heads):
         qs[h * BLK : (h + 1) * BLK, :] = q_ref[:, h * hd : (h + 1) * hd]
         ds[h * BLK : (h + 1) * BLK, :] = do_ref[:, h * hd : (h + 1) * hd]
@@ -263,6 +261,8 @@
                 dq_ref[:, head * hd : (head + 1) * hd] = dq[h * BLK : (h + 1) * BLK, :]
 
     scores(0)
+    if dq_ref is not None:
+        kt[:, :nk] = kcat[:nk, :].astype(F32).T.astype(BF16)
     for c in range(chunks):
         if c + 1 < chunks:
             scores(c + 1)

time: 78.1 us -> 78.1 us (level)
  no operation moved by 1% of the time
where the time goes in v11:
time: 78.1 us; the launch traced here: 77.7 us
  Pallas kernels  22.6 us (29%)
  blocking collectives  18.5 us (24%)
  waiting for transfers between devices  17.1 us (22%)
  starting transfers between devices  13.6 us (17%)
  matrix products  2.63 us (3%)
  local copies, waits for them, and re-layouts  2.49 us (3%)
    all_to_all x1, blocking collectives, exchange(): return lax.all_to_all(x, 'ctx', split_axis=0, concat_axis=0, tiled=True)  18.5 us
    all_to_all x2, waiting for transfers between devices, exchange(): return lax.all_to_all(x, 'ctx', split_axis=0, concat_axis=0, tiled=True)  17.1 us
    pallas_call x2, Pallas kernels, attend(): pl.pallas_call(functools.partial(attend_kernel, ranks, qb, heads, lists,...  12.2 us
    all_to_all x2, starting transfers between devices, exchange(): return lax.all_to_all(x, 'ctx', split_axis=0, concat_axis=0, tiled=True)  11.5 us
    pallas_call x1, Pallas kernels, body(): pl.pallas_call(functools.partial(tail_kernel, ranks, qb, heads, lists), g...  6.25 us
    unnamed x24, local copies, waits for them, and re-layouts  2.48 us
    pallas_call x1, Pallas kernels, body(): pl.pallas_call(functools.partial(pack_kernel, ranks, qb, lists), out_shap...  2 us
    ppermute x1, starting transfers between devices, body(): w_other = lax.ppermute(w_send, 'head', swap)  1.61 us
  transfers between devices with their start and end apart: 4, of which 2 were waited for; matrix products, arithmetic and copies ran while one was open for 3% of the time, Pallas kernels for 9%

profile of v11, /device:TPU:0, one launch (start us, length us, event | category | flops | bytes accessed | tf_op | source)
XLA Modules:
  0.0 77.7 jit_solution(5235026830035385022)
XLA Ops:
  0.6 0.0 copy-start.3
  0.6 0.0 copy-start
  0.7 2.0 %pack.1 = bf16[16,136,128]{2,1,0:T(8,128)(2,1)} custom-call(s32[1]{0:T(128)} %bitcast.rank_ref.refs_0_, s32[15,64]{1,0:T(8,128)} %bitcast.7, bf16[256,128]{1,0:T(8,128)(2,1)} %refs_4_.3, bf16[256,128]{1,0:T(8,128)(2,1)} %refs_5_.3, bf16[4,128]{1,0:T(4,128)(2,1)} %ck_ref.1, bf16[4,128]{1,0:T(4,128)(2,1)} %cv_ref.1), custom_call_target="tpu_custom_call" | custom-call | tf_op jit(solution)/shard_map/pack/pallas_call | solution.py:341
  2.7 7.4 %all-to-all-start = ((bf16[16,136,128]{2,1,0:T(8,128)(2,1)}), bf16[16,136,128]{2,1,0:T(8,128)(2,1)S(1)}, u32[]{:S(2)}, u32[]{:S(2)}) async-start(bf16[16,136,128]{2,1,0:T(8,128)(2,1)} %pack.1), calls=%async_computation | async-start | bytes 1114112 | tf_op jit(solution)/shard_map/all_to_all | solution.py:339
  10.0 0.0 copy-done.3
  10.0 0.0 copy-done
  10.0 0.0 copy-start.1
  10.1 1.2 %copy-done.1 = bf16[256,2048]{1,0:T(8,128)(2,1)S(1)} copy-done((bf16[256,2048]{1,0:T(8,128)(2,1)S(1)}, bf16[256,2048]{1,0:T(8,128)(2,1)}, u32[]{:S(2)}) %copy-start.1) | copy-done | bytes 1048600
  11.3 0.0 copy-start.2
  11.3 0.0 copy-start.5
  11.3 0.0 copy-start.6
  11.3 0.0 copy-start.8
  11.3 0.6 gate.1.refs_6_.gate_ref
  11.9 0.0 copy-start.7
  11.9 13.1 %all-to-all-done.refs_7_.refs_8_ = bf16[16,136,128]{2,1,0:T(8,128)(2,1)S(1)} async-done(((bf16[16,136,128]{2,1,0:T(8,128)(2,1)}), bf16[16,136,128]{2,1,0:T(8,128)(2,1)S(1)}, u32[]{:S(2)}, u32[]{:S(2)}) %all-to-all-start) | async-done | bytes 557088 | tf_op jit(solution)/shard_map/all_to_all | solution.py:339
  25.0 0.0 copy-done.2
  25.0 0.0 copy-done.5
  25.0 0.0 copy-done.6
  25.1 0.0 copy-done.8
  25.1 0.0 copy-start.9
  25.1 1.2 %copy-done.9 = bf16[256,2048]{1,0:T(8,128)(2,1)S(1)} copy-done((bf16[256,2048]{1,0:T(8,128)(2,1)S(1)}, bf16[256,2048]{1,0:T(8,128)(2,1)}, u32[]{:S(2)}) %copy-start.9) | copy-done | bytes 1048600
  26.3 6.2 %attend0.1 = (bf16[256,2048]{1,0:T(8,128)(2,1)}, f32[128,256]{1,0:T(8,128)S(1)}, f32[32,256]{1,0:T(8,128)S(1)}, f32[64,256]{1,0:T(8,128)S(1)}, bf16[16,128,128]{...) custom-call(s32[1]{0:T(128)} %bitcast.rank_ref.refs_0_, s32[15,64]{1,0:T(8,128)S(1)} %bitcast.8, ...), custom_call_target="tpu_custom_call" | custom-call | flops 1677721600 | bytes 4194304 | tf_op jit(solution)/shard_map/attend0/pallas_call | solution.py:418
  32.5 0.0 copy-start.10
  32.5 18.5 %all_to_all.15.picks_ref.refs_8_ = bf16[16,128,128]{2,1,0:T(8,128)(2,1)S(1)} all-to-all(bf16[16,128,128]{2,1,0:T(8,128)(2,1)S(1)} %get-tuple-element.21), channel_id=1, replica_groups=mesh['ctx'=16,'head'=2] {'ctx'}, dimensions={0} | all-to-all | bytes 1048576 | tf_op jit(solution)/shard_map/all_to_all | solution.py:339
  51.0 0.0 copy-start.4
  51.0 0.0 copy-done.7
  51.0 5.9 %attend1.1 = (f32[256,256]{1,0:T(8,128)S(1)}, f32[32,256]{1,0:T(8,128)S(1)}, f32[64,256]{1,0:T(8,128)S(1)}, bf16[16,136,128]{2,1,0:T(8,128)(2,1)}) custom-call(s32[1]{0:T(128)} %bitcast.rank_ref.refs_0_, s32[15,64]{1,0:T(8,128)S(1)} %bitcast.9, bf16[256,2048]{1,0:T(8,128)(2,1)S(1)} %copy-done.9, bf16[256,2048]{1,0:T(8,128)(2,1)S(1)} %copy-done.2, ...), custom_call_target="tpu_custom_call" | custom-call | flops 1677721600 | bytes 4194304 | tf_op jit(solution)/shard_map/attend1/pallas_call | solution.py:418
  57.0 0.0 copy-done.10
  57.0 0.0 copy-done.4
  57.0 4.1 %all-to-all-start.2 = ((bf16[16,136,128]{2,1,0:T(8,128)(2,1)}), bf16[16,136,128]{2,1,0:T(8,128)(2,1)S(1)}, u32[]{:S(2)}, u32[]{:S(2)}) async-start(bf16[16,136,128]{2,1,0:T(8,128)(2,1)} %get-tuple-element.28), calls=%async_computation.2 | async-start | bytes 1114112 | tf_op jit(solution)/shard_map/all_to_all | solution.py:339
  61.1 1.6 %collective-permute-start.1 = (bf16[1280,32]{0,1:T(8,128)(2,1)S(1)}, bf16[1280,32]{0,1:T(8,128)(2,1)S(1)}, u32[]{:S(2)}, u32[]{:S(2)}) collective-permute-start(bf16[1280,32]{0,1:T(8,128)(2,1)S(1)} %constant_dynamic-slice_fusion), channel_id=1, source_target_pairs={{0,1},{1,0},{2,3},{3,2},{4,5},{5,4},{6,7},{7,6},{8,9},{9,8},{10,11... | collective-permute-start | bytes 245768 | tf_op jit(solution)/shard_map/ppermute | solution.py:366
  62.7 0.5 collective-permute-start
  63.2 1.4 %fusion.1 = f32[256,1280]{1,0:T(8,128)} fusion(bf16[32,256]{1,0:T(8,128)(2,1)S(1)} %convert_element_type.6, bf16[2560,32]{0,1:T(8,128)(2,1)S(1)} %copy-done.3, s32[]{:T(128)S(6)} %select_n.6), kind=kOutput, calls=%fused_computation.2 | convolution fusion | flops 20971520 | bytes 1409028 | tf_op jit(solution)/shard_map/dot_general | solution.py:464
  64.7 0.0 copy-start.11
  64.7 6.2 %tail.1 = bf16[256,2048]{1,0:T(8,128)(2,1)} custom-call(s32[1]{0:T(128)} %bitcast.rank_ref.refs_0_, bf16[256,2048]{1,0:T(8,128)(2,1)} %refs_2_.3, bf16[256,2048]{1,0:T(8,128)(2,1)} %refs_3_.3, bf16[256,128]{1,0:T(8,128)(2,1)} %refs_4_.3, bf16[256,128]{1,0:T(8,128)(2,1)} %refs_5_.3, f32[4,2,1024]{2,1,0:T(2,128)} %copy-done.7, ...), custom_call_target="tpu_custom_call", output_to_operand_aliasing={{}: (8, {})} | custom-call | flops 1677721600 | bytes 4194304 | tf_op jit(solution)/shard_map/tail/pallas_call | solution.py:435
  70.9 0.0 collective-permute-done.1
  70.9 0.0 collective-permute-done
  70.9 0.0 copy-done.11
  70.9 1.2 %fusion = bf16[256,1280]{1,0:T(8,128)(2,1)} fusion(f32[256,1280]{1,0:T(8,128)S(1)} %copy-done.11, bf16[32,256]{1,0:T(8,128)(2,1)S(1)} %collective-permute-done, bf16[1280,32]{0,1:T(8,128)(2,1)S(1)} %collective-permute-done.1), kind=kOutput, calls=%fused_computation.1 | convolution fusion | flops 21626880 | bytes 2064384 | tf_op jit(solution)/shard_map/dot_general | solution.py:465
  72.1 4.0 %all-to-all-done.2.home_ref = bf16[16,136,128]{2,1,0:T(8,128)(2,1)S(1)} async-done(((bf16[16,136,128]{2,1,0:T(8,128)(2,1)}), bf16[16,136,128]{2,1,0:T(8,128)(2,1)S(1)}, u32[]{:S(2)}, u32[]{:S(2)}) %all-to-all-start.2) | async-done | bytes 557088 | tf_op jit(solution)/shard_map/all_to_all | solution.py:339
  76.1 1.6 %finish.1 = (bf16[256,128]{1,0:T(8,128)(2,1)}, bf16[256,128]{1,0:T(8,128)(2,1)}, bf16[4,128]{1,0:T(4,128)(2,1)}, bf16[4,128]{1,0:T(4,128)(2,1)}) custom-call(s32[1]{0:T(128)} %bitcast.rank_ref.refs_0_, s32[15,64]{1,0:T(8,128)S(1)} %bitcast.10, f32[256,256]{1,0:T(8,128)S(1)} %get-tuple-element.26.part_ref, f32[64,256]{1,0:T(8,128)S(1)} %get-tuple-element.27.dc_ref, ...), custom_call_target="tpu_custom_call" | custom-call | tf_op jit(solution)/shard_map/finish/pallas_call | solution.py:448
  (2 shorter events, 0.0 us)
Async XLA Ops:
  0.6 9.4 %copy-start.3 = (bf16[2560,32]{0,1:T(8,128)(2,1)S(1)}, bf16[2560,32]{0,1:T(8,128)(2,1)}, u32[]{:S(2)}) copy-start(bf16[2560,32]{0,1:T(8,128)(2,1)} %param.16) | copy-start | bytes 491524
  0.6 9.4 %copy-start = (bf16[256,2560]{1,0:T(8,128)(2,1)S(1)}, bf16[256,2560]{1,0:T(8,128)(2,1)}, u32[]{:S(2)}) copy-start(bf16[256,2560]{1,0:T(8,128)(2,1)} %x_ref.1) | copy-start | bytes 3932164
  2.7 22.4 %all-to-all-start = ((bf16[16,136,128]{2,1,0:T(8,128)(2,1)}), bf16[16,136,128]{2,1,0:T(8,128)(2,1)S(1)}, u32[]{:S(2)}, u32[]{:S(2)}) async-start(bf16[16,136,128]{2,1,0:T(8,128)(2,1)} %pack.1), calls=%async_computation | async-start | bytes 1114112 | tf_op jit(solution)/shard_map/all_to_all | solution.py:339
  10.0 1.2 %copy-start.1 = (bf16[256,2048]{1,0:T(8,128)(2,1)S(1)}, bf16[256,2048]{1,0:T(8,128)(2,1)}, u32[]{:S(2)}) copy-start(bf16[256,2048]{1,0:T(8,128)(2,1)} %refs_3_.3) | copy-start | bytes 3145732
  11.3 13.8 %copy-start.2 = (bf16[256,2048]{1,0:T(8,128)(2,1)S(1)}, bf16[256,2048]{1,0:T(8,128)(2,1)}, u32[]{:S(2)}) copy-start(bf16[256,2048]{1,0:T(8,128)(2,1)} %refs_3_.3) | copy-start | bytes 3145732
  11.3 13.8 %copy-start.5 = (bf16[256,128]{1,0:T(8,128)(2,1)S(1)}, bf16[256,128]{1,0:T(8,128)(2,1)}, u32[]{:S(2)}) copy-start(bf16[256,128]{1,0:T(8,128)(2,1)} %refs_4_.3) | copy-start | bytes 196612
  11.3 13.8 %copy-start.6 = (bf16[256,128]{1,0:T(8,128)(2,1)S(1)}, bf16[256,128]{1,0:T(8,128)(2,1)}, u32[]{:S(2)}) copy-start(bf16[256,128]{1,0:T(8,128)(2,1)} %refs_5_.3) | copy-start | bytes 196612
  11.3 13.8 %copy-start.8 = (s32[64,15]{0,1:T(8,128)S(1)}, s32[64,15]{0,1:T(8,128)}, u32[]{:S(2)}) copy-start(s32[64,15]{0,1:T(8,128)} %param.14) | copy-start | bytes 11524
  11.9 39.1 %copy-start.7 = (f32[4,2,1024]{2,1,0:T(2,128)}, f32[4,2,1024]{2,1,0:T(2,128)S(1)}, u32[]{:S(2)}) copy-start(f32[4,2,1024]{2,1,0:T(2,128)S(1)} %gate.1.refs_6_.gate_ref) | copy-start | bytes 98308
  25.1 1.2 %copy-start.9 = (bf16[256,2048]{1,0:T(8,128)(2,1)S(1)}, bf16[256,2048]{1,0:T(8,128)(2,1)}, u32[]{:S(2)}) copy-start(bf16[256,2048]{1,0:T(8,128)(2,1)} %refs_2_.3) | copy-start | bytes 3145732
  32.5 24.4 %copy-start.10 = (bf16[64,256]{1,0:T(8,128)(2,1)}, bf16[64,256]{1,0:T(8,128)(2,1)S(1)}, u32[]{:S(2)}) copy-start(bf16[64,256]{1,0:T(8,128)(2,1)S(1)} %get-tuple-element.20.ckv_ref.refs_7_) | copy-start | bytes 98308
  51.0 5.9 %copy-start.4 = (bf16[16,128,128]{2,1,0:T(8,128)(2,1)}, bf16[16,128,128]{2,1,0:T(8,128)(2,1)S(1)}, u32[]{:S(2)}) copy-start(bf16[16,128,128]{2,1,0:T(8,128)(2,1)S(1)} %all_to_all.15.picks_ref.refs_8_) | copy-start | bytes 1572868
  57.0 19.1 %all-to-all-start.2 = ((bf16[16,136,128]{2,1,0:T(8,128)(2,1)}), bf16[16,136,128]{2,1,0:T(8,128)(2,1)S(1)}, u32[]{:S(2)}, u32[]{:S(2)}) async-start(bf16[16,136,128]{2,1,0:T(8,128)(2,1)} %get-tuple-element.28), calls=%async_computation.2 | async-start | bytes 1114112 | tf_op jit(solution)/shard_map/all_to_all | solution.py:339
  61.1 9.8 %collective-permute-start.1 = (bf16[1280,32]{0,1:T(8,128)(2,1)S(1)}, bf16[1280,32]{0,1:T(8,128)(2,1)S(1)}, u32[]{:S(2)}, u32[]{:S(2)}) collective-permute-start(bf16[1280,32]{0,1:T(8,128)(2,1)S(1)} %constant_dynamic-slice_fusion), channel_id=1, source_target_pairs={{0,1},{1,0},{2,3},{3,2},{4,5},{5,4},{6,7},{7,6},{8,9},{9,8},{10,11... | collective-permute-start | bytes 245768 | tf_op jit(solution)/shard_map/ppermute | solution.py:366
  62.7 8.2 %collective-permute-start = (bf16[32,256]{1,0:T(8,128)(2,1)S(1)}, bf16[32,256]{1,0:T(8,128)(2,1)S(1)}, u32[]{:S(2)}, u32[]{:S(2)}) collective-permute-start(bf16[32,256]{1,0:T(8,128)(2,1)S(1)} %convert_element_type.6), channel_id=1, source_target_pairs={{0,1},{1,0},{2,3},{3,2},{4,5},{5,4},{6,7},{7,6},{8,9},{9,8},{10,11... | collective-permute-start | bytes 49160 | tf_op jit(solution)/shard_map/ppermute | solution.py:461
  64.7 6.3 %copy-start.11 = (f32[256,1280]{1,0:T(8,128)S(1)}, f32[256,1280]{1,0:T(8,128)}, u32[]{:S(2)}) copy-start(f32[256,1280]{1,0:T(8,128)} %fusion.1) | copy-start | bytes 3932164
